TPU v7x, 32 devices: a whole 2x2x4 slice. The times are simulated.
32 devices in a mesh: cuts: 4 (over z), energy: 2 (over y), group: 4 (over x, core).
Axes of the slice: x: 2, y: 2, z: 4, core: 2. Of those that a mesh axis runs over, the one named last changes fastest.
Arguments:
- transfer: float32 [2, 12, 512, 512], P('energy', 'cuts'), may hold values from -1.5 to 1.5
- source: float32 [2, 6144, 512], P('energy', 'cuts', 'group'), may hold values from -4 to 4
- coupling: bfloat16 [512, 512], replicated, may hold values from -0.25 to 0.25
- strength: float32 [8], replicated, may hold values from 0.2 to 1
- mode_shift: int32 [8], replicated, may hold values from 0 to 1, as said below
Outputs:
- green: float32 [2, 6144, 512], P('energy', 'cuts', 'group')
- scattered: float32 [2, 6144, 512], P('energy', 'cuts', 'group')
Inputs may be any that keep to these rules, and one draw needn't show every extreme that they name: `mode_shift`: every energy offset of 0 to 1 is taken by at least one mode.
All inputs are finite; a program needn't handle non-finite values.
Results may differ from a plain program's by a relative error of at most 0.0035.
Values sent between devices are 32-bit elements; how exact they have to be, the bound alone decides.
No kernel may reach another device: no remote copies, remote signals or barrier semaphores. Data moves between devices by JAX's collectives and lax.ppermute only.
A program may use at most 64 MiB of HBM per device.

v0:
```python
import jax
import jax.numpy as jnp
from jax import lax
from jax.sharding import PartitionSpec as P


def shifted(value, axis, by):
    devices = lax.axis_size(axis)
    pairs = [(i, i + by) for i in range(devices) if 0 <= i + by < devices]
    return lax.ppermute(value, axis, pairs)


def padded(value, sides, width):
    for axis, dim in sides:
        devices, length = (lax.axis_size(axis), value.shape[dim])
        up = [(i, (i + 1) % devices) for i in range(devices - 1)]
        down = [(j, i) for i, j in up]
        last = lax.slice_in_dim(value, length - width, length, axis=dim)
        initial = lax.slice_in_dim(value, 0, width, axis=dim)
        before = lax.ppermute(last, axis, up)
        after = lax.ppermute(initial, axis, down)
        value = jnp.concatenate([before, value, after], axis=dim)
    return value


def matmul(left, right):
    return jnp.dot(left, right, precision=lax.Precision.HIGHEST, preferred_element_type=jnp.float32)


def body(transfer, source, coupling, strength, mode_shift):
    mats = transfer[0]
    count = mats.shape[0]
    orbs = mats.shape[1]
    srcs = source[0].reshape(count, orbs, source.shape[2])
    locals_list = []
    products = []
    for block in range(count):
        if block == 0:
            state = srcs[0]
            product = mats[0]
        else:
            state = matmul(mats[block], state) + srcs[block]
            product = matmul(mats[block], product)
        locals_list.append(state)
        products.append(product)
    composite = products[-1]
    offset = locals_list[-1]

    def advance(step, incoming):
        leaving = matmul(composite, incoming) + offset
        return shifted(leaving, "cuts", 1)

    incoming = lax.fori_loop(0, lax.axis_size("cuts") - 1, advance, jnp.zeros_like(offset))
    green = jnp.stack(
        [locals_list[block] + matmul(products[block], incoming) for block in range(count)]
    )
    partial_sq = jnp.sum(green * green, axis=2)
    totals = lax.psum(partial_sq, "group")
    density = totals / (green.shape[2] * lax.axis_size("group"))
    edges = padded(density, (("cuts", 0),), 1)
    smoothed = density + 0.5 * (edges[:-2] + edges[2:])
    every_energy = lax.all_gather(smoothed[None], "energy", axis=0, tiled=True)
    points = every_energy.shape[0]
    here = lax.axis_index("energy")
    goal_value = (here + mode_shift) % points
    onehot = (goal_value[:, None] == jnp.arange(points, dtype=jnp.int32)[None, :]).astype(
        jnp.float32
    )
    weights = jnp.sum(strength[:, None] * onehot, axis=0)
    selfen = jnp.einsum("f,fko->ko", weights, every_energy, precision=lax.Precision.HIGHEST)
    low = green.astype(jnp.bfloat16)
    inner = jnp.einsum("oi,kon->kin", coupling, low, preferred_element_type=jnp.float32)
    scaled = (inner * selfen[:, :, None]).astype(jnp.bfloat16)
    scattered = jnp.einsum("io,kon->kin", coupling, scaled, preferred_element_type=jnp.float32)
    width = green.shape[2]
    return (green.reshape(1, count * orbs, width), scattered.reshape(1, count * orbs, width))


def solution(mesh):
    in_specs = (P("energy", "cuts", None, None), P("energy", "cuts", "group"), P(), P(), P())
    out_specs = (P("energy", "cuts", "group"), P("energy", "cuts", "group"))
    return jax.shard_map(body, mesh=mesh, in_specs=in_specs, out_specs=out_specs, check_vma=False)
```

profile of v0, /device:TPU:0, one launch (start us, length us, event | category | flops | bytes accessed | tf_op | source)
XLA Modules:
  0.0 77.4 jit_solution(16092757013658263163)
XLA Ops:
  0.6 3.4 %fusion.11 = f32[512,512]{1,0:T(8,128)S(1)} fusion(f32[1,3,512,512]{3,2,1,0:T(8,128)} %param.7), kind=kOutput, calls=%fused_computation.19 | convolution fusion | flops 1610612736 | bytes 3145728 | tf_op jit(solution)/shard_map/dot_general | solution.py:27
  4.1 5.7 %fusion.8 = f32[512,512]{1,0:T(8,128)} fusion(f32[512,512]{1,0:T(8,128)S(1)} %fusion.11, f32[1,3,512,512]{3,2,1,0:T(8,128)} %param.7), kind=kOutput, calls=%fused_computation.16 | convolution fusion | flops 1610612736 | bytes 3145728 | tf_op jit(solution)/shard_map/dot_general | solution.py:27
  9.8 1.6 %copy.20 = f32[512,512]{1,0:T(8,128)S(1)} copy(f32[512,512]{0,1:T(8,128)} %bitcast.73) | data formatting | bytes 2097152 | tf_op jit(solution)/shard_map/while | solution.py:53
  11.3 2.3 %convolution_add_fusion.3 = f32[512,128]{1,0:T(8,128)S(1)} fusion(f32[1,3,512,512]{3,2,1,0:T(8,128)} %param.7, f32[1,1536,128]{2,1,0:T(8,128)} %param.8), kind=kOutput, calls=%fused_computation.14 | convolution fusion | flops 402718720 | bytes 1835008 | tf_op jit(solution)/shard_map/dot_general | solution.py:27
  13.7 2.3 %fusion.2 = f32[512,128]{1,0:T(8,128)S(1)} fusion(f32[512,128]{1,0:T(8,128)S(1)} %convolution_add_fusion.3, f32[1,3,512,512]{3,2,1,0:T(8,128)} %param.7, f32[1,1536,128]{2,1,0:T(8,128)} %param.8), kind=kOutput, calls=%fused_computation.7 | convolution fusion | flops 402718720 | bytes 1835008 | tf_op jit(solution)/shard_map/dot_general | solution.py:27
  16.1 31.0 %while.10 = (s32[]{:T(128)}, f32[512,128]{1,0:T(8,128)S(1)}, f32[512,512]{1,0:T(8,128)S(1)}, f32[512,128]{1,0:T(8,128)S(1)}, s32[]{:T(128)}) while((s32[]{:T(128)}, f32[512,128]{1,0:T(8,128)S(1)}, f32[512,512]{1,0:T(8,128)S(1)}, f32[512,128]{1,0:T(8,128)S(1)}, s32[]{:T(128)}) %tuple.28), condition=%wide.region_1.0_spmd, body=%wide.region_0.0_spmd.sunk | while | flops 402718720 | bytes 2883685 | solution.py:53
  16.3 1.0 %convolution_add_fusion.5 = f32[512,128]{1,0:T(8,128)S(1)} fusion(f32[512,128]{1,0:T(8,128)S(1)} %get-tuple-element.91, f32[512,512]{1,0:T(8,128)S(1)} %get-tuple-element.90, f32[512,128]{1,0:T(8,128)S(1)} %get-tuple-element.84), kind=kOutput, calls=%fused_computation.clone.1 | convolution fusion | flops 402718720 | bytes 1835008 | tf_op jit(solution)/shard_map/while/body/eval_jaxpr/dot_general | solution.py:27
  17.3 4.9 %collective-permute-start = (f32[512,128]{1,0:T(8,128)S(1)}, f32[512,128]{1,0:T(8,128)S(1)}, u32[]{:S(2)}, u32[]{:S(2)}) collective-permute-start(f32[512,128]{1,0:T(8,128)S(1)} %convolution_add_fusion.5), channel_id=1, source_target_pairs={{0,8},{8,16},{16,24},{1,9},{9,17},{17,25},{2,10},{10,18},{18,26},{... | collective-permute-start | bytes 786440 | tf_op jit(solution)/shard_map/while/body/eval_jaxpr/ppermute | solution.py:10
  22.2 5.5 %collective-permute-done = f32[512,128]{1,0:T(8,128)S(1)} collective-permute-done((f32[512,128]{1,0:T(8,128)S(1)}, f32[512,128]{1,0:T(8,128)S(1)}, u32[]{:S(2)}, u32[]{:S(2)}) %collective-permute-start) | collective-permute-done | bytes 262176 | tf_op jit(solution)/shard_map/while/body/eval_jaxpr/ppermute | solution.py:10
  27.7 1.0 %convolution_add_fusion.5 = f32[512,128]{1,0:T(8,128)S(1)} fusion(f32[512,128]{1,0:T(8,128)S(1)} %get-tuple-element.91, f32[512,512]{1,0:T(8,128)S(1)} %get-tuple-element.90, f32[512,128]{1,0:T(8,128)S(1)} %get-tuple-element.84), kind=kOutput, calls=%fused_computation.clone.1 | convolution fusion | flops 402718720 | bytes 1835008 | tf_op jit(solution)/shard_map/while/body/eval_jaxpr/dot_general | solution.py:27
  28.7 4.4 %collective-permute-start = (f32[512,128]{1,0:T(8,128)S(1)}, f32[512,128]{1,0:T(8,128)S(1)}, u32[]{:S(2)}, u32[]{:S(2)}) collective-permute-start(f32[512,128]{1,0:T(8,128)S(1)} %convolution_add_fusion.5), channel_id=1, source_target_pairs={{0,8},{8,16},{16,24},{1,9},{9,17},{17,25},{2,10},{10,18},{18,26},{... | collective-permute-start | bytes 786440 | tf_op jit(solution)/shard_map/while/body/eval_jaxpr/ppermute | solution.py:10
  33.1 4.7 %collective-permute-done = f32[512,128]{1,0:T(8,128)S(1)} collective-permute-done((f32[512,128]{1,0:T(8,128)S(1)}, f32[512,128]{1,0:T(8,128)S(1)}, u32[]{:S(2)}, u32[]{:S(2)}) %collective-permute-start) | collective-permute-done | bytes 262176 | tf_op jit(solution)/shard_map/while/body/eval_jaxpr/ppermute | solution.py:10
  38.8 4.4 %collective-permute-start = (f32[512,128]{1,0:T(8,128)S(1)}, f32[512,128]{1,0:T(8,128)S(1)}, u32[]{:S(2)}, u32[]{:S(2)}) collective-permute-start(f32[512,128]{1,0:T(8,128)S(1)} %convolution_add_fusion.5), channel_id=1, source_target_pairs={{0,8},{8,16},{16,24},{1,9},{9,17},{17,25},{2,10},{10,18},{18,26},{... | collective-permute-start | bytes 786440 | tf_op jit(solution)/shard_map/while/body/eval_jaxpr/ppermute | solution.py:10
  43.2 3.9 %collective-permute-done = f32[512,128]{1,0:T(8,128)S(1)} collective-permute-done((f32[512,128]{1,0:T(8,128)S(1)}, f32[512,128]{1,0:T(8,128)S(1)}, u32[]{:S(2)}, u32[]{:S(2)}) %collective-permute-start) | collective-permute-done | bytes 262176 | tf_op jit(solution)/shard_map/while/body/eval_jaxpr/ppermute | solution.py:10
  47.1 3.1 %fusion.5 = f32[1,512,128]{2,1,0:T(8,128)S(1)} fusion(f32[512,128]{1,0:T(8,128)S(1)} %get-tuple-element.94, f32[512,512]{1,0:T(8,128)} %fusion.8, f32[512,128]{1,0:T(8,128)S(1)} %get-tuple-element.24), kind=kOutput, calls=%fused_computation.11 | convolution fusion | flops 402718720 | bytes 1835008 | tf_op jit(solution)/shard_map/dot_general | solution.py:27
  50.1 1.9 %fusion.6 = f32[1,512,128]{2,1,0:T(8,128)S(1)} fusion(f32[512,128]{1,0:T(8,128)} %copy-done.1, f32[512,512]{1,0:T(8,128)S(1)} %fusion.11, f32[512,128]{1,0:T(8,128)S(1)} %get-tuple-element.24), kind=kOutput, calls=%fused_computation.13 | convolution fusion | flops 402718720 | bytes 1835008 | tf_op jit(solution)/shard_map/dot_general | solution.py:27
  52.1 2.3 %fusion.4 = f32[1,512,128]{2,1,0:T(8,128)S(1)} fusion(f32[512,128]{1,0:T(8,128)S(1)} %get-tuple-element.24, f32[1,3,512,512]{3,2,1,0:T(8,128)} %param.7, f32[1,1536,128]{2,1,0:T(8,128)} %param.8), kind=kOutput, calls=%fused_computation.9 | convolution fusion | flops 402718720 | bytes 1835008 | tf_op jit(solution)/shard_map/dot_general | solution.py:27
  54.3 1.0 %multiply_reduce_fusion = (f32[3,512]{1,0:T(4,128)S(1)}, f32[3,512,128]{2,1,0:T(8,128)}) fusion(f32[1,512,128]{2,1,0:T(8,128)S(1)} %fusion.5, f32[1,512,128]{2,1,0:T(8,128)S(1)} %fusion.6, f32[1,512,128]{2,1,0:T(8,128)S(1)} %fusion.4), kind=kLoop, calls=%fused_computation.30 | loop fusion | flops 784896 | bytes 1579008 | tf_op jit(solution)/shard_map/reduce_sum | solution.py:57
  55.3 5.7 %psum.7 = f32[3,512]{1,0:T(4,128)S(1)} all-reduce(f32[3,512]{1,0:T(4,128)S(1)} %get-tuple-element.49), channel_id=1, replica_groups=mesh['cuts'=4,'energy'=2,'group'=4] {'group'}, use_global_device_ids=true, to_apply=%region_4.5 | all-reduce | flops 1536 | bytes 12288 | tf_op jit(solution)/shard_map/psum | solution.py:58
  61.1 4.4 %collective-permute-start.1 = (f32[1,512]{1,0:T(1,128)S(1)}, f32[1,512]{1,0:T(1,128)S(1)}, u32[]{:S(2)}, u32[]{:S(2)}) collective-permute-start(f32[1,512]{1,0:T(1,128)S(1)} %get-tuple-element.51), channel_id=1, source_target_pairs={{0,8},{8,16},{16,24},{1,9},{9,17},{17,25},{2,10},{10,18},{18,26},{... | collective-permute-start | bytes 6152 | tf_op jit(solution)/shard_map/ppermute | solution.py:20
  65.5 1.3 %collective-permute-start.2 = (f32[1,512]{1,0:T(1,128)S(1)}, f32[1,512]{1,0:T(1,128)S(1)}, u32[]{:S(2)}, u32[]{:S(2)}) collective-permute-start(f32[1,512]{1,0:T(1,128)S(1)} %get-tuple-element.52), channel_id=1, source_target_pairs={{8,0},{16,8},{24,16},{9,1},{17,9},{25,17},{10,2},{18,10},{26,18},{... | collective-permute-start | bytes 6152 | tf_op jit(solution)/shard_map/ppermute | solution.py:21
  67.0 4.0 %collective-permute-done.2 = f32[1,512]{1,0:T(1,128)S(1)} collective-permute-done((f32[1,512]{1,0:T(1,128)S(1)}, f32[1,512]{1,0:T(1,128)S(1)}, u32[]{:S(2)}, u32[]{:S(2)}) %collective-permute-start.2) | collective-permute-done | bytes 2080 | tf_op jit(solution)/shard_map/ppermute | solution.py:21
  71.0 4.4 %all-gather.1 = f32[2,3,512]{2,1,0:T(4,128)S(1)} all-gather(f32[1,3,512]{2,1,0:T(4,128)S(1)} %fusion.33), channel_id=2, replica_groups=mesh['cuts'=4,'energy'=2,'group'=4] {'energy'}, dimensions={0}, use_global_device_ids=true | all-gather | bytes 18432 | tf_op jit(solution)/shard_map/all_gather | solution.py:62
  76.2 1.2 %copy.23 = f32[3,512,128]{2,1,0:T(8,128)} copy(f32[3,512,128]{1,2,0:T(8,128)S(1)} %convolution_bitcast_fusion) | data formatting | bytes 1572864 | tf_op jit(solution)/shard_map/io,kon->kin/transpose | solution.py:74
  (19 shorter events, 2.0 us)
Async XLA Ops:
  0.6 74.9 %copy-start = (bf16[512,512]{1,0:T(8,128)(2,1)S(1)}, bf16[512,512]{1,0:T(8,128)(2,1)}, u32[]{:S(2)}) copy-start(bf16[512,512]{1,0:T(8,128)(2,1)} %param.9) | copy-start | bytes 1572868
  13.7 2.4 %copy-start.1 = (f32[512,128]{1,0:T(8,128)}, f32[512,128]{1,0:T(8,128)S(1)}, u32[]{:S(2)}) copy-start(f32[512,128]{1,0:T(8,128)S(1)} %convolution_add_fusion.3) | copy-start | bytes 786436
  17.3 10.5 %collective-permute-start = (f32[512,128]{1,0:T(8,128)S(1)}, f32[512,128]{1,0:T(8,128)S(1)}, u32[]{:S(2)}, u32[]{:S(2)}) collective-permute-start(f32[512,128]{1,0:T(8,128)S(1)} %convolution_add_fusion.5), channel_id=1, source_target_pairs={{0,8},{8,16},{16,24},{1,9},{9,17},{17,25},{2,10},{10,18},{18,26},{... | collective-permute-start | bytes 786440 | tf_op jit(solution)/shard_map/while/body/eval_jaxpr/ppermute | solution.py:10
  28.7 9.1 %collective-permute-start = (f32[512,128]{1,0:T(8,128)S(1)}, f32[512,128]{1,0:T(8,128)S(1)}, u32[]{:S(2)}, u32[]{:S(2)}) collective-permute-start(f32[512,128]{1,0:T(8,128)S(1)} %convolution_add_fusion.5), channel_id=1, source_target_pairs={{0,8},{8,16},{16,24},{1,9},{9,17},{17,25},{2,10},{10,18},{18,26},{... | collective-permute-start | bytes 786440 | tf_op jit(solution)/shard_map/while/body/eval_jaxpr/ppermute | solution.py:10
  38.8 8.3 %collective-permute-start = (f32[512,128]{1,0:T(8,128)S(1)}, f32[512,128]{1,0:T(8,128)S(1)}, u32[]{:S(2)}, u32[]{:S(2)}) collective-permute-start(f32[512,128]{1,0:T(8,128)S(1)} %convolution_add_fusion.5), channel_id=1, source_target_pairs={{0,8},{8,16},{16,24},{1,9},{9,17},{17,25},{2,10},{10,18},{18,26},{... | collective-permute-start | bytes 786440 | tf_op jit(solution)/shard_map/while/body/eval_jaxpr/ppermute | solution.py:10
  47.1 19.8 %copy-start.2 = (s32[8]{0:T(128)S(1)}, s32[8]{0:T(128)}, u32[]{:S(2)}) copy-start(s32[8]{0:T(128)} %param.11) | copy-start | bytes 100
  47.1 19.8 %copy-start.3 = (f32[8]{0:T(128)S(1)}, f32[8]{0:T(128)}, u32[]{:S(2)}) copy-start(f32[8]{0:T(128)} %param.10) | copy-start | bytes 100
  61.1 5.9 %collective-permute-start.1 = (f32[1,512]{1,0:T(1,128)S(1)}, f32[1,512]{1,0:T(1,128)S(1)}, u32[]{:S(2)}, u32[]{:S(2)}) collective-permute-start(f32[1,512]{1,0:T(1,128)S(1)} %get-tuple-element.51), channel_id=1, source_target_pairs={{0,8},{8,16},{16,24},{1,9},{9,17},{17,25},{2,10},{10,18},{18,26},{... | collective-permute-start | bytes 6152 | tf_op jit(solution)/shard_map/ppermute | solution.py:20
  65.5 5.5 %collective-permute-start.2 = (f32[1,512]{1,0:T(1,128)S(1)}, f32[1,512]{1,0:T(1,128)S(1)}, u32[]{:S(2)}, u32[]{:S(2)}) collective-permute-start(f32[1,512]{1,0:T(1,128)S(1)} %get-tuple-element.52), channel_id=1, source_target_pairs={{8,0},{16,8},{24,16},{9,1},{17,9},{25,17},{10,2},{18,10},{26,18},{... | collective-permute-start | bytes 6152 | tf_op jit(solution)/shard_map/ppermute | solution.py:21
where the time goes:
time: 77.9 us; the launch traced here: 77.4 us
  matrix products  24.8 us (32%)
  starting transfers between devices  19.4 us (25%)
  waiting for transfers between devices  18.1 us (23%)
  blocking collectives  10.1 us (13%)
  local copies, waits for them, and re-layouts  2.76 us (4%)
  other arithmetic  1.17 us (2%)
  between operations  0.81 us (1%)
    dot_general x10, matrix products, matmul(): jnp.dot(left, right, precision=lax.Precision.HIGHEST, preferred_element_t...  24 us
    ppermute x3, waiting for transfers between devices, shifted(): return lax.ppermute(value, axis, pairs)  14 us
    ppermute x3, starting transfers between devices, shifted(): return lax.ppermute(value, axis, pairs)  13.7 us
    psum x1, blocking collectives, body(): totals = lax.psum(partial_sq, 'group')  5.73 us
    ppermute x1, starting transfers between devices, padded(): before = lax.ppermute(last, axis, up)  4.38 us
    all_gather x1, blocking collectives, body(): every_energy = lax.all_gather(smoothed[None], 'energy', axis=0, tiled=True)  4.36 us
    ppermute x1, waiting for transfers between devices, padded(): after = lax.ppermute(initial, axis, down)  4.02 us
  transfers between devices with their start and end apart: 5, of which 4 were waited for; matrix products, arithmetic and copies ran while one was open for 0% of the time, Pallas kernels for 0%

commit v1 on v0

v1 whole, which is shorter than its diff:
```python
import functools

import jax
import jax.numpy as jnp
from jax import lax
from jax.experimental import pallas as pl
from jax.experimental.pallas import tpu as pltpu
from jax.sharding import PartitionSpec as P

F32 = jnp.float32
BF16 = jnp.bfloat16
VMEM = pl.BlockSpec(memory_space=pltpu.VMEM)
HBM = pl.BlockSpec(memory_space=pltpu.HBM)
PARAMS = pltpu.CompilerParams(vmem_limit_bytes=48 * 1024 * 1024)


def split(value):
    high = value.astype(BF16)
    return high, (value - high.astype(F32)).astype(BF16)


def dot(left, right):
    return jnp.dot(left, right, preferred_element_type=F32)


def dot_t(left, right):
    return lax.dot_general(left, right, (((1,), (1,)), ((), ())), preferred_element_type=F32)


def product(left_high, left_low, state):
    high, low = split(state)
    width = state.shape[1]
    both = dot(left_high, jnp.concatenate([high, low], axis=1))
    return both[:, :width] + (both[:, width:] + dot(left_low, high))


def local_kernel(mats_ref, srcs_ref, local_ref, mats, srcs, sems, src_sem):
    count, orbs = mats_ref.shape[0], mats_ref.shape[1]
    src_copy = pltpu.make_async_copy(srcs_ref, srcs, src_sem)
    src_copy.start()
    copies = [
        pltpu.make_async_copy(mats_ref.at[k], mats.at[k], sems.at[k]) for k in range(1, count)
    ]
    for copy in copies:
        copy.start()
    src_copy.wait()
    state = srcs[:orbs, :]
    local_ref[:orbs, :] = state
    for k in range(1, count):
        copies[k - 1].wait()
        rows = slice(k * orbs, (k + 1) * orbs)
        state = product(*split(mats[k]), state) + srcs[rows, :]
        local_ref[rows, :] = state


def local_chain(mats, srcs):
    return pl.pallas_call(
        local_kernel,
        out_shape=jax.ShapeDtypeStruct(srcs.shape, F32),
        in_specs=[HBM, HBM],
        out_specs=VMEM,
        scratch_shapes=[
            pltpu.VMEM(mats.shape, F32),
            pltpu.VMEM(srcs.shape, F32),
            pltpu.SemaphoreType.DMA((mats.shape[0],)),
            pltpu.SemaphoreType.DMA,
        ],
        compiler_params=PARAMS,
        name="local_chain",
    )(mats, srcs)


def composite_kernel(mats_ref, high_ref, low_ref, mats, sems):
    count, orbs = mats_ref.shape[0], mats_ref.shape[1]
    copies = [pltpu.make_async_copy(mats_ref.at[k], mats.at[k], sems.at[k]) for k in range(count)]
    for copy in copies:
        copy.start()
    copies[0].wait()
    high, low = split(mats[0])
    high_ref[:orbs, :], low_ref[:orbs, :] = high, low
    for k in range(1, count):
        copies[k].wait()
        left_high, left_low = split(mats[k])
        full = dot(left_high, high) + (dot(left_high, low) + dot(left_low, high))
        high, low = split(full)
        rows = slice(k * orbs, (k + 1) * orbs)
        high_ref[rows, :], low_ref[rows, :] = high, low


def composites(mats):
    count, orbs, _ = mats.shape
    shape = jax.ShapeDtypeStruct((count * orbs, orbs), BF16)
    return pl.pallas_call(
        composite_kernel,
        out_shape=(shape, shape),
        in_specs=[HBM],
        out_specs=(VMEM, VMEM),
        scratch_shapes=[pltpu.VMEM(mats.shape, F32), pltpu.SemaphoreType.DMA((count,))],
        compiler_params=PARAMS,
        cost_estimate=pl.CostEstimate(
            flops=6 * (count - 1) * orbs**3, bytes_accessed=8 * count * orbs**2, transcendentals=0
        ),
        name="composites",
    )(mats)


def relay_kernel(step, high_ref, low_ref, local_ref, got_ref, incoming_ref, out_ref, kept_ref):
    orbs = got_ref.shape[0]
    got = got_ref[...]
    rows = slice(high_ref.shape[0] - orbs, None)
    out_ref[...] = product(high_ref[rows, :], low_ref[rows, :], got) + local_ref[rows, :]
    kept_ref[...] = jnp.where(lax.axis_index("cuts") == step, got, incoming_ref[...])


def relay(step, high, low, local, got, incoming):
    shape = jax.ShapeDtypeStruct(got.shape, F32)
    return pl.pallas_call(
        functools.partial(relay_kernel, step),
        out_shape=(shape, shape),
        in_specs=[VMEM] * 5,
        out_specs=(VMEM, VMEM),
        compiler_params=PARAMS,
        name="relay",
    )(high, low, local, got, incoming)


def row_sums(value):
    squares = value * value
    high, low = split(squares)
    ones = jnp.ones((8, value.shape[1]), BF16)
    return (dot_t(ones, high) + dot_t(ones, low))[:1, :]


def green_kernel(step, high_ref, low_ref, local_ref, got_ref, incoming_ref, green_ref, sums_ref):
    orbs = got_ref.shape[0]
    count = local_ref.shape[0] // orbs
    state = jnp.where(lax.axis_index("cuts") == step, got_ref[...], incoming_ref[...])
    sums = [row_sums(state)]
    for k in range(count):
        rows = slice(k * orbs, (k + 1) * orbs)
        block = product(high_ref[rows, :], low_ref[rows, :], state) + local_ref[rows, :]
        green_ref[rows, :] = block
        sums.append(row_sums(block))
    sums_ref[...] = jnp.concatenate(sums, axis=0)


def green_blocks(step, high, low, local, got, incoming):
    orbs = got.shape[0]
    count = local.shape[0] // orbs
    return pl.pallas_call(
        functools.partial(green_kernel, step),
        out_shape=(
            jax.ShapeDtypeStruct(local.shape, F32),
            jax.ShapeDtypeStruct((count + 1, orbs), F32),
        ),
        in_specs=[VMEM] * 5,
        out_specs=(VMEM, VMEM),
        compiler_params=PARAMS,
        name="green_blocks",
    )(high, low, local, got, incoming)


def inner_kernel(coupling_ref, green_ref, inner_ref):
    orbs = coupling_ref.shape[0]
    coupling = coupling_ref[...]
    for k in range(green_ref.shape[0] // orbs):
        low = green_ref[k * orbs : (k + 1) * orbs, :].astype(BF16)
        inner_ref[k] = dot(low.T, coupling)


def inner_blocks(coupling, green):
    orbs = coupling.shape[0]
    count, width = green.shape[0] // orbs, green.shape[1]
    return pl.pallas_call(
        inner_kernel,
        out_shape=jax.ShapeDtypeStruct((count, width, orbs), F32),
        in_specs=[VMEM, VMEM],
        out_specs=VMEM,
        compiler_params=PARAMS,
        cost_estimate=pl.CostEstimate(
            flops=2 * count * width * orbs**2, bytes_accessed=2 * orbs**2, transcendentals=0
        ),
        name="inner_blocks",
    )(coupling, green)


def scatter_kernel(coupling_ref, inner_ref, mixed_ref, after_ref, out_ref):
    count, _, orbs = inner_ref.shape
    rows = [mixed_ref[k : k + 1, :] for k in range(count + 1)]
    last = lax.axis_index("cuts") == lax.axis_size("cuts") - 1
    rows.append(jnp.where(last, 0.0, after_ref[...]))
    coupling = coupling_ref[...]
    for k in range(count):
        selfen = rows[k + 1] + 0.5 * (rows[k] + rows[k + 2])
        scaled = (inner_ref[k] * selfen).astype(BF16)
        out_ref[k * orbs : (k + 1) * orbs, :] = dot_t(coupling, scaled)


def scatter_blocks(coupling, inner, mixed, after):
    count, width, orbs = inner.shape
    return pl.pallas_call(
        scatter_kernel,
        out_shape=jax.ShapeDtypeStruct((count * orbs, width), F32),
        in_specs=[VMEM] * 4,
        out_specs=VMEM,
        compiler_params=PARAMS,
        name="scatter_blocks",
    )(coupling, inner, mixed, after)


def relay_pairs(step, cuts, group):
    pairs = []
    for c in range(cuts):
        for g in range(group):
            if c == step - 1:
                to = (c + 1, g)
            elif c == step:
                to = (c - 1, g)
            else:
                to = (c, g ^ 1 if g ^ 1 < group else g)
            pairs.append((c * group + g, to[0] * group + to[1]))
    return pairs


def exchanged(value, axis, offset):
    devices = lax.axis_size(axis)
    return lax.ppermute(value, axis, [(i, (i + offset) % devices) for i in range(devices)])


def body(transfer, source, coupling, strength, mode_shift):
    mats, srcs = transfer[0], source[0]
    orbs, width = mats.shape[1], srcs.shape[1]
    cuts, group, points = (lax.axis_size(a) for a in ("cuts", "group", "energy"))
    local = local_chain(mats, srcs)
    leaving = local[local.shape[0] - orbs :, :]
    incoming = jnp.zeros((orbs, width), F32)
    high, low = composites(mats)
    got = incoming
    for step in range(1, cuts):
        got = lax.ppermute(leaving, ("cuts", "group"), relay_pairs(step, cuts, group))
        if step < cuts - 1:
            leaving, incoming = relay(step, high, low, local, got, incoming)
    green, sums = green_blocks(cuts - 1, high, low, local, got, incoming)
    inner = inner_blocks(coupling, green)

    parts = [exchanged(sums, "group", offset) for offset in range(1, group)]
    density = (sums + sum(parts)) / (width * group)
    here = lax.axis_index("energy")
    goal = (here + mode_shift) % points
    mixed = 0.0
    for offset in range(points):
        there = density if offset == 0 else exchanged(density, "energy", offset)
        weight = jnp.sum(jnp.where(goal == (here - offset) % points, strength, 0.0))
        mixed = mixed + weight * there
    after = exchanged(mixed[1:2], "cuts", -1)
    scattered = scatter_blocks(coupling, inner, mixed, after)
    return green[None], scattered[None]


def solution(mesh):
    in_specs = (P("energy", "cuts", None, None), P("energy", "cuts", "group"), P(), P(), P())
    out_specs = (P("energy", "cuts", "group"), P("energy", "cuts", "group"))
    return jax.shard_map(body, mesh=mesh, in_specs=in_specs, out_specs=out_specs, check_vma=False)
```

time: 77.9 us -> 44.5 us (0.57)
  matrix products: 24.8 us -> 0 us
  waiting for transfers between devices: 18.1 us -> 7.85 us
  blocking collectives: 10.1 us -> 0 us
  Pallas kernels: 0 us -> 9.83 us
  local copies, waits for them, and re-layouts: 2.76 us -> 4.2 us
    dot_general x12 -> x0, matrix products: 24.8 us -> none  [the longest x10 24 us: matmul(): jnp.dot(left, right, precision=lax.Precision.HIGHEST, preferred_element_t...]
    ppermute x5 -> x8, waiting for transfers between devices: 18.1 us -> 7.85 us  [the longest x3 5.64 us: body(): lax.ppermute(leaving, ('cuts', 'group'), relay_pairs(step, cuts, group))]
    pallas_call x0 -> x7, Pallas kernels: none -> 9.83 us  [the longest x1 3.58 us: composites(): pl.pallas_call(composite_kernel, out_shape=(shape, shape), in_specs=[HBM]...]
    psum x1 -> x0, blocking collectives: 5.73 us -> none  [body(): totals = lax.psum(partial_sq, 'group')]
    all_gather x1 -> x0, blocking collectives: 4.36 us -> none  [body(): every_energy = lax.all_gather(smoothed[None], 'energy', axis=0, tiled=True)]
    unnamed x8 -> x12, local copies, waits for them, and re-layouts: 0.02 us -> 4.16 us
    while x1 -> x0, local copies, waits for them, and re-layouts: 1.55 us -> none  [body(): lax.fori_loop(0, lax.axis_size('cuts') - 1, advance, jnp.zeros_like(offset))]
    transpose x1 -> x0, local copies, waits for them, and re-layouts: 1.15 us -> none  [body(): jnp.einsum('io,kon->kin', coupling, scaled, preferred_element_type=jnp.fl...]
  transfers between devices with their start and end apart: 5 -> 8, of which waited for: 4 -> 6; matrix products, arithmetic and copies ran while one was open for 0% -> 1% of each run, Pallas kernels for 0% -> 9%
where the time goes in v1:
time: 44.5 us; the launch traced here: 44.2 us
  starting transfers between devices  19.7 us (44%)
  Pallas kernels  9.83 us (22%)
  waiting for transfers between devices  7.85 us (18%)
  local copies, waits for them, and re-layouts  4.2 us (9%)
  between operations  1.38 us (3%)
  other arithmetic  1.29 us (3%)
    ppermute x5, starting transfers between devices, exchanged(): lax.ppermute(value, axis, [(i, (i + offset) % devices) for i in range(dev...  16.3 us
    ppermute x3, waiting for transfers between devices, body(): lax.ppermute(leaving, ('cuts', 'group'), relay_pairs(step, cuts, group))  5.64 us
    unnamed x12, local copies, waits for them, and re-layouts  4.16 us
    pallas_call x1, Pallas kernels, composites(): pl.pallas_call(composite_kernel, out_shape=(shape, shape), in_specs=[HBM]...  3.58 us
    ppermute x3, starting transfers between devices, body(): lax.ppermute(leaving, ('cuts', 'group'), relay_pairs(step, cuts, group))  3.36 us
    pallas_call x1, Pallas kernels, green_blocks(): pl.pallas_call(functools.partial(green_kernel, step), out_shape=(jax.Shap...  2.36 us
    ppermute x5, waiting for transfers between devices, exchanged(): lax.ppermute(value, axis, [(i, (i + offset) % devices) for i in range(dev...  2.21 us
    pallas_call x1, Pallas kernels, scatter_blocks(): pl.pallas_call(scatter_kernel, out_shape=jax.ShapeDtypeStruct((count * or...  1.47 us
  transfers between devices with their start and end apart: 8, of which 6 were waited for; matrix products, arithmetic and copies ran while one was open for 1% of the time, Pallas kernels for 9%

profile of v1, /device:TPU:0, one launch (start us, length us, event | category | flops | bytes accessed | tf_op | source)
XLA Modules:
  0.0 44.2 jit_solution(2663699418706888421)
XLA Ops:
  0.6 1.9 %copy-done = f32[1,3,512,512]{3,2,1,0:T(8,128)S(1)} copy-done((f32[1,3,512,512]{3,2,1,0:T(8,128)S(1)}, f32[1,3,512,512]{3,2,1,0:T(8,128)}, u32[]{:S(2)}) %copy-start) | copy-done | bytes 3145752
  2.5 1.1 %copy-done.2 = f32[1,1536,128]{2,1,0:T(8,128)S(1)} copy-done((f32[1,1536,128]{2,1,0:T(8,128)S(1)}, f32[1,1536,128]{2,1,0:T(8,128)}, u32[]{:S(2)}) %copy-start.2) | copy-done | bytes 786456
  3.7 1.2 %local_chain.1.local_ref = f32[1536,128]{1,0:T(8,128)S(1)} custom-call(f32[3,512,512]{2,1,0:T(8,128)S(1)} %bitcast.5, f32[1536,128]{1,0:T(8,128)S(1)} %bitcast.6), custom_call_target="tpu_custom_call" | custom-call | tf_op jit(solution)/shard_map/local_chain/pallas_call | solution.py:57
  4.8 3.1 %collective-permute-start = (f32[512,128]{1,0:T(8,128)S(1)}, f32[512,128]{1,0:T(8,128)S(1)}, u32[]{:S(2)}, u32[]{:S(2)}) collective-permute-start(f32[512,128]{1,0:T(8,128)S(1)} %slice.8), channel_id=1, source_target_pairs={{0,8},{1,9},{2,10},{3,11},{8,0},{9,1},{10,2},{11,3},{16,17},{17,16... | collective-permute-start | bytes 786440 | tf_op jit(solution)/shard_map/ppermute | solution.py:240
  7.9 3.6 %composites.1 = (bf16[1536,512]{1,0:T(8,128)(2,1)S(1)}, bf16[1536,512]{1,0:T(8,128)(2,1)S(1)}) custom-call(f32[3,512,512]{2,1,0:T(8,128)} %bitcast.4), custom_call_target="tpu_custom_call" | custom-call | flops 1610612736 | bytes 6291456 | tf_op jit(solution)/shard_map/composites/pallas_call | solution.py:93
  11.5 2.7 %collective-permute-done.got_ref = f32[512,128]{1,0:T(8,128)S(1)} collective-permute-done((f32[512,128]{1,0:T(8,128)S(1)}, f32[512,128]{1,0:T(8,128)S(1)}, u32[]{:S(2)}, u32[]{:S(2)}) %collective-permute-start) | collective-permute-done | bytes 262176 | tf_op jit(solution)/shard_map/ppermute | solution.py:240
  14.3 0.4 %relay.2 = (f32[512,128]{1,0:T(8,128)S(1)}, f32[512,128]{1,0:T(8,128)S(1)}) custom-call(bf16[1536,512]{1,0:T(8,128)(2,1)S(1)} %get-tuple-element.10.high_ref, bf16[1536,512]{1,0:T(8,128)(2,1)S(1)} %get-tuple-element.11.low_ref, f32[1536,128]{1,0:T(8,128)S(1)} %local_chain.1.local_ref, f32[512,128]{1,0:T(8,128)S(1)} %collective-permute-done.got_ref, ...), custom_call_target="tpu_custom_call" | custom-call | tf_op jit(solution)/shard_map/relay/pallas_call | solution.py:117
  14.8 1.5 %collective-permute-done.1.got_ref = f32[512,128]{1,0:T(8,128)S(1)} collective-permute-done((f32[512,128]{1,0:T(8,128)S(1)}, f32[512,128]{1,0:T(8,128)S(1)}, u32[]{:S(2)}, u32[]{:S(2)}) %collective-permute-start.1) | collective-permute-done | bytes 262176 | tf_op jit(solution)/shard_map/ppermute | solution.py:240
  16.3 0.4 relay.3
  16.7 0.2 collective-permute-start.2
  17.0 1.4 %collective-permute-done.2.got_ref = f32[512,128]{1,0:T(8,128)S(1)} collective-permute-done((f32[512,128]{1,0:T(8,128)S(1)}, f32[512,128]{1,0:T(8,128)S(1)}, u32[]{:S(2)}, u32[]{:S(2)}) %collective-permute-start.2) | collective-permute-done | bytes 262176 | tf_op jit(solution)/shard_map/ppermute | solution.py:240
  18.4 2.4 %green_blocks.1 = (f32[1536,128]{1,0:T(8,128)}, f32[4,512]{1,0:T(4,128)S(1)}) custom-call(bf16[1536,512]{1,0:T(8,128)(2,1)S(1)} %get-tuple-element.10.high_ref, bf16[1536,512]{1,0:T(8,128)(2,1)S(1)} %get-tuple-element.11.low_ref, f32[1536,128]{1,0:T(8,128)S(1)} %local_chain.1.local_ref, f32[512,128]{1,0:T(8,128)S(1)} %collective-permute-done.2.got_ref, ...), custom_call_target="tpu_custom_call" | custom-call | tf_op jit(solution)/shard_map/green_blocks/pallas_call | solution.py:150
  20.8 1.7 %collective-permute-start.4 = (f32[4,512]{1,0:T(4,128)S(1)}, f32[4,512]{1,0:T(4,128)S(1)}, u32[]{:S(2)}, u32[]{:S(2)}) collective-permute-start(f32[4,512]{1,0:T(4,128)S(1)} %get-tuple-element.17), channel_id=1, source_target_pairs={{0,2},{1,3},{2,0},{3,1},{4,6},{5,7},{6,4},{7,5},{8,10},{9,11},{10,... | collective-permute-start | bytes 24584 | tf_op jit(solution)/shard_map/ppermute | solution.py:227
  22.5 1.3 %collective-permute-start.5 = (f32[4,512]{1,0:T(4,128)S(1)}, f32[4,512]{1,0:T(4,128)S(1)}, u32[]{:S(2)}, u32[]{:S(2)}) collective-permute-start(f32[4,512]{1,0:T(4,128)S(1)} %get-tuple-element.17), channel_id=1, source_target_pairs={{0,3},{1,0},{2,1},{3,2},{4,7},{5,4},{6,5},{7,6},{8,11},{9,8},{10,9... | collective-permute-start | bytes 24584 | tf_op jit(solution)/shard_map/ppermute | solution.py:227
  23.9 0.6 %collective-permute-done.4 = f32[4,512]{1,0:T(4,128)S(1)} collective-permute-done((f32[4,512]{1,0:T(4,128)S(1)}, f32[4,512]{1,0:T(4,128)S(1)}, u32[]{:S(2)}, u32[]{:S(2)}) %collective-permute-start.4) | collective-permute-done | bytes 8224 | tf_op jit(solution)/shard_map/ppermute | solution.py:227
  24.5 0.7 %collective-permute-done.5 = f32[4,512]{1,0:T(4,128)S(1)} collective-permute-done((f32[4,512]{1,0:T(4,128)S(1)}, f32[4,512]{1,0:T(4,128)S(1)}, u32[]{:S(2)}, u32[]{:S(2)}) %collective-permute-start.5) | collective-permute-done | bytes 8224 | tf_op jit(solution)/shard_map/ppermute | solution.py:227
  25.2 1.5 %collective-permute-start.6 = (f32[4,512]{1,0:T(4,128)S(1)}, f32[4,512]{1,0:T(4,128)S(1)}, u32[]{:S(2)}, u32[]{:S(2)}) collective-permute-start(f32[4,512]{1,0:T(4,128)S(1)} %get-tuple-element.20), channel_id=1, source_target_pairs={{0,4},{4,0},{1,5},{5,1},{2,6},{6,2},{3,7},{7,3},{8,12},{12,8},{9,1... | collective-permute-start | bytes 24584 | tf_op jit(solution)/shard_map/ppermute | solution.py:227
  26.7 0.6 %fusion = (f32[]{:T(128)}, f32[]{:T(128)}) fusion(f32[8]{0:T(128)S(1)} %copy-done.4, s32[]{:T(128)S(6)} %select_n.25, s32[]{:T(128)S(6)} %select_n.27, s32[8]{0:T(128)S(1)} %copy-done.5, s32[]{:T(128)S(6)} %axis_index.15), kind=kLoop, calls=%fused_computation.8 | loop fusion | flops 142 | bytes 84 | tf_op jit(solution)/shard_map/reduce_sum | solution.py:253
  28.0 0.8 %collective-permute-done.6 = f32[4,512]{1,0:T(4,128)S(1)} collective-permute-done((f32[4,512]{1,0:T(4,128)S(1)}, f32[4,512]{1,0:T(4,128)S(1)}, u32[]{:S(2)}, u32[]{:S(2)}) %collective-permute-start.6) | collective-permute-done | bytes 8224 | tf_op jit(solution)/shard_map/ppermute | solution.py:227
  28.9 0.6 %multiply_add_fusion.mixed_ref = f32[4,512]{1,0:T(4,128)S(1)} fusion(f32[4,512]{1,0:T(4,128)S(1)} %collective-permute-done.6, f32[4,512]{1,0:T(4,128)S(1)} %get-tuple-element.21, f32[]{:T(128)} %get-tuple-element.19, f32[]{:T(128)S(6)} %mul.14), kind=kLoop, calls=%fused_computation | loop fusion | flops 6144 | bytes 24584 | tf_op jit(solution)/shard_map/add | solution.py:254
  29.5 11.7 %collective-permute-start.7 = (f32[1,512]{1,0:T(1,128)S(1)}, f32[1,512]{1,0:T(1,128)S(1)}, u32[]{:S(2)}, u32[]{:S(2)}) collective-permute-start(f32[1,512]{1,0:T(1,128)S(1)} %slice.9), channel_id=1, source_target_pairs={{0,24},{8,0},{16,8},{24,16},{1,25},{9,1},{17,9},{25,17},{2,26},{10... | collective-permute-start | bytes 6152 | tf_op jit(solution)/shard_map/ppermute | solution.py:227
  41.2 1.1 %copy-done.3 = f32[1536,128]{1,0:T(8,128)S(1)} copy-done((f32[1536,128]{1,0:T(8,128)S(1)}, f32[1536,128]{1,0:T(8,128)}, u32[]{:S(2)}) %copy-start.3) | copy-done | bytes 786456
  42.4 0.4 inner_blocks.1.inner_ref
  42.8 1.5 %scatter_blocks.1 = f32[1536,128]{1,0:T(8,128)} custom-call(bf16[512,512]{1,0:T(8,128)(2,1)S(1)} %copy-done.1, f32[3,128,512]{2,1,0:T(8,128)S(1)} %inner_blocks.1.inner_ref, f32[4,512]{1,0:T(4,128)S(1)} %multiply_add_fusion.mixed_ref, f32[1,512]{1,0:T(1,128)S(1)} %collective-permute-done.7.after_ref), custom_call_target="tpu_custom_call" | custom-call | tf_op jit(solution)/shard_map/scatter_blocks/pallas_call | solution.py:201
  (17 shorter events, 0.3 us)
Async XLA Ops:
  0.6 1.9 %copy-start = (f32[1,3,512,512]{3,2,1,0:T(8,128)S(1)}, f32[1,3,512,512]{3,2,1,0:T(8,128)}, u32[]{:S(2)}) copy-start(f32[1,3,512,512]{3,2,1,0:T(8,128)} %param.5) | copy-start | bytes 9437188
  2.5 1.1 %copy-start.2 = (f32[1,1536,128]{2,1,0:T(8,128)S(1)}, f32[1,1536,128]{2,1,0:T(8,128)}, u32[]{:S(2)}) copy-start(f32[1,1536,128]{2,1,0:T(8,128)} %param.6) | copy-start | bytes 2359300
  4.8 9.4 %collective-permute-start = (f32[512,128]{1,0:T(8,128)S(1)}, f32[512,128]{1,0:T(8,128)S(1)}, u32[]{:S(2)}, u32[]{:S(2)}) collective-permute-start(f32[512,128]{1,0:T(8,128)S(1)} %slice.8), channel_id=1, source_target_pairs={{0,8},{1,9},{2,10},{3,11},{8,0},{9,1},{10,2},{11,3},{16,17},{17,16... | collective-permute-start | bytes 786440 | tf_op jit(solution)/shard_map/ppermute | solution.py:240
  14.7 1.6 %collective-permute-start.1 = (f32[512,128]{1,0:T(8,128)S(1)}, f32[512,128]{1,0:T(8,128)S(1)}, u32[]{:S(2)}, u32[]{:S(2)}) collective-permute-start(f32[512,128]{1,0:T(8,128)S(1)} %get-tuple-element.12), channel_id=1, source_target_pairs={{0,1},{1,0},{2,3},{3,2},{8,16},{9,17},{10,18},{11,19},{16,8},{17,9... | collective-permute-start | bytes 786440 | tf_op jit(solution)/shard_map/ppermute | solution.py:240
  16.7 1.6 %collective-permute-start.2 = (f32[512,128]{1,0:T(8,128)S(1)}, f32[512,128]{1,0:T(8,128)S(1)}, u32[]{:S(2)}, u32[]{:S(2)}) collective-permute-start(f32[512,128]{1,0:T(8,128)S(1)} %get-tuple-element.14), channel_id=1, source_target_pairs={{0,1},{1,0},{2,3},{3,2},{8,9},{9,8},{10,11},{11,10},{16,24},{17,25... | collective-permute-start | bytes 786440 | tf_op jit(solution)/shard_map/ppermute | solution.py:240
  18.4 8.4 %copy-start.4 = (f32[8]{0:T(128)S(1)}, f32[8]{0:T(128)}, u32[]{:S(2)}) copy-start(f32[8]{0:T(128)} %param.8) | copy-start | bytes 100
  18.4 8.4 %copy-start.5 = (s32[8]{0:T(128)S(1)}, s32[8]{0:T(128)}, u32[]{:S(2)}) copy-start(s32[8]{0:T(128)} %param.9) | copy-start | bytes 100
  18.4 22.9 %copy-start.1 = (bf16[512,512]{1,0:T(8,128)(2,1)S(1)}, bf16[512,512]{1,0:T(8,128)(2,1)}, u32[]{:S(2)}) copy-start(bf16[512,512]{1,0:T(8,128)(2,1)} %coupling_ref.3) | copy-start | bytes 1572868
  20.7 3.1 %collective-permute-start.3 = (f32[4,512]{1,0:T(4,128)S(1)}, f32[4,512]{1,0:T(4,128)S(1)}, u32[]{:S(2)}, u32[]{:S(2)}) collective-permute-start(f32[4,512]{1,0:T(4,128)S(1)} %get-tuple-element.17), channel_id=1, source_target_pairs={{0,1},{1,2},{2,3},{3,0},{4,5},{5,6},{6,7},{7,4},{8,9},{9,10},{10,1... | collective-permute-start | bytes 24584 | tf_op jit(solution)/shard_map/ppermute | solution.py:227
  20.8 3.7 %collective-permute-start.4 = (f32[4,512]{1,0:T(4,128)S(1)}, f32[4,512]{1,0:T(4,128)S(1)}, u32[]{:S(2)}, u32[]{:S(2)}) collective-permute-start(f32[4,512]{1,0:T(4,128)S(1)} %get-tuple-element.17), channel_id=1, source_target_pairs={{0,2},{1,3},{2,0},{3,1},{4,6},{5,7},{6,4},{7,5},{8,10},{9,11},{10,... | collective-permute-start | bytes 24584 | tf_op jit(solution)/shard_map/ppermute | solution.py:227
  22.5 2.7 %collective-permute-start.5 = (f32[4,512]{1,0:T(4,128)S(1)}, f32[4,512]{1,0:T(4,128)S(1)}, u32[]{:S(2)}, u32[]{:S(2)}) collective-permute-start(f32[4,512]{1,0:T(4,128)S(1)} %get-tuple-element.17), channel_id=1, source_target_pairs={{0,3},{1,0},{2,1},{3,2},{4,7},{5,4},{6,5},{7,6},{8,11},{9,8},{10,9... | collective-permute-start | bytes 24584 | tf_op jit(solution)/shard_map/ppermute | solution.py:227
  25.2 3.7 %collective-permute-start.6 = (f32[4,512]{1,0:T(4,128)S(1)}, f32[4,512]{1,0:T(4,128)S(1)}, u32[]{:S(2)}, u32[]{:S(2)}) collective-permute-start(f32[4,512]{1,0:T(4,128)S(1)} %get-tuple-element.20), channel_id=1, source_target_pairs={{0,4},{4,0},{1,5},{5,1},{2,6},{6,2},{3,7},{7,3},{8,12},{12,8},{9,1... | collective-permute-start | bytes 24584 | tf_op jit(solution)/shard_map/ppermute | solution.py:227
  29.5 13.2 %collective-permute-start.7 = (f32[1,512]{1,0:T(1,128)S(1)}, f32[1,512]{1,0:T(1,128)S(1)}, u32[]{:S(2)}, u32[]{:S(2)}) collective-permute-start(f32[1,512]{1,0:T(1,128)S(1)} %slice.9), channel_id=1, source_target_pairs={{0,24},{8,0},{16,8},{24,16},{1,25},{9,1},{17,9},{25,17},{2,26},{10... | collective-permute-start | bytes 6152 | tf_op jit(solution)/shard_map/ppermute | solution.py:227
  41.2 1.1 %copy-start.3 = (f32[1536,128]{1,0:T(8,128)S(1)}, f32[1536,128]{1,0:T(8,128)}, u32[]{:S(2)}) copy-start(f32[1536,128]{1,0:T(8,128)} %get-tuple-element.16.green_ref) | copy-start | bytes 2359300

commit v2 on v1

v2 whole, which is shorter than its diff:
```python
import functools

import jax
import jax.numpy as jnp
from jax import lax
from jax.experimental import pallas as pl
from jax.experimental.pallas import tpu as pltpu
from jax.sharding import PartitionSpec as P

F32 = jnp.float32
BF16 = jnp.bfloat16
VMEM = pl.BlockSpec(memory_space=pltpu.VMEM)
SMEM = pl.BlockSpec(memory_space=pltpu.SMEM)
HBM = pl.BlockSpec(memory_space=pltpu.HBM)
PARAMS = pltpu.CompilerParams(vmem_limit_bytes=32 * 1024 * 1024)
WHOLE = pltpu.CompilerParams(vmem_limit_bytes=53 * 1024 * 1024)
PIECES = 2


def split(value):
    high = value.astype(BF16)
    return high, (value - high.astype(F32)).astype(BF16)


def dot(left, right):
    return jnp.dot(left, right, preferred_element_type=F32)


def dot_t(left, right):
    return lax.dot_general(left, right, (((1,), (1,)), ((), ())), preferred_element_type=F32)


def product(left_high, left_low, state):
    high, low = split(state)
    width = state.shape[1]
    both = dot(left_high, jnp.concatenate([high, low], axis=1))
    return both[:, :width] + (both[:, width:] + dot(left_low, high))


def product_rows(state, right_high, right_low):
    high, low = split(state)
    height = state.shape[0]
    both = dot(jnp.concatenate([high, low], axis=0), right_high)
    return both[:height] + (both[height:] + dot(high, right_low))


def local_kernel(mats_ref, srcs_ref, *rest):
    outs, (mats, srcs, sems, src_sem) = rest[:-4], rest[-4:]
    middle_ref, leaving_refs = outs[0], outs[1:]
    count, orbs = mats_ref.shape[0], mats_ref.shape[1]
    src_copy = pltpu.make_async_copy(srcs_ref, srcs, src_sem)
    copies = [
        pltpu.make_async_copy(mats_ref.at[k], mats.at[k], sems.at[k]) for k in range(1, count)
    ]
    src_copy.start()
    for copy in copies:
        copy.start()
    src_copy.wait()
    state = srcs[:orbs, :]
    for k in range(1, count):
        copies[k - 1].wait()
        state = product(*split(mats[k]), state) + srcs[k * orbs : (k + 1) * orbs, :]
        if k < count - 1:
            middle_ref[k - 1] = state
    turned = state.T
    height = turned.shape[0] // len(leaving_refs)
    for piece, leaving_ref in enumerate(leaving_refs):
        leaving_ref[...] = turned[piece * height : (piece + 1) * height, :]


def local_chain(mats, srcs, pieces):
    count, orbs, _ = mats.shape
    width = srcs.shape[1]
    leaving = jax.ShapeDtypeStruct((width // pieces, orbs), F32)
    outs = pl.pallas_call(
        local_kernel,
        out_shape=(jax.ShapeDtypeStruct((count - 2, orbs, width), F32),) + (leaving,) * pieces,
        in_specs=[HBM, HBM],
        out_specs=(VMEM,) * (1 + pieces),
        scratch_shapes=[
            pltpu.VMEM(mats.shape, F32),
            pltpu.VMEM(srcs.shape, F32),
            pltpu.SemaphoreType.DMA((count,)),
            pltpu.SemaphoreType.DMA,
        ],
        compiler_params=WHOLE,
        name="local_chain",
    )(mats, srcs)
    return outs[0], list(outs[1:])


def composite_kernel(mats_ref, middle_ref, high_ref, low_ref):
    full = mats_ref[0]
    count = mats_ref.shape[0]
    for k in range(1, count):
        left_high, left_low = split(mats_ref[k])
        high, low = split(full)
        full = dot(left_high, high) + (dot(left_high, low) + dot(left_low, high))
        if k < count - 1:
            middle_ref[k - 1] = full
    high_ref[...], low_ref[...] = split(full.T)


def composites(mats):
    count, orbs, _ = mats.shape
    shape = jax.ShapeDtypeStruct((orbs, orbs), BF16)
    return pl.pallas_call(
        composite_kernel,
        out_shape=(jax.ShapeDtypeStruct((count - 2, orbs, orbs), F32), shape, shape),
        in_specs=[VMEM],
        out_specs=(VMEM,) * 3,
        compiler_params=PARAMS,
        cost_estimate=pl.CostEstimate(
            flops=6 * (count - 1) * orbs**3, bytes_accessed=8 * count * orbs**2, transcendentals=0
        ),
        name="composites",
    )(mats)


def turned_kernel(
    points, scale, first_ref, srcs_ref, mats_ref, local_ref, strength_ref, shift_ref, _, high_ref, low_ref, turned_ref, weight_ref
):
    orbs = first_ref.shape[1]
    here = lax.axis_index("energy")
    for offset in range(points):
        total = jnp.float32(0.0)
        for mode in range(strength_ref.shape[0]):
            taken = lax.rem(here + shift_ref[mode], points) == lax.rem(here + points - offset, points)
            total = total + jnp.where(taken, strength_ref[mode], 0.0)
        weight_ref[offset : offset + 1, :] = jnp.full((1, orbs), total * scale, F32)
    for k in range(mats_ref.shape[0] + 1):
        columns = slice(k * orbs, (k + 1) * orbs)
        matrix = first_ref[0] if k == 0 else mats_ref[k - 1]
        local = srcs_ref[:orbs, :] if k == 0 else local_ref[k - 1]
        high_ref[:, columns], low_ref[:, columns] = split(matrix.T)
        turned_ref[:, columns] = local.T


def turned_blocks(mats, srcs, middle, local, strength, shift, after, points, scale):
    count, orbs, _ = mats.shape
    width = srcs.shape[1]
    length = (count - 1) * orbs
    shape = jax.ShapeDtypeStruct((orbs, length), BF16)
    return pl.pallas_call(
        functools.partial(turned_kernel, points, scale),
        out_shape=(
            shape,
            shape,
            jax.ShapeDtypeStruct((width, length), F32),
            jax.ShapeDtypeStruct((points, orbs), F32),
        ),
        in_specs=[VMEM, VMEM, VMEM, VMEM, SMEM, SMEM, VMEM],
        out_specs=(VMEM,) * 4,
        compiler_params=PARAMS,
        name="turned_blocks",
    )(mats, srcs, middle, local, strength, shift, after)


def relay_kernel(step, first, high_ref, low_ref, offset_ref, got_ref, _, *rest):
    out_ref, kept_ref = rest[-2:]
    got = got_ref[...]
    out_ref[...] = product_rows(got, high_ref[...], low_ref[...]) + offset_ref[...]
    other = 0.0 if first else rest[0][...]
    kept_ref[...] = jnp.where(lax.axis_index("cuts") == step, got, other)


def relay(step, last, offset, got, incoming, after):
    shape = jax.ShapeDtypeStruct(got.shape, F32)
    args = [*last, offset, got, after] + ([] if incoming is None else [incoming])
    return pl.pallas_call(
        functools.partial(relay_kernel, step, incoming is None),
        out_shape=(shape, shape),
        in_specs=[VMEM] * len(args),
        out_specs=(VMEM, VMEM),
        compiler_params=PARAMS,
        name="relay",
    )(*args)


def green_kernel(
    step, piece, high_ref, low_ref, turned_ref, last_high_ref, last_low_ref, offset_ref, got_ref, incoming_ref, *rest
):
    green_ref, sums_ref = rest[-2:]
    height, orbs = got_ref.shape
    length = high_ref.shape[1]
    rows = slice(piece * height, (piece + 1) * height)
    state = jnp.where(lax.axis_index("cuts") == step, got_ref[...], incoming_ref[...])
    sums = [jnp.sum(state * state, axis=0, keepdims=True)]
    green = product_rows(state, high_ref[...], low_ref[...]) + turned_ref[rows, :]
    green_ref[:, :length] = green
    for k in range(length // orbs):
        block = green[:, k * orbs : (k + 1) * orbs]
        sums.append(jnp.sum(block * block, axis=0, keepdims=True))
    block = product_rows(state, last_high_ref[...], last_low_ref[...]) + offset_ref[...]
    green_ref[:, length:] = block
    sums.append(jnp.sum(block * block, axis=0, keepdims=True))
    total = jnp.concatenate(sums, axis=0)
    sums_ref[...] = total if len(rest) == 2 else total + rest[0][...]


def green_piece(step, piece, blocks, last, offset, got, incoming, sums):
    height, orbs = got.shape
    count = blocks[0].shape[1] // orbs + 1
    args = [*blocks, *last, offset, got, incoming] + ([] if sums is None else [sums])
    return pl.pallas_call(
        functools.partial(green_kernel, step, piece),
        out_shape=(
            jax.ShapeDtypeStruct((height, count * orbs), F32),
            jax.ShapeDtypeStruct((count + 1, orbs), F32),
        ),
        in_specs=[VMEM] * len(args),
        out_specs=(VMEM, VMEM),
        compiler_params=PARAMS,
        name="green_piece",
    )(*args)


def inner_kernel(coupling_ref, *rest):
    green_refs, (inner_ref, turned_ref) = rest[:-2], rest[-2:]
    orbs = coupling_ref.shape[0]
    coupling = coupling_ref[...]
    green = jnp.concatenate([g[...] for g in green_refs], axis=0)
    low = green.astype(BF16)
    for k in range(low.shape[1] // orbs):
        columns = slice(k * orbs, (k + 1) * orbs)
        inner_ref[:, columns] = dot(low[:, columns], coupling)
        turned_ref[columns, :] = green[:, columns].T


def inner_blocks(coupling, pieces):
    height, length = pieces[0].shape
    width = height * len(pieces)
    return pl.pallas_call(
        inner_kernel,
        out_shape=(
            jax.ShapeDtypeStruct((width, length), F32),
            jax.ShapeDtypeStruct((length, width), F32),
        ),
        in_specs=[VMEM] * (1 + len(pieces)),
        out_specs=(VMEM, VMEM),
        compiler_params=PARAMS,
        cost_estimate=pl.CostEstimate(
            flops=2 * width * length * coupling.shape[0], bytes_accessed=12 * width * length, transcendentals=0
        ),
        name="inner_blocks",
    )(coupling, *pieces)


def scatter_kernel(coupling_ref, inner_ref, green_ref, *rest):
    mixed_ref, *after_refs, out_ref, kept_ref, staged, sems, kept_sem = rest
    kept_copy = pltpu.make_async_copy(green_ref, kept_ref, kept_sem)
    kept_copy.start()
    orbs = coupling_ref.shape[0]
    count = inner_ref.shape[1] // orbs
    here = lax.axis_index("cuts")
    after = jnp.where(lax.rem(here, 2) == 0, after_refs[0][1:2, :], after_refs[1][1:2, :])
    rows = [mixed_ref[k : k + 1, :] for k in range(count + 1)]
    rows.append(jnp.where(here == lax.axis_size("cuts") - 1, 0.0, after))
    coupling = coupling_ref[...]
    copies = []
    for k in range(count):
        selfen = rows[k + 1] + 0.5 * (rows[k] + rows[k + 2])
        columns = slice(k * orbs, (k + 1) * orbs)
        scaled = (inner_ref[:, columns] * selfen).astype(BF16)
        staged[columns, :] = dot_t(coupling, scaled)
        copies.append(pltpu.make_async_copy(staged.at[columns], out_ref.at[columns], sems.at[k]))
        copies[-1].start()
    for copy in copies:
        copy.wait()
    kept_copy.wait()


def scatter_blocks(coupling, inner, green, mixed, after):
    width, length = inner.shape
    orbs = coupling.shape[0]
    shape = jax.ShapeDtypeStruct((length, width), F32)
    return pl.pallas_call(
        scatter_kernel,
        out_shape=(shape, shape),
        in_specs=[VMEM] * (4 + len(after)),
        out_specs=(HBM, HBM),
        scratch_shapes=[
            pltpu.VMEM((length, width), F32),
            pltpu.SemaphoreType.DMA((length // orbs,)),
            pltpu.SemaphoreType.DMA,
        ],
        compiler_params=PARAMS,
        name="scatter_blocks",
    )(coupling, inner, green, mixed, *after)


def paired(lower, cuts, group):
    pairs = []
    for c in range(cuts):
        for g in range(group):
            if c in lower:
                to = (c + 1, g)
            elif c - 1 in lower:
                to = (c - 1, g)
            else:
                to = (c, g ^ 1 if g ^ 1 < group else g)
            pairs.append((c * group + g, to[0] * group + to[1]))
    return pairs


def turned_round(value, axis, offset):
    devices = lax.axis_size(axis)
    return lax.ppermute(value, axis, [(i, (i + offset) % devices) for i in range(devices)])


def body(transfer, source, coupling, strength, mode_shift):
    mats, srcs = transfer[0], source[0]
    width = srcs.shape[1]
    cuts, group, points = (lax.axis_size(a) for a in ("cuts", "group", "energy"))
    pieces = PIECES if width % (8 * PIECES) == 0 else 1
    local, offsets = local_chain(mats, srcs, pieces)
    middle, *last = composites(mats)
    leaving, incoming, blocks = offsets, [None] * pieces, None
    for step in range(1, cuts):
        pairs = paired([step - 1], cuts, group)
        got = [lax.ppermute(piece, ("cuts", "group"), pairs) for piece in leaving]
        if step < cuts - 1:
            leaving, after = [], last[0] if blocks is None else weights
            for piece in range(pieces):
                after, incoming[piece] = relay(
                    step, last, offsets[piece], got[piece], incoming[piece], after
                )
                leaving.append(after)
        if blocks is None:
            *blocks, weights = turned_blocks(
                mats, srcs, middle, local, strength, mode_shift, leaving[-1], points, 1.0 / (width * group)
            )
    green, sums = [], None
    for piece in range(pieces):
        part, sums = green_piece(
            cuts - 1, piece, blocks, last, offsets[piece], got[piece], incoming[piece], sums
        )
        green.append(part)

    parts = [turned_round(sums, "group", k) for k in range(1, group)]
    total = sums + sum(parts)
    inner, kept = inner_blocks(coupling, green)
    mixed = total * weights[:1]
    for k in range(1, points):
        mixed = mixed + turned_round(total, "energy", k) * weights[k : k + 1]
    after = [
        lax.ppermute(mixed, ("cuts", "group"), paired(range(first, cuts - 1, 2), cuts, group))
        for first in (0, 1)
    ]
    scattered, kept = scatter_blocks(coupling, inner, kept, mixed, after)
    return kept[None], scattered[None]


def solution(mesh):
    in_specs = (P("energy", "cuts", None, None), P("energy", "cuts", "group"), P(), P(), P())
    out_specs = (P("energy", "cuts", "group"), P("energy", "cuts", "group"))
    return jax.shard_map(body, mesh=mesh, in_specs=in_specs, out_specs=out_specs, check_vma=False)
```

time: 44.5 us -> 36.5 us (0.82)
  the two profiles are of different devices: /device:TPU:0 before, /device:TPU:16 now
where the time goes in v2:
time: 36.5 us; the launch traced here: 36.3 us
  waiting for transfers between devices  12.9 us (35%)
  starting transfers between devices  12.3 us (34%)
  Pallas kernels  10.3 us (28%)
  between operations  0.77 us (2%)
    ppermute x6, starting transfers between devices, body(): got = [lax.ppermute(piece, ('cuts', 'group'), pairs) for piece in leaving]  7.27 us
    ppermute x6, waiting for transfers between devices, body(): got = [lax.ppermute(piece, ('cuts', 'group'), pairs) for piece in leaving]  6.13 us
    ppermute x4, starting transfers between devices, turned_round(): lax.ppermute(value, axis, [(i, (i + offset) % devices) for i in range(dev...  4.51 us
    ppermute x4, waiting for transfers between devices, turned_round(): lax.ppermute(value, axis, [(i, (i + offset) % devices) for i in range(dev...  3.5 us
    ppermute x2, waiting for transfers between devices, body(): lax.ppermute(mixed, ('cuts', 'group'), paired(range(first, cuts - 1, 2),...  3.25 us
    pallas_call x1, Pallas kernels, local_chain(): pl.pallas_call(local_kernel, out_shape=(jax.ShapeDtypeStruct((count - 2,...  2.61 us
    pallas_call x1, Pallas kernels, composites(): pl.pallas_call(composite_kernel, out_shape=(jax.ShapeDtypeStruct((count -...  2.13 us
    pallas_call x1, Pallas kernels, scatter_blocks(): pl.pallas_call(scatter_kernel, out_shape=(shape, shape), in_specs=[VMEM]...  1.4 us
  transfers between devices with their start and end apart: 12, of which 10 were waited for; matrix products, arithmetic and copies ran while one was open for 0% of the time, Pallas kernels for 16%

profile of v2, /device:TPU:16, one launch (start us, length us, event | category | flops | bytes accessed | tf_op | source)
XLA Modules:
  0.0 36.3 jit_solution(9790862324692715866)
XLA Ops:
  0.6 2.6 %local_chain.1 = (f32[1,512,128]{2,1,0:T(8,128)S(1)}, f32[64,512]{1,0:T(8,128)S(1)}, f32[64,512]{1,0:T(8,128)S(1)}) custom-call(f32[3,512,512]{2,1,0:T(8,128)} %bitcast.6, f32[1536,128]{1,0:T(8,128)} %bitcast.9), custom_call_target="tpu_custom_call" | custom-call | tf_op jit(solution)/shard_map/local_chain/pallas_call | solution.py:75
  3.4 0.5 %collective-permute-start = (f32[64,512]{1,0:T(8,128)S(1)}, f32[64,512]{1,0:T(8,128)S(1)}, u32[]{:S(2)}, u32[]{:S(2)}) collective-permute-start(f32[64,512]{1,0:T(8,128)S(1)} %get-tuple-element.32.offset_ref), channel_id=1, source_target_pairs={{0,8},{1,9},{2,10},{3,11},{8,0},{9,1},{10,2},{11,3},{16,17},{17,16... | collective-permute-start | bytes 393224 | tf_op jit(solution)/shard_map/ppermute | solution.py:321
  3.8 2.1 %composites.1 = (f32[1,512,512]{2,1,0:T(8,128)S(1)}, bf16[512,512]{1,0:T(8,128)(2,1)S(1)}, bf16[512,512]{1,0:T(8,128)(2,1)S(1)}) custom-call(f32[3,512,512]{2,1,0:T(8,128)S(1)} %bitcast.7), custom_call_target="tpu_custom_call" | custom-call | flops 1610612736 | bytes 6291456 | tf_op jit(solution)/shard_map/composites/pallas_call | solution.py:107
  6.3 4.2 %collective-permute-start.2 = (f32[64,512]{1,0:T(8,128)S(1)}, f32[64,512]{1,0:T(8,128)S(1)}, u32[]{:S(2)}, u32[]{:S(2)}) collective-permute-start(f32[64,512]{1,0:T(8,128)S(1)} %get-tuple-element.34._), channel_id=1, source_target_pairs={{0,1},{1,0},{2,3},{3,2},{8,16},{9,17},{10,18},{11,19},{16,8},{17,9... | collective-permute-start | bytes 393224 | tf_op jit(solution)/shard_map/ppermute | solution.py:321
  10.8 1.4 %collective-permute-start.4 = (f32[64,512]{1,0:T(8,128)S(1)}, f32[64,512]{1,0:T(8,128)S(1)}, u32[]{:S(2)}, u32[]{:S(2)}) collective-permute-start(f32[64,512]{1,0:T(8,128)S(1)} %get-tuple-element.35._), channel_id=1, source_target_pairs={{0,1},{1,0},{2,3},{3,2},{8,16},{9,17},{10,18},{11,19},{16,8},{17,9... | collective-permute-start | bytes 393224 | tf_op jit(solution)/shard_map/ppermute | solution.py:321
  12.2 1.3 %turned_blocks.1 = (bf16[512,1024]{1,0:T(8,128)(2,1)S(1)}, bf16[512,1024]{1,0:T(8,128)(2,1)S(1)}, f32[128,1024]{1,0:T(8,128)S(1)}, f32[2,512]{1,0:T(2,128)S(1)}) custom-call(f32[3,512,512]{2,1,0:T(8,128)S(1)} %bitcast.8, f32[1536,128]{1,0:T(8,128)S(1)} %bitcast.10, f32[1,512,512]{2,1,0:T(8,128)S(1)} %get-tuple-element.28.mats_ref, ...), custom_call_target="tpu_custom_call" | custom-call | tf_op jit(solution)/shard_map/turned_blocks/pallas_call | solution.py:144
  13.5 1.3 %collective-permute-done.2.got_ref = f32[64,512]{1,0:T(8,128)S(1)} collective-permute-done((f32[64,512]{1,0:T(8,128)S(1)}, f32[64,512]{1,0:T(8,128)S(1)}, u32[]{:S(2)}, u32[]{:S(2)}) %collective-permute-start.2) | collective-permute-done | bytes 131104 | tf_op jit(solution)/shard_map/ppermute | solution.py:321
  15.2 1.0 %collective-permute-done.4.got_ref = f32[64,512]{1,0:T(8,128)S(1)} collective-permute-done((f32[64,512]{1,0:T(8,128)S(1)}, f32[64,512]{1,0:T(8,128)S(1)}, u32[]{:S(2)}, u32[]{:S(2)}) %collective-permute-start.4) | collective-permute-done | bytes 131104 | tf_op jit(solution)/shard_map/ppermute | solution.py:321
  16.5 1.1 %collective-permute-start.5 = (f32[64,512]{1,0:T(8,128)S(1)}, f32[64,512]{1,0:T(8,128)S(1)}, u32[]{:S(2)}, u32[]{:S(2)}) collective-permute-start(f32[64,512]{1,0:T(8,128)S(1)} %get-tuple-element.45), channel_id=1, source_target_pairs={{0,1},{1,0},{2,3},{3,2},{8,9},{9,8},{10,11},{11,10},{16,24},{17,25... | collective-permute-start | bytes 393224 | tf_op jit(solution)/shard_map/ppermute | solution.py:321
  17.6 3.0 %collective-permute-done.3.got_ref = f32[64,512]{1,0:T(8,128)S(1)} collective-permute-done((f32[64,512]{1,0:T(8,128)S(1)}, f32[64,512]{1,0:T(8,128)S(1)}, u32[]{:S(2)}, u32[]{:S(2)}) %collective-permute-start.3) | collective-permute-done | bytes 131104 | tf_op jit(solution)/shard_map/ppermute | solution.py:321
  20.6 0.7 %green_piece.2 = (f32[64,1536]{1,0:T(8,128)S(1)}, f32[4,512]{1,0:T(4,128)S(1)}) custom-call(bf16[512,1024]{1,0:T(8,128)(2,1)S(1)} %get-tuple-element.36.high_ref, bf16[512,1024]{1,0:T(8,128)(2,1)S(1)} %get-tuple-element.37.low_ref, f32[128,1024]{1,0:T(8,128)S(1)} %get-tuple-element.38.turned_ref, ...), custom_call_target="tpu_custom_call" | custom-call | tf_op jit(solution)/shard_map/green_piece/pallas_call | solution.py:205
  21.3 0.7 %collective-permute-done.5.got_ref = f32[64,512]{1,0:T(8,128)S(1)} collective-permute-done((f32[64,512]{1,0:T(8,128)S(1)}, f32[64,512]{1,0:T(8,128)S(1)}, u32[]{:S(2)}, u32[]{:S(2)}) %collective-permute-start.5) | collective-permute-done | bytes 131104 | tf_op jit(solution)/shard_map/ppermute | solution.py:321
  22.0 0.7 %green_piece.3 = (f32[64,1536]{1,0:T(8,128)S(1)}, f32[4,512]{1,0:T(4,128)S(1)}) custom-call(bf16[512,1024]{1,0:T(8,128)(2,1)S(1)} %get-tuple-element.36.high_ref, bf16[512,1024]{1,0:T(8,128)(2,1)S(1)} %get-tuple-element.37.low_ref, f32[128,1024]{1,0:T(8,128)S(1)} %get-tuple-element.38.turned_ref, ...), custom_call_target="tpu_custom_call" | custom-call | tf_op jit(solution)/shard_map/green_piece/pallas_call | solution.py:205
  22.8 1.6 %collective-permute-start.7 = (f32[4,512]{1,0:T(4,128)S(1)}, f32[4,512]{1,0:T(4,128)S(1)}, u32[]{:S(2)}, u32[]{:S(2)}) collective-permute-start(f32[4,512]{1,0:T(4,128)S(1)} %get-tuple-element.51), channel_id=1, source_target_pairs={{0,2},{1,3},{2,0},{3,1},{4,6},{5,7},{6,4},{7,5},{8,10},{9,11},{10,... | collective-permute-start | bytes 24584 | tf_op jit(solution)/shard_map/ppermute | solution.py:308
  24.3 1.4 %collective-permute-start.8 = (f32[4,512]{1,0:T(4,128)S(1)}, f32[4,512]{1,0:T(4,128)S(1)}, u32[]{:S(2)}, u32[]{:S(2)}) collective-permute-start(f32[4,512]{1,0:T(4,128)S(1)} %get-tuple-element.51), channel_id=1, source_target_pairs={{0,3},{1,0},{2,1},{3,2},{4,7},{5,4},{6,5},{7,6},{8,11},{9,8},{10,9... | collective-permute-start | bytes 24584 | tf_op jit(solution)/shard_map/ppermute | solution.py:308
  25.8 0.7 %collective-permute-done.7 = f32[4,512]{1,0:T(4,128)S(1)} collective-permute-done((f32[4,512]{1,0:T(4,128)S(1)}, f32[4,512]{1,0:T(4,128)S(1)}, u32[]{:S(2)}, u32[]{:S(2)}) %collective-permute-start.7) | collective-permute-done | bytes 8224 | tf_op jit(solution)/shard_map/ppermute | solution.py:308
  26.5 0.6 %collective-permute-done.8 = f32[4,512]{1,0:T(4,128)S(1)} collective-permute-done((f32[4,512]{1,0:T(4,128)S(1)}, f32[4,512]{1,0:T(4,128)S(1)}, u32[]{:S(2)}, u32[]{:S(2)}) %collective-permute-start.8) | collective-permute-done | bytes 8224 | tf_op jit(solution)/shard_map/ppermute | solution.py:308
  27.1 1.5 %collective-permute-start.9 = (f32[4,512]{1,0:T(4,128)S(1)}, f32[4,512]{1,0:T(4,128)S(1)}, u32[]{:S(2)}, u32[]{:S(2)}) collective-permute-start(f32[4,512]{1,0:T(4,128)S(1)} %add_add_fusion), channel_id=1, source_target_pairs={{0,4},{4,0},{1,5},{5,1},{2,6},{6,2},{3,7},{7,3},{8,12},{12,8},{9,1... | collective-permute-start | bytes 24584 | tf_op jit(solution)/shard_map/ppermute | solution.py:308
  28.6 2.1 %collective-permute-done.9 = f32[4,512]{1,0:T(4,128)S(1)} collective-permute-done((f32[4,512]{1,0:T(4,128)S(1)}, f32[4,512]{1,0:T(4,128)S(1)}, u32[]{:S(2)}, u32[]{:S(2)}) %collective-permute-start.9) | collective-permute-done | bytes 8224 | tf_op jit(solution)/shard_map/ppermute | solution.py:308
  30.7 0.5 %collective-permute-start.10 = (f32[4,512]{1,0:T(4,128)S(1)}, f32[4,512]{1,0:T(4,128)S(1)}, u32[]{:S(2)}, u32[]{:S(2)}) collective-permute-start(f32[4,512]{1,0:T(4,128)S(1)} %multiply_add_fusion.rest_0_), channel_id=1, source_target_pairs={{0,8},{1,9},{2,10},{3,11},{8,0},{9,1},{10,2},{11,3},{16,24},{17,25... | collective-permute-start | bytes 24584 | tf_op jit(solution)/shard_map/ppermute | solution.py:347
  31.3 0.4 %inner_blocks.1 = (f32[128,1536]{1,0:T(8,128)S(1)}, f32[1536,128]{1,0:T(8,128)S(1)}) custom-call(bf16[512,512]{1,0:T(8,128)(2,1)S(1)} %copy-done.2, f32[64,1536]{1,0:T(8,128)S(1)} %get-tuple-element.43.rest_0_, f32[64,1536]{1,0:T(8,128)S(1)} %get-tuple-element.48.rest_1_), custom_call_target="tpu_custom_call" | custom-call | flops 201326592 | bytes 2359296 | tf_op jit(solution)/shard_map/inner_blocks/pallas_call | solution.py:233
  31.7 2.7 %collective-permute-done.10.rest_1_ = f32[4,512]{1,0:T(4,128)S(1)} collective-permute-done((f32[4,512]{1,0:T(4,128)S(1)}, f32[4,512]{1,0:T(4,128)S(1)}, u32[]{:S(2)}, u32[]{:S(2)}) %collective-permute-start.10) | collective-permute-done | bytes 8224 | tf_op jit(solution)/shard_map/ppermute | solution.py:347
  34.4 0.5 %collective-permute-done.11.rest_2_ = f32[4,512]{1,0:T(4,128)S(1)} collective-permute-done((f32[4,512]{1,0:T(4,128)S(1)}, f32[4,512]{1,0:T(4,128)S(1)}, u32[]{:S(2)}, u32[]{:S(2)}) %collective-permute-start.11) | collective-permute-done | bytes 8224 | tf_op jit(solution)/shard_map/ppermute | solution.py:347
  34.9 1.4 %scatter_blocks.1 = (f32[1536,128]{1,0:T(8,128)}, f32[1536,128]{1,0:T(8,128)}) custom-call(bf16[512,512]{1,0:T(8,128)(2,1)S(1)} %copy-done.2, f32[128,1536]{1,0:T(8,128)S(1)} %get-tuple-element.49.inner_ref, f32[1536,128]{1,0:T(8,128)S(1)} %get-tuple-element.50.green_ref, f32[4,512]{1,0:T(4,128)S(1)} %multiply_add_fusion.rest_0_, ...), custom_call_target="tpu_custom_call" | custom-call | tf_op jit(solution)/shard_map/scatter_blocks/pallas_call | solution.py:277
  (24 shorter events, 1.6 us)
Async XLA Ops:
  0.6 3.2 %copy-start = (f32[1,3,512,512]{3,2,1,0:T(8,128)S(1)}, f32[1,3,512,512]{3,2,1,0:T(8,128)}, u32[]{:S(2)}) copy-start(f32[1,3,512,512]{3,2,1,0:T(8,128)} %param.5) | copy-start | bytes 9437188
  3.3 2.7 %collective-permute-start.1 = (f32[64,512]{1,0:T(8,128)S(1)}, f32[64,512]{1,0:T(8,128)S(1)}, u32[]{:S(2)}, u32[]{:S(2)}) collective-permute-start(f32[64,512]{1,0:T(8,128)S(1)} %get-tuple-element.33.offset_ref), channel_id=1, source_target_pairs={{0,8},{1,9},{2,10},{3,11},{8,0},{9,1},{10,2},{11,3},{16,17},{17,16... | collective-permute-start | bytes 393224 | tf_op jit(solution)/shard_map/ppermute | solution.py:321
  3.3 8.9 %copy-start.1 = (f32[1,1536,128]{2,1,0:T(8,128)S(1)}, f32[1,1536,128]{2,1,0:T(8,128)}, u32[]{:S(2)}) copy-start(f32[1,1536,128]{2,1,0:T(8,128)} %param.6) | copy-start | bytes 2359300
  3.3 8.8 %copy-start.3 = (f32[8]{0:T(128)S(1)}, f32[8]{0:T(128)}, u32[]{:S(2)}) copy-start(f32[8]{0:T(128)} %strength_ref.1) | copy-start | bytes 100
  3.4 8.8 %copy-start.4 = (s32[8]{0:T(128)S(1)}, s32[8]{0:T(128)}, u32[]{:S(2)}) copy-start(s32[8]{0:T(128)} %shift_ref.1) | copy-start | bytes 100
  3.4 7.2 %collective-permute-start = (f32[64,512]{1,0:T(8,128)S(1)}, f32[64,512]{1,0:T(8,128)S(1)}, u32[]{:S(2)}, u32[]{:S(2)}) collective-permute-start(f32[64,512]{1,0:T(8,128)S(1)} %get-tuple-element.32.offset_ref), channel_id=1, source_target_pairs={{0,8},{1,9},{2,10},{3,11},{8,0},{9,1},{10,2},{11,3},{16,17},{17,16... | collective-permute-start | bytes 393224 | tf_op jit(solution)/shard_map/ppermute | solution.py:321
  6.3 8.5 %collective-permute-start.2 = (f32[64,512]{1,0:T(8,128)S(1)}, f32[64,512]{1,0:T(8,128)S(1)}, u32[]{:S(2)}, u32[]{:S(2)}) collective-permute-start(f32[64,512]{1,0:T(8,128)S(1)} %get-tuple-element.34._), channel_id=1, source_target_pairs={{0,1},{1,0},{2,3},{3,2},{8,16},{9,17},{10,18},{11,19},{16,8},{17,9... | collective-permute-start | bytes 393224 | tf_op jit(solution)/shard_map/ppermute | solution.py:321
  10.8 5.4 %collective-permute-start.4 = (f32[64,512]{1,0:T(8,128)S(1)}, f32[64,512]{1,0:T(8,128)S(1)}, u32[]{:S(2)}, u32[]{:S(2)}) collective-permute-start(f32[64,512]{1,0:T(8,128)S(1)} %get-tuple-element.35._), channel_id=1, source_target_pairs={{0,1},{1,0},{2,3},{3,2},{8,16},{9,17},{10,18},{11,19},{16,8},{17,9... | collective-permute-start | bytes 393224 | tf_op jit(solution)/shard_map/ppermute | solution.py:321
  15.1 5.5 %collective-permute-start.3 = (f32[64,512]{1,0:T(8,128)S(1)}, f32[64,512]{1,0:T(8,128)S(1)}, u32[]{:S(2)}, u32[]{:S(2)}) collective-permute-start(f32[64,512]{1,0:T(8,128)S(1)} %get-tuple-element.41._), channel_id=1, source_target_pairs={{0,1},{1,0},{2,3},{3,2},{8,9},{9,8},{10,11},{11,10},{16,24},{17,25... | collective-permute-start | bytes 393224 | tf_op jit(solution)/shard_map/ppermute | solution.py:321
  16.5 5.5 %collective-permute-start.5 = (f32[64,512]{1,0:T(8,128)S(1)}, f32[64,512]{1,0:T(8,128)S(1)}, u32[]{:S(2)}, u32[]{:S(2)}) collective-permute-start(f32[64,512]{1,0:T(8,128)S(1)} %get-tuple-element.45), channel_id=1, source_target_pairs={{0,1},{1,0},{2,3},{3,2},{8,9},{9,8},{10,11},{11,10},{16,24},{17,25... | collective-permute-start | bytes 393224 | tf_op jit(solution)/shard_map/ppermute | solution.py:321
  20.6 10.6 %copy-start.2 = (bf16[512,512]{1,0:T(8,128)(2,1)S(1)}, bf16[512,512]{1,0:T(8,128)(2,1)}, u32[]{:S(2)}) copy-start(bf16[512,512]{1,0:T(8,128)(2,1)} %coupling_ref.3) | copy-start | bytes 1572868
  22.7 3.1 %collective-permute-start.6 = (f32[4,512]{1,0:T(4,128)S(1)}, f32[4,512]{1,0:T(4,128)S(1)}, u32[]{:S(2)}, u32[]{:S(2)}) collective-permute-start(f32[4,512]{1,0:T(4,128)S(1)} %get-tuple-element.51), channel_id=1, source_target_pairs={{0,1},{1,2},{2,3},{3,0},{4,5},{5,6},{6,7},{7,4},{8,9},{9,10},{10,1... | collective-permute-start | bytes 24584 | tf_op jit(solution)/shard_map/ppermute | solution.py:308
  22.8 3.7 %collective-permute-start.7 = (f32[4,512]{1,0:T(4,128)S(1)}, f32[4,512]{1,0:T(4,128)S(1)}, u32[]{:S(2)}, u32[]{:S(2)}) collective-permute-start(f32[4,512]{1,0:T(4,128)S(1)} %get-tuple-element.51), channel_id=1, source_target_pairs={{0,2},{1,3},{2,0},{3,1},{4,6},{5,7},{6,4},{7,5},{8,10},{9,11},{10,... | collective-permute-start | bytes 24584 | tf_op jit(solution)/shard_map/ppermute | solution.py:308
  24.3 2.8 %collective-permute-start.8 = (f32[4,512]{1,0:T(4,128)S(1)}, f32[4,512]{1,0:T(4,128)S(1)}, u32[]{:S(2)}, u32[]{:S(2)}) collective-permute-start(f32[4,512]{1,0:T(4,128)S(1)} %get-tuple-element.51), channel_id=1, source_target_pairs={{0,3},{1,0},{2,1},{3,2},{4,7},{5,4},{6,5},{7,6},{8,11},{9,8},{10,9... | collective-permute-start | bytes 24584 | tf_op jit(solution)/shard_map/ppermute | solution.py:308
  27.1 3.7 %collective-permute-start.9 = (f32[4,512]{1,0:T(4,128)S(1)}, f32[4,512]{1,0:T(4,128)S(1)}, u32[]{:S(2)}, u32[]{:S(2)}) collective-permute-start(f32[4,512]{1,0:T(4,128)S(1)} %add_add_fusion), channel_id=1, source_target_pairs={{0,4},{4,0},{1,5},{5,1},{2,6},{6,2},{3,7},{7,3},{8,12},{12,8},{9,1... | collective-permute-start | bytes 24584 | tf_op jit(solution)/shard_map/ppermute | solution.py:308
  30.7 3.7 %collective-permute-start.10 = (f32[4,512]{1,0:T(4,128)S(1)}, f32[4,512]{1,0:T(4,128)S(1)}, u32[]{:S(2)}, u32[]{:S(2)}) collective-permute-start(f32[4,512]{1,0:T(4,128)S(1)} %multiply_add_fusion.rest_0_), channel_id=1, source_target_pairs={{0,8},{1,9},{2,10},{3,11},{8,0},{9,1},{10,2},{11,3},{16,24},{17,25... | collective-permute-start | bytes 24584 | tf_op jit(solution)/shard_map/ppermute | solution.py:347
  31.3 3.7 %collective-permute-start.11 = (f32[4,512]{1,0:T(4,128)S(1)}, f32[4,512]{1,0:T(4,128)S(1)}, u32[]{:S(2)}, u32[]{:S(2)}) collective-permute-start(f32[4,512]{1,0:T(4,128)S(1)} %multiply_add_fusion.rest_0_), channel_id=1, source_target_pairs={{0,1},{1,0},{2,3},{3,2},{8,16},{9,17},{10,18},{11,19},{16,8},{17,9... | collective-permute-start | bytes 24584 | tf_op jit(solution)/shard_map/ppermute | solution.py:347

commit v3 on v2

--- a/solution.py
+++ b/solution.py
@@ -44,77 +44,104 @@
     return both[:height] + (both[height:] + dot(high, right_low))
 
 
-def local_kernel(mats_ref, srcs_ref, *rest):
-    outs, (mats, srcs, sems, src_sem) = rest[:-4], rest[-4:]
-    middle_ref, leaving_refs = outs[0], outs[1:]
+def chain_step(matrix, state, srcs):
+    return product(*split(matrix), state) + srcs
+
+
+def store_pieces(refs, state):
+    turned = state.T
+    height = turned.shape[0] // len(refs)
+    for piece, ref in enumerate(refs):
+        ref[...] = turned[piece * height : (piece + 1) * height, :]
+
+
+def first_kernel(mats_ref, srcs_ref, *rest):
+    leaving_refs, (mats, srcs, sems, src_sem) = rest[:-4], rest[-4:]
     count, orbs = mats_ref.shape[0], mats_ref.shape[1]
-    src_copy = pltpu.make_async_copy(srcs_ref, srcs, src_sem)
-    copies = [
-        pltpu.make_async_copy(mats_ref.at[k], mats.at[k], sems.at[k]) for k in range(1, count)
-    ]
-    src_copy.start()
-    for copy in copies:
-        copy.start()
-    src_copy.wait()
-    state = srcs[:orbs, :]
-    for k in range(1, count):
-        copies[k - 1].wait()
-        state = product(*split(mats[k]), state) + srcs[k * orbs : (k + 1) * orbs, :]
-        if k < count - 1:
-            middle_ref[k - 1] = state
-    turned = state.T
-    height = turned.shape[0] // len(leaving_refs)
-    for piece, leaving_ref in enumerate(leaving_refs):
-        leaving_ref[...] = turned[piece * height : (piece + 1) * height, :]
-
-
-def local_chain(mats, srcs, pieces):
+    first = lax.axis_index("cuts") == 0
+
+    @pl.when(first)
+    def _():
+        src_copy = pltpu.make_async_copy(srcs_ref, srcs, src_sem)
+        copies = [
+            pltpu.make_async_copy(mats_ref.at[k], mats.at[k], sems.at[k]) for k in range(1, count)
+        ]
+        src_copy.start()
+        for copy in copies:
+            copy.start()
+        src_copy.wait()
+        state = srcs[:orbs, :]
+        for k in range(1, count):
+            copies[k - 1].wait()
+            state = chain_step(mats[k], state, srcs[k * orbs : (k + 1) * orbs, :])
+        store_pieces(leaving_refs, state)
+
+    @pl.when(jnp.logical_not(first))
+    def _():
+        for ref in leaving_refs:
+            ref[...] = jnp.zeros_like(ref)
+
+
+def first_chain(mats, srcs, pieces):
     count, orbs, _ = mats.shape
     width = srcs.shape[1]
     leaving = jax.ShapeDtypeStruct((width // pieces, orbs), F32)
-    outs = pl.pallas_call(
-        local_kernel,
-        out_shape=(jax.ShapeDtypeStruct((count - 2, orbs, width), F32),) + (leaving,) * pieces,
-        in_specs=[HBM, HBM],
-        out_specs=(VMEM,) * (1 + pieces),
-        scratch_shapes=[
-            pltpu.VMEM(mats.shape, F32),
-            pltpu.VMEM(srcs.shape, F32),
-            pltpu.SemaphoreType.DMA((count,)),
-            pltpu.SemaphoreType.DMA,
-        ],
-        compiler_params=WHOLE,
-        name="local_chain",
-    )(mats, srcs)
-    return outs[0], list(outs[1:])
-
-
-def composite_kernel(mats_ref, middle_ref, high_ref, low_ref):
+    return list(
+        pl.pallas_call(
+            first_kernel,
+            out_shape=(leaving,) * pieces,
+            in_specs=[HBM, HBM],
+            out_specs=(VMEM,) * pieces,
+            scratch_shapes=[
+                pltpu.VMEM(mats.shape, F32),
+                pltpu.VMEM(srcs.shape, F32),
+                pltpu.SemaphoreType.DMA((count,)),
+                pltpu.SemaphoreType.DMA,
+            ],
+            compiler_params=WHOLE,
+            name="first_chain",
+        )(mats, srcs)
+    )
+
+
+def composite_kernel(mats_ref, srcs_ref, middle_ref, local_ref, high_ref, low_ref, *offset_refs):
     full = mats_ref[0]
-    count = mats_ref.shape[0]
+    count, orbs = mats_ref.shape[0], mats_ref.shape[1]
+    state = srcs_ref[:orbs, :]
     for k in range(1, count):
         left_high, left_low = split(mats_ref[k])
+        state = product(left_high, left_low, state) + srcs_ref[k * orbs : (k + 1) * orbs, :]
         high, low = split(full)
         full = dot(left_high, high) + (dot(left_high, low) + dot(left_low, high))
         if k < count - 1:
             middle_ref[k - 1] = full
+            local_ref[k - 1] = state
+    store_pieces(offset_refs, state)
     high_ref[...], low_ref[...] = split(full.T)
 
 
-def composites(mats):
+def composites(mats, srcs, pieces):
     count, orbs, _ = mats.shape
+    width = srcs.shape[1]
     shape = jax.ShapeDtypeStruct((orbs, orbs), BF16)
-    return pl.pallas_call(
+    outs = pl.pallas_call(
         composite_kernel,
-        out_shape=(jax.ShapeDtypeStruct((count - 2, orbs, orbs), F32), shape, shape),
-        in_specs=[VMEM],
-        out_specs=(VMEM,) * 3,
+        out_shape=(
+            jax.ShapeDtypeStruct((count - 2, orbs, orbs), F32),
+            jax.ShapeDtypeStruct((count - 2, orbs, width), F32),
+            shape,
+            shape,
+        )
+        + (jax.ShapeDtypeStruct((width // pieces, orbs), F32),) * pieces,
+        in_specs=[VMEM, VMEM],
+        out_specs=(VMEM,) * (4 + pieces),
         compiler_params=PARAMS,
         cost_estimate=pl.CostEstimate(
             flops=6 * (count - 1) * orbs**3, bytes_accessed=8 * count * orbs**2, transcendentals=0
         ),
         name="composites",
-    )(mats)
+    )(mats, srcs)
+    return outs[0], outs[1], outs[2:4], list(outs[4:])
 
 
 def turned_kernel(
@@ -253,7 +280,7 @@
     orbs = coupling_ref.shape[0]
     count = inner_ref.shape[1] // orbs
     here = lax.axis_index("cuts")
-    after = jnp.where(lax.rem(here, 2) == 0, after_refs[0][1:2, :], after_refs[1][1:2, :])
+    after = jnp.where(lax.rem(here, 2) == 1, after_refs[0][1:2, :], after_refs[1][1:2, :])
     rows = [mixed_ref[k : k + 1, :] for k in range(count + 1)]
     rows.append(jnp.where(here == lax.axis_size("cuts") - 1, 0.0, after))
     coupling = coupling_ref[...]
@@ -289,23 +316,32 @@
     )(coupling, inner, green, mixed, *after)
 
 
-def paired(lower, cuts, group):
+def paired(lower, cuts, group, other=0):
     pairs = []
     for c in range(cuts):
         for g in range(group):
             if c in lower:
-                to = (c + 1, g)
+                to = (c + 1, g ^ other)
             elif c - 1 in lower:
-                to = (c - 1, g)
+                to = (c - 1, g ^ other)
             else:
                 to = (c, g ^ 1 if g ^ 1 < group else g)
             pairs.append((c * group + g, to[0] * group + to[1]))
     return pairs
 
 
-def turned_round(value, axis, offset):
-    devices = lax.axis_size(axis)
-    return lax.ppermute(value, axis, [(i, (i + offset) % devices) for i in range(devices)])
+def one_way(lower, cuts, group):
+    return [(lower * group + g, (lower + 1) * group + g) for g in range(group)]
+
+
+def across(value, energy, group):
+    points, members = lax.axis_size("energy"), lax.axis_size("group")
+    pairs = [
+        (e * members + g, (e + energy) % points * members + (g ^ group))
+        for e in range(points)
+        for g in range(members)
+    ]
+    return lax.ppermute(value, ("energy", "group"), pairs)
 
 
 def body(transfer, source, coupling, strength, mode_shift):
@@ -313,23 +349,25 @@
     width = srcs.shape[1]
     cuts, group, points = (lax.axis_size(a) for a in ("cuts", "group", "energy"))
     pieces = PIECES if width % (8 * PIECES) == 0 else 1
-    local, offsets = local_chain(mats, srcs, pieces)
-    middle, *last = composites(mats)
-    leaving, incoming, blocks = offsets, [None] * pieces, None
+    leaving = first_chain(mats, srcs, pieces)
+    middle, local, last, offsets = composites(mats, srcs, pieces)
+    incoming = [None] * pieces
     for step in range(1, cuts):
-        pairs = paired([step - 1], cuts, group)
+        if step < cuts - 1:
+            pairs = paired([step - 1], cuts, group)
+        else:
+            pairs = one_way(step - 1, cuts, group)
         got = [lax.ppermute(piece, ("cuts", "group"), pairs) for piece in leaving]
         if step < cuts - 1:
-            leaving, after = [], last[0] if blocks is None else weights
+            leaving, after = [], last[0]
             for piece in range(pieces):
                 after, incoming[piece] = relay(
                     step, last, offsets[piece], got[piece], incoming[piece], after
                 )
                 leaving.append(after)
-        if blocks is None:
-            *blocks, weights = turned_blocks(
-                mats, srcs, middle, local, strength, mode_shift, leaving[-1], points, 1.0 / (width * group)
-            )
+    *blocks, weights = turned_blocks(
+        mats, srcs, middle, local, strength, mode_shift, leaving[-1], points, 1.0 / (width * group)
+    )
     green, sums = [], None
     for piece in range(pieces):
         part, sums = green_piece(
@@ -337,15 +375,17 @@
         )
         green.append(part)
 
-    parts = [turned_round(sums, "group", k) for k in range(1, group)]
-    total = sums + sum(parts)
+    sums = sums + sum(across(sums, 0, k) for k in range(1, group))
+    other = 1 if group % 2 == 0 else 0
+    mixed = sums * weights[:1]
+    for offset in range(1, points):
+        mixed = mixed + across(sums, offset, other) * weights[offset : offset + 1]
     inner, kept = inner_blocks(coupling, green)
-    mixed = total * weights[:1]
-    for k in range(1, points):
-        mixed = mixed + turned_round(total, "energy", k) * weights[k : k + 1]
     after = [
-        lax.ppermute(mixed, ("cuts", "group"), paired(range(first, cuts - 1, 2), cuts, group))
-        for first in (0, 1)
+        lax.ppermute(
+            mixed, ("cuts", "group"), paired(range(first, cuts - 1, 2), cuts, group, other)
+        )
+        for first in (1, 0)
     ]
     scattered, kept = scatter_blocks(coupling, inner, kept, mixed, after)
     return kept[None], scattered[None]

time: 36.5 us -> 35.4 us (0.970)
  the two profiles are of different devices: /device:TPU:16 before, /device:TPU:0 now
where the time goes in v3:
time: 35.4 us; the launch traced here: 35.2 us
  starting transfers between devices  13.6 us (38%)
  Pallas kernels  10.9 us (31%)
  waiting for transfers between devices  9.85 us (28%)
  between operations  0.81 us (2%)
    ppermute x2, starting transfers between devices, body(): lax.ppermute(mixed, ('cuts', 'group'), paired(range(first, cuts - 1, 2),...  6.24 us
    ppermute x4, waiting for transfers between devices, across(): return lax.ppermute(value, ('energy', 'group'), pairs)  4.92 us
    ppermute x6, waiting for transfers between devices, body(): got = [lax.ppermute(piece, ('cuts', 'group'), pairs) for piece in leaving]  3.96 us
    ppermute x4, starting transfers between devices, across(): return lax.ppermute(value, ('energy', 'group'), pairs)  3.79 us
    ppermute x6, starting transfers between devices, body(): got = [lax.ppermute(piece, ('cuts', 'group'), pairs) for piece in leaving]  3.57 us
    pallas_call x1, Pallas kernels, first_chain(): pl.pallas_call(first_kernel, out_shape=(leaving,) * pieces, in_specs=[HBM...  2.63 us
    pallas_call x1, Pallas kernels, composites(): pl.pallas_call(composite_kernel, out_shape=(jax.ShapeDtypeStruct((count -...  2.62 us
    pallas_call x1, Pallas kernels, scatter_blocks(): pl.pallas_call(scatter_kernel, out_shape=(shape, shape), in_specs=[VMEM]...  1.4 us
  transfers between devices with their start and end apart: 12, of which 7 were waited for; matrix products, arithmetic and copies ran while one was open for 0% of the time, Pallas kernels for 18%

profile of v3, /device:TPU:0, one launch (start us, length us, event | category | flops | bytes accessed | tf_op | source)
XLA Modules:
  0.0 35.2 jit_solution(5398634721738590116)
XLA Ops:
  0.6 2.6 %first_chain.1 = (f32[64,512]{1,0:T(8,128)S(1)}, f32[64,512]{1,0:T(8,128)S(1)}) custom-call(f32[3,512,512]{2,1,0:T(8,128)} %bitcast.6, f32[1536,128]{1,0:T(8,128)} %bitcast.9), custom_call_target="tpu_custom_call" | custom-call | tf_op jit(solution)/shard_map/first_chain/pallas_call | solution.py:90
  3.3 0.5 %collective-permute-start.1 = (f32[64,512]{1,0:T(8,128)S(1)}, f32[64,512]{1,0:T(8,128)S(1)}, u32[]{:S(2)}, u32[]{:S(2)}) collective-permute-start(f32[64,512]{1,0:T(8,128)S(1)} %get-tuple-element.37), channel_id=1, source_target_pairs={{0,8},{1,9},{2,10},{3,11},{8,0},{9,1},{10,2},{11,3},{16,17},{17,16... | collective-permute-start | bytes 393224 | tf_op jit(solution)/shard_map/ppermute | solution.py:360
  3.8 1.6 %collective-permute-start = (f32[64,512]{1,0:T(8,128)S(1)}, f32[64,512]{1,0:T(8,128)S(1)}, u32[]{:S(2)}, u32[]{:S(2)}) collective-permute-start(f32[64,512]{1,0:T(8,128)S(1)} %get-tuple-element.35), channel_id=1, source_target_pairs={{0,8},{1,9},{2,10},{3,11},{8,0},{9,1},{10,2},{11,3},{16,17},{17,16... | collective-permute-start | bytes 393224 | tf_op jit(solution)/shard_map/ppermute | solution.py:360
  5.4 2.6 %composites.1 = (f32[1,512,512]{2,1,0:T(8,128)S(1)}, f32[1,512,128]{2,1,0:T(8,128)S(1)}, bf16[512,512]{1,0:T(8,128)(2,1)S(1)}, bf16[512,512]{1,0:T(8,128)(2,1)S(...) custom-call(f32[3,512,512]{2,1,0:T(8,128)S(1)} %bitcast.7, f32[1536,128]{1,0:T(8,128)S(1)} %bitcast.10), custom_call_target="tpu_custom_call" | custom-call | flops 1610612736 | bytes 6291456 | tf_op jit(solution)/shard_map/composites/pallas_call | solution.py:127
  8.0 1.6 %collective-permute-done.1.got_ref = f32[64,512]{1,0:T(8,128)S(1)} collective-permute-done((f32[64,512]{1,0:T(8,128)S(1)}, f32[64,512]{1,0:T(8,128)S(1)}, u32[]{:S(2)}, u32[]{:S(2)}) %collective-permute-start.1) | collective-permute-done | bytes 131104 | tf_op jit(solution)/shard_map/ppermute | solution.py:360
  10.0 2.0 %collective-permute-done.got_ref = f32[64,512]{1,0:T(8,128)S(1)} collective-permute-done((f32[64,512]{1,0:T(8,128)S(1)}, f32[64,512]{1,0:T(8,128)S(1)}, u32[]{:S(2)}, u32[]{:S(2)}) %collective-permute-start) | collective-permute-done | bytes 131104 | tf_op jit(solution)/shard_map/ppermute | solution.py:360
  12.0 0.3 relay.5
  12.4 0.3 relay.6
  12.7 0.7 %collective-permute-start.4 = (f32[64,512]{1,0:T(8,128)S(1)}, f32[64,512]{1,0:T(8,128)S(1)}, u32[]{:S(2)}, u32[]{:S(2)}) collective-permute-start(f32[64,512]{1,0:T(8,128)S(1)} %get-tuple-element.41._), channel_id=1, source_target_pairs={{16,24},{17,25},{18,26},{19,27},{20,28},{21,29},{22,30},{23,31}} | collective-permute-start | bytes 393224 | tf_op jit(solution)/shard_map/ppermute | solution.py:360
  13.4 0.3 collective-permute-done.2.got_ref
  13.7 0.3 relay.7
  14.0 0.7 %collective-permute-start.5 = (f32[64,512]{1,0:T(8,128)S(1)}, f32[64,512]{1,0:T(8,128)S(1)}, u32[]{:S(2)}, u32[]{:S(2)}) collective-permute-start(f32[64,512]{1,0:T(8,128)S(1)} %get-tuple-element.43._), channel_id=1, source_target_pairs={{16,24},{17,25},{18,26},{19,27},{20,28},{21,29},{22,30},{23,31}} | collective-permute-start | bytes 393224 | tf_op jit(solution)/shard_map/ppermute | solution.py:360
  14.7 1.4 %turned_blocks.1 = (bf16[512,1024]{1,0:T(8,128)(2,1)S(1)}, bf16[512,1024]{1,0:T(8,128)(2,1)S(1)}, f32[128,1024]{1,0:T(8,128)S(1)}, f32[2,512]{1,0:T(2,128)S(1)}) custom-call(f32[3,512,512]{2,1,0:T(8,128)S(1)} %bitcast.8, f32[1536,128]{1,0:T(8,128)S(1)} %bitcast.11, f32[1,512,512]{2,1,0:T(8,128)S(1)} %get-tuple-element.30.mats_ref, ...), custom_call_target="tpu_custom_call" | custom-call | tf_op jit(solution)/shard_map/turned_blocks/pallas_call | solution.py:171
  16.1 0.7 %green_piece.2 = (f32[64,1536]{1,0:T(8,128)S(1)}, f32[4,512]{1,0:T(4,128)S(1)}) custom-call(bf16[512,1024]{1,0:T(8,128)(2,1)S(1)} %get-tuple-element.44.high_ref, bf16[512,1024]{1,0:T(8,128)(2,1)S(1)} %get-tuple-element.45.low_ref, f32[128,1024]{1,0:T(8,128)S(1)} %get-tuple-element.46.turned_ref, ...), custom_call_target="tpu_custom_call" | custom-call | tf_op jit(solution)/shard_map/green_piece/pallas_call | solution.py:232
  16.8 0.7 %green_piece.3 = (f32[64,1536]{1,0:T(8,128)S(1)}, f32[4,512]{1,0:T(4,128)S(1)}) custom-call(bf16[512,1024]{1,0:T(8,128)(2,1)S(1)} %get-tuple-element.44.high_ref, bf16[512,1024]{1,0:T(8,128)(2,1)S(1)} %get-tuple-element.45.low_ref, f32[128,1024]{1,0:T(8,128)S(1)} %get-tuple-element.46.turned_ref, ...), custom_call_target="tpu_custom_call" | custom-call | tf_op jit(solution)/shard_map/green_piece/pallas_call | solution.py:232
  17.7 2.3 %collective-permute-start.7 = (f32[4,512]{1,0:T(4,128)S(1)}, f32[4,512]{1,0:T(4,128)S(1)}, u32[]{:S(2)}, u32[]{:S(2)}) collective-permute-start(f32[4,512]{1,0:T(4,128)S(1)} %get-tuple-element.54), channel_id=1, source_target_pairs={{0,2},{1,3},{2,0},{3,1},{4,6},{5,7},{6,4},{7,5},{8,10},{9,11},{10,... | collective-permute-start | bytes 24584 | tf_op jit(solution)/shard_map/ppermute | solution.py:344
  20.0 1.6 %collective-permute-done.7 = f32[4,512]{1,0:T(4,128)S(1)} collective-permute-done((f32[4,512]{1,0:T(4,128)S(1)}, f32[4,512]{1,0:T(4,128)S(1)}, u32[]{:S(2)}, u32[]{:S(2)}) %collective-permute-start.7) | collective-permute-done | bytes 8224 | tf_op jit(solution)/shard_map/ppermute | solution.py:344
  21.6 1.5 %collective-permute-done.8 = f32[4,512]{1,0:T(4,128)S(1)} collective-permute-done((f32[4,512]{1,0:T(4,128)S(1)}, f32[4,512]{1,0:T(4,128)S(1)}, u32[]{:S(2)}, u32[]{:S(2)}) %collective-permute-start.8) | collective-permute-done | bytes 8224 | tf_op jit(solution)/shard_map/ppermute | solution.py:344
  23.1 1.2 %collective-permute-start.9 = (f32[4,512]{1,0:T(4,128)S(1)}, f32[4,512]{1,0:T(4,128)S(1)}, u32[]{:S(2)}, u32[]{:S(2)}) collective-permute-start(f32[4,512]{1,0:T(4,128)S(1)} %add_add_fusion), channel_id=1, source_target_pairs={{0,5},{1,4},{2,7},{3,6},{4,1},{5,0},{6,3},{7,2},{8,13},{9,12},{10,... | collective-permute-start | bytes 24584 | tf_op jit(solution)/shard_map/ppermute | solution.py:344
  24.3 1.8 %collective-permute-done.9 = f32[4,512]{1,0:T(4,128)S(1)} collective-permute-done((f32[4,512]{1,0:T(4,128)S(1)}, f32[4,512]{1,0:T(4,128)S(1)}, u32[]{:S(2)}, u32[]{:S(2)}) %collective-permute-start.9) | collective-permute-done | bytes 8224 | tf_op jit(solution)/shard_map/ppermute | solution.py:344
  26.3 6.1 %collective-permute-start.11 = (f32[4,512]{1,0:T(4,128)S(1)}, f32[4,512]{1,0:T(4,128)S(1)}, u32[]{:S(2)}, u32[]{:S(2)}) collective-permute-start(f32[4,512]{1,0:T(4,128)S(1)} %multiply_add_fusion.rest_0_), channel_id=1, source_target_pairs={{0,9},{1,8},{2,11},{3,10},{8,1},{9,0},{10,3},{11,2},{16,25},{17,24... | collective-permute-start | bytes 24584 | tf_op jit(solution)/shard_map/ppermute | solution.py:385
  32.4 0.4 %inner_blocks.1 = (f32[128,1536]{1,0:T(8,128)S(1)}, f32[1536,128]{1,0:T(8,128)S(1)}) custom-call(bf16[512,512]{1,0:T(8,128)(2,1)S(1)} %copy-done.2, f32[64,1536]{1,0:T(8,128)S(1)} %get-tuple-element.48.rest_0_, f32[64,1536]{1,0:T(8,128)S(1)} %get-tuple-element.51.rest_1_), custom_call_target="tpu_custom_call" | custom-call | flops 201326592 | bytes 2359296 | tf_op jit(solution)/shard_map/inner_blocks/pallas_call | solution.py:260
  32.8 1.0 %collective-permute-done.11.rest_2_ = f32[4,512]{1,0:T(4,128)S(1)} collective-permute-done((f32[4,512]{1,0:T(4,128)S(1)}, f32[4,512]{1,0:T(4,128)S(1)}, u32[]{:S(2)}, u32[]{:S(2)}) %collective-permute-start.11) | collective-permute-done | bytes 8224 | tf_op jit(solution)/shard_map/ppermute | solution.py:385
  33.8 1.4 %scatter_blocks.1 = (f32[1536,128]{1,0:T(8,128)}, f32[1536,128]{1,0:T(8,128)}) custom-call(bf16[512,512]{1,0:T(8,128)(2,1)S(1)} %copy-done.2, f32[128,1536]{1,0:T(8,128)S(1)} %get-tuple-element.52.inner_ref, f32[1536,128]{1,0:T(8,128)S(1)} %get-tuple-element.53.green_ref, f32[4,512]{1,0:T(4,128)S(1)} %multiply_add_fusion.rest_0_, ...), custom_call_target="tpu_custom_call" | custom-call | tf_op jit(solution)/shard_map/scatter_blocks/pallas_call | solution.py:304
  (24 shorter events, 0.8 us)
Async XLA Ops:
  0.6 4.7 %copy-start = (f32[1,3,512,512]{3,2,1,0:T(8,128)S(1)}, f32[1,3,512,512]{3,2,1,0:T(8,128)}, u32[]{:S(2)}) copy-start(f32[1,3,512,512]{3,2,1,0:T(8,128)} %param.5) | copy-start | bytes 9437188
  0.6 4.7 %copy-start.1 = (f32[1,1536,128]{2,1,0:T(8,128)S(1)}, f32[1,1536,128]{2,1,0:T(8,128)}, u32[]{:S(2)}) copy-start(f32[1,1536,128]{2,1,0:T(8,128)} %param.6) | copy-start | bytes 2359300
  3.3 6.4 %collective-permute-start.1 = (f32[64,512]{1,0:T(8,128)S(1)}, f32[64,512]{1,0:T(8,128)S(1)}, u32[]{:S(2)}, u32[]{:S(2)}) collective-permute-start(f32[64,512]{1,0:T(8,128)S(1)} %get-tuple-element.37), channel_id=1, source_target_pairs={{0,8},{1,9},{2,10},{3,11},{8,0},{9,1},{10,2},{11,3},{16,17},{17,16... | collective-permute-start | bytes 393224 | tf_op jit(solution)/shard_map/ppermute | solution.py:360
  3.8 8.2 %collective-permute-start = (f32[64,512]{1,0:T(8,128)S(1)}, f32[64,512]{1,0:T(8,128)S(1)}, u32[]{:S(2)}, u32[]{:S(2)}) collective-permute-start(f32[64,512]{1,0:T(8,128)S(1)} %get-tuple-element.35), channel_id=1, source_target_pairs={{0,8},{1,9},{2,10},{3,11},{8,0},{9,1},{10,2},{11,3},{16,17},{17,16... | collective-permute-start | bytes 393224 | tf_op jit(solution)/shard_map/ppermute | solution.py:360
  9.6 5.1 %copy-start.3 = (f32[8]{0:T(128)S(1)}, f32[8]{0:T(128)}, u32[]{:S(2)}) copy-start(f32[8]{0:T(128)} %strength_ref.1) | copy-start | bytes 100
  9.6 5.1 %copy-start.4 = (s32[8]{0:T(128)S(1)}, s32[8]{0:T(128)}, u32[]{:S(2)}) copy-start(s32[8]{0:T(128)} %shift_ref.1) | copy-start | bytes 100
  9.9 2.4 %collective-permute-start.3 = (f32[64,512]{1,0:T(8,128)S(1)}, f32[64,512]{1,0:T(8,128)S(1)}, u32[]{:S(2)}, u32[]{:S(2)}) collective-permute-start(f32[64,512]{1,0:T(8,128)S(1)} %get-tuple-element.38._), channel_id=1, source_target_pairs={{0,1},{1,0},{2,3},{3,2},{8,16},{9,17},{10,18},{11,19},{16,8},{17,9... | collective-permute-start | bytes 393224 | tf_op jit(solution)/shard_map/ppermute | solution.py:360
  12.3 1.4 %collective-permute-start.2 = (f32[64,512]{1,0:T(8,128)S(1)}, f32[64,512]{1,0:T(8,128)S(1)}, u32[]{:S(2)}, u32[]{:S(2)}) collective-permute-start(f32[64,512]{1,0:T(8,128)S(1)} %get-tuple-element.39), channel_id=1, source_target_pairs={{0,1},{1,0},{2,3},{3,2},{8,16},{9,17},{10,18},{11,19},{16,8},{17,9... | collective-permute-start | bytes 393224 | tf_op jit(solution)/shard_map/ppermute | solution.py:360
  12.7 3.4 %collective-permute-start.4 = (f32[64,512]{1,0:T(8,128)S(1)}, f32[64,512]{1,0:T(8,128)S(1)}, u32[]{:S(2)}, u32[]{:S(2)}) collective-permute-start(f32[64,512]{1,0:T(8,128)S(1)} %get-tuple-element.41._), channel_id=1, source_target_pairs={{16,24},{17,25},{18,26},{19,27},{20,28},{21,29},{22,30},{23,31}} | collective-permute-start | bytes 393224 | tf_op jit(solution)/shard_map/ppermute | solution.py:360
  14.0 2.7 %collective-permute-start.5 = (f32[64,512]{1,0:T(8,128)S(1)}, f32[64,512]{1,0:T(8,128)S(1)}, u32[]{:S(2)}, u32[]{:S(2)}) collective-permute-start(f32[64,512]{1,0:T(8,128)S(1)} %get-tuple-element.43._), channel_id=1, source_target_pairs={{16,24},{17,25},{18,26},{19,27},{20,28},{21,29},{22,30},{23,31}} | collective-permute-start | bytes 393224 | tf_op jit(solution)/shard_map/ppermute | solution.py:360
  16.1 16.4 %copy-start.2 = (bf16[512,512]{1,0:T(8,128)(2,1)S(1)}, bf16[512,512]{1,0:T(8,128)(2,1)}, u32[]{:S(2)}) copy-start(bf16[512,512]{1,0:T(8,128)(2,1)} %coupling_ref.3) | copy-start | bytes 1572868
  17.5 2.6 %collective-permute-start.6 = (f32[4,512]{1,0:T(4,128)S(1)}, f32[4,512]{1,0:T(4,128)S(1)}, u32[]{:S(2)}, u32[]{:S(2)}) collective-permute-start(f32[4,512]{1,0:T(4,128)S(1)} %get-tuple-element.54), channel_id=1, source_target_pairs={{0,1},{1,0},{2,3},{3,2},{4,5},{5,4},{6,7},{7,6},{8,9},{9,8},{10,11... | collective-permute-start | bytes 24584 | tf_op jit(solution)/shard_map/ppermute | solution.py:344
  17.7 4.0 %collective-permute-start.7 = (f32[4,512]{1,0:T(4,128)S(1)}, f32[4,512]{1,0:T(4,128)S(1)}, u32[]{:S(2)}, u32[]{:S(2)}) collective-permute-start(f32[4,512]{1,0:T(4,128)S(1)} %get-tuple-element.54), channel_id=1, source_target_pairs={{0,2},{1,3},{2,0},{3,1},{4,6},{5,7},{6,4},{7,5},{8,10},{9,11},{10,... | collective-permute-start | bytes 24584 | tf_op jit(solution)/shard_map/ppermute | solution.py:344
  20.0 3.1 %collective-permute-start.8 = (f32[4,512]{1,0:T(4,128)S(1)}, f32[4,512]{1,0:T(4,128)S(1)}, u32[]{:S(2)}, u32[]{:S(2)}) collective-permute-start(f32[4,512]{1,0:T(4,128)S(1)} %get-tuple-element.54), channel_id=1, source_target_pairs={{0,3},{1,2},{2,1},{3,0},{4,7},{5,6},{6,5},{7,4},{8,11},{9,10},{10,... | collective-permute-start | bytes 24584 | tf_op jit(solution)/shard_map/ppermute | solution.py:344
  23.1 3.1 %collective-permute-start.9 = (f32[4,512]{1,0:T(4,128)S(1)}, f32[4,512]{1,0:T(4,128)S(1)}, u32[]{:S(2)}, u32[]{:S(2)}) collective-permute-start(f32[4,512]{1,0:T(4,128)S(1)} %add_add_fusion), channel_id=1, source_target_pairs={{0,5},{1,4},{2,7},{3,6},{4,1},{5,0},{6,3},{7,2},{8,13},{9,12},{10,... | collective-permute-start | bytes 24584 | tf_op jit(solution)/shard_map/ppermute | solution.py:344
  26.2 6.6 %collective-permute-start.10 = (f32[4,512]{1,0:T(4,128)S(1)}, f32[4,512]{1,0:T(4,128)S(1)}, u32[]{:S(2)}, u32[]{:S(2)}) collective-permute-start(f32[4,512]{1,0:T(4,128)S(1)} %multiply_add_fusion.rest_0_), channel_id=1, source_target_pairs={{0,1},{1,0},{2,3},{3,2},{8,17},{9,16},{10,19},{11,18},{16,9},{17,8... | collective-permute-start | bytes 24584 | tf_op jit(solution)/shard_map/ppermute | solution.py:385
  26.3 7.5 %collective-permute-start.11 = (f32[4,512]{1,0:T(4,128)S(1)}, f32[4,512]{1,0:T(4,128)S(1)}, u32[]{:S(2)}, u32[]{:S(2)}) collective-permute-start(f32[4,512]{1,0:T(4,128)S(1)} %multiply_add_fusion.rest_0_), channel_id=1, source_target_pairs={{0,9},{1,8},{2,11},{3,10},{8,1},{9,0},{10,3},{11,2},{16,25},{17,24... | collective-permute-start | bytes 24584 | tf_op jit(solution)/shard_map/ppermute | solution.py:385

commit v4 on v3

--- a/solution.py
+++ b/solution.py
@@ -13,8 +13,8 @@
 SMEM = pl.BlockSpec(memory_space=pltpu.SMEM)
 HBM = pl.BlockSpec(memory_space=pltpu.HBM)
 PARAMS = pltpu.CompilerParams(vmem_limit_bytes=32 * 1024 * 1024)
-WHOLE = pltpu.CompilerParams(vmem_limit_bytes=53 * 1024 * 1024)
-PIECES = 2
+WHOLE = pltpu.CompilerParams(vmem_limit_bytes=107 * 512 * 1024)
+SHARES = (9, 7)
 
 
 def split(value):
@@ -48,11 +48,19 @@
     return product(*split(matrix), state) + srcs
 
 
+def heights_of(width):
+    if width % 8 or width // 8 < sum(SHARES):
+        return (width,)
+    ends = [8 * (width // 8 * sum(SHARES[: k + 1]) // sum(SHARES)) for k in range(len(SHARES))]
+    return tuple(end - start for start, end in zip([0, *ends], ends))
+
+
 def store_pieces(refs, state):
     turned = state.T
-    height = turned.shape[0] // len(refs)
-    for piece, ref in enumerate(refs):
-        ref[...] = turned[piece * height : (piece + 1) * height, :]
+    start = 0
+    for ref in refs:
+        ref[...] = turned[start : start + ref.shape[0], :]
+        start += ref.shape[0]
 
 
 def first_kernel(mats_ref, srcs_ref, *rest):
@@ -82,16 +90,14 @@
             ref[...] = jnp.zeros_like(ref)
 
 
-def first_chain(mats, srcs, pieces):
+def first_chain(mats, srcs, heights):
     count, orbs, _ = mats.shape
-    width = srcs.shape[1]
-    leaving = jax.ShapeDtypeStruct((width // pieces, orbs), F32)
     return list(
         pl.pallas_call(
             first_kernel,
-            out_shape=(leaving,) * pieces,
+            out_shape=tuple(jax.ShapeDtypeStruct((height, orbs), F32) for height in heights),
             in_specs=[HBM, HBM],
-            out_specs=(VMEM,) * pieces,
+            out_specs=(VMEM,) * len(heights),
             scratch_shapes=[
                 pltpu.VMEM(mats.shape, F32),
                 pltpu.VMEM(srcs.shape, F32),
@@ -120,7 +126,7 @@
     high_ref[...], low_ref[...] = split(full.T)
 
 
-def composites(mats, srcs, pieces):
+def composites(mats, srcs, heights):
     count, orbs, _ = mats.shape
     width = srcs.shape[1]
     shape = jax.ShapeDtypeStruct((orbs, orbs), BF16)
@@ -132,9 +138,9 @@
             shape,
             shape,
         )
-        + (jax.ShapeDtypeStruct((width // pieces, orbs), F32),) * pieces,
+        + tuple(jax.ShapeDtypeStruct((height, orbs), F32) for height in heights),
         in_specs=[VMEM, VMEM],
-        out_specs=(VMEM,) * (4 + pieces),
+        out_specs=(VMEM,) * (4 + len(heights)),
         compiler_params=PARAMS,
         cost_estimate=pl.CostEstimate(
             flops=6 * (count - 1) * orbs**3, bytes_accessed=8 * count * orbs**2, transcendentals=0
@@ -205,12 +211,12 @@
 
 
 def green_kernel(
-    step, piece, high_ref, low_ref, turned_ref, last_high_ref, last_low_ref, offset_ref, got_ref, incoming_ref, *rest
+    step, start, high_ref, low_ref, turned_ref, last_high_ref, last_low_ref, offset_ref, got_ref, incoming_ref, *rest
 ):
     green_ref, sums_ref = rest[-2:]
     height, orbs = got_ref.shape
     length = high_ref.shape[1]
-    rows = slice(piece * height, (piece + 1) * height)
+    rows = slice(start, start + height)
     state = jnp.where(lax.axis_index("cuts") == step, got_ref[...], incoming_ref[...])
     sums = [jnp.sum(state * state, axis=0, keepdims=True)]
     green = product_rows(state, high_ref[...], low_ref[...]) + turned_ref[rows, :]
@@ -225,12 +231,12 @@
     sums_ref[...] = total if len(rest) == 2 else total + rest[0][...]
 
 
-def green_piece(step, piece, blocks, last, offset, got, incoming, sums):
+def green_piece(step, start, blocks, last, offset, got, incoming, sums):
     height, orbs = got.shape
     count = blocks[0].shape[1] // orbs + 1
     args = [*blocks, *last, offset, got, incoming] + ([] if sums is None else [sums])
     return pl.pallas_call(
-        functools.partial(green_kernel, step, piece),
+        functools.partial(green_kernel, step, start),
         out_shape=(
             jax.ShapeDtypeStruct((height, count * orbs), F32),
             jax.ShapeDtypeStruct((count + 1, orbs), F32),
@@ -255,8 +261,8 @@
 
 
 def inner_blocks(coupling, pieces):
-    height, length = pieces[0].shape
-    width = height * len(pieces)
+    length = pieces[0].shape[1]
+    width = sum(piece.shape[0] for piece in pieces)
     return pl.pallas_call(
         inner_kernel,
         out_shape=(
@@ -273,22 +279,21 @@
     )(coupling, *pieces)
 
 
-def scatter_kernel(coupling_ref, inner_ref, green_ref, *rest):
-    mixed_ref, *after_refs, out_ref, kept_ref, staged, sems, kept_sem = rest
+def smoothed(rows, k):
+    return rows[k + 1] + 0.5 * (rows[k] + rows[k + 2])
+
+
+def scatter_kernel(coupling_ref, inner_ref, green_ref, mixed_ref, out_ref, kept_ref, staged, sems, kept_sem):
     kept_copy = pltpu.make_async_copy(green_ref, kept_ref, kept_sem)
     kept_copy.start()
     orbs = coupling_ref.shape[0]
     count = inner_ref.shape[1] // orbs
-    here = lax.axis_index("cuts")
-    after = jnp.where(lax.rem(here, 2) == 1, after_refs[0][1:2, :], after_refs[1][1:2, :])
     rows = [mixed_ref[k : k + 1, :] for k in range(count + 1)]
-    rows.append(jnp.where(here == lax.axis_size("cuts") - 1, 0.0, after))
     coupling = coupling_ref[...]
     copies = []
-    for k in range(count):
-        selfen = rows[k + 1] + 0.5 * (rows[k] + rows[k + 2])
+    for k in range(count - 1):
         columns = slice(k * orbs, (k + 1) * orbs)
-        scaled = (inner_ref[:, columns] * selfen).astype(BF16)
+        scaled = (inner_ref[:, columns] * smoothed(rows, k)).astype(BF16)
         staged[columns, :] = dot_t(coupling, scaled)
         copies.append(pltpu.make_async_copy(staged.at[columns], out_ref.at[columns], sems.at[k]))
         copies[-1].start()
@@ -297,23 +302,73 @@
     kept_copy.wait()
 
 
-def scatter_blocks(coupling, inner, green, mixed, after):
+def scatter_blocks(coupling, inner, green, mixed):
     width, length = inner.shape
     orbs = coupling.shape[0]
     shape = jax.ShapeDtypeStruct((length, width), F32)
     return pl.pallas_call(
         scatter_kernel,
         out_shape=(shape, shape),
-        in_specs=[VMEM] * (4 + len(after)),
+        in_specs=[VMEM] * 4,
         out_specs=(HBM, HBM),
         scratch_shapes=[
-            pltpu.VMEM((length, width), F32),
-            pltpu.SemaphoreType.DMA((length // orbs,)),
+            pltpu.VMEM((length - orbs, width), F32),
+            pltpu.SemaphoreType.DMA((length // orbs - 1,)),
             pltpu.SemaphoreType.DMA,
         ],
         compiler_params=PARAMS,
         name="scatter_blocks",
-    )(coupling, inner, green, mixed, *after)
+    )(coupling, inner, green, mixed)
+
+
+def last_kernel(coupling_ref, inner_ref, mixed_ref, _, *rest):
+    *after_refs, out_ref, staged, sem = rest
+    orbs = coupling_ref.shape[0]
+    count = inner_ref.shape[1] // orbs
+    here = lax.axis_index("cuts")
+    after = jnp.zeros((1, orbs), F32)
+    for lower, after_ref in enumerate(after_refs):
+        after = jnp.where(here == lower, after_ref[:1, :], after)
+    rows = [mixed_ref[k : k + 1, :] for k in range(count + 1)] + [after]
+    columns = slice((count - 1) * orbs, count * orbs)
+    scaled = (inner_ref[:, columns] * smoothed(rows, count - 1)).astype(BF16)
+    staged[...] = dot_t(coupling_ref[...], scaled)
+    copy = pltpu.make_async_copy(staged, out_ref.at[columns], sem)
+    copy.start()
+    copy.wait()
+
+
+def last_block(coupling, inner, mixed, partial, after):
+    orbs = coupling.shape[0]
+    return pl.pallas_call(
+        last_kernel,
+        out_shape=jax.ShapeDtypeStruct(partial.shape, F32),
+        in_specs=[VMEM] * 3 + [HBM] + [VMEM] * len(after),
+        out_specs=HBM,
+        scratch_shapes=[pltpu.VMEM((orbs, partial.shape[1]), F32), pltpu.SemaphoreType.DMA],
+        input_output_aliases={3: 0},
+        compiler_params=PARAMS,
+        name="last_block",
+    )(coupling, inner, mixed, partial, *after)
+
+
+def edge_kernel(mixed_ref, _, *out_refs):
+    for out_ref in out_refs:
+        out_ref[...] = jnp.broadcast_to(mixed_ref[1:2, :], out_ref.shape)
+
+
+def edge_rows(mixed, after, cuts):
+    return pl.pallas_call(
+        edge_kernel,
+        out_shape=tuple(
+            jax.ShapeDtypeStruct((4 * (cuts - 1 - lower), mixed.shape[1]), F32)
+            for lower in range(cuts - 1)
+        ),
+        in_specs=[VMEM, VMEM],
+        out_specs=(VMEM,) * (cuts - 1),
+        compiler_params=PARAMS,
+        name="edge_rows",
+    )(mixed, after)
 
 
 def paired(lower, cuts, group, other=0):
@@ -348,10 +403,11 @@
     mats, srcs = transfer[0], source[0]
     width = srcs.shape[1]
     cuts, group, points = (lax.axis_size(a) for a in ("cuts", "group", "energy"))
-    pieces = PIECES if width % (8 * PIECES) == 0 else 1
-    leaving = first_chain(mats, srcs, pieces)
-    middle, local, last, offsets = composites(mats, srcs, pieces)
-    incoming = [None] * pieces
+    heights = heights_of(width)
+    pieces = len(heights)
+    middle, local, last, offsets = composites(mats, srcs, heights)
+    leaving = first_chain(mats, srcs, heights[:1]) + offsets[1:]
+    incoming, blocks = [None] * pieces, None
     for step in range(1, cuts):
         if step < cuts - 1:
             pairs = paired([step - 1], cuts, group)
@@ -359,35 +415,40 @@
             pairs = one_way(step - 1, cuts, group)
         got = [lax.ppermute(piece, ("cuts", "group"), pairs) for piece in leaving]
         if step < cuts - 1:
-            leaving, after = [], last[0]
+            leaving, after = [], last[0] if blocks is None else weights
             for piece in range(pieces):
                 after, incoming[piece] = relay(
                     step, last, offsets[piece], got[piece], incoming[piece], after
                 )
                 leaving.append(after)
-    *blocks, weights = turned_blocks(
-        mats, srcs, middle, local, strength, mode_shift, leaving[-1], points, 1.0 / (width * group)
-    )
+        if blocks is None:
+            *blocks, weights = turned_blocks(
+                mats, srcs, middle, local, strength, mode_shift, leaving[-1], points, 1.0 / (width * group)
+            )
     green, sums = [], None
     for piece in range(pieces):
         part, sums = green_piece(
-            cuts - 1, piece, blocks, last, offsets[piece], got[piece], incoming[piece], sums
+            cuts - 1, sum(heights[:piece]), blocks, last, offsets[piece], got[piece], incoming[piece], sums
         )
         green.append(part)
 
-    sums = sums + sum(across(sums, 0, k) for k in range(1, group))
     other = 1 if group % 2 == 0 else 0
+    if other:
+        sums = sums + across(sums, 0, 1)
+    sums = sums + sum(across(sums, 0, k + other) for k in range(1 + other, group, 1 + other))
     mixed = sums * weights[:1]
     for offset in range(1, points):
         mixed = mixed + across(sums, offset, other) * weights[offset : offset + 1]
     inner, kept = inner_blocks(coupling, green)
+    edges = edge_rows(mixed, inner, cuts)
     after = [
         lax.ppermute(
-            mixed, ("cuts", "group"), paired(range(first, cuts - 1, 2), cuts, group, other)
+            edges[lower], ("cuts", "group"), paired([lower], cuts, group, other)
         )
-        for first in (1, 0)
+        for lower in range(cuts - 1)
     ]
-    scattered, kept = scatter_blocks(coupling, inner, kept, mixed, after)
+    partial, kept = scatter_blocks(coupling, inner, kept, mixed)
+    scattered = last_block(coupling, inner, mixed, partial, after)
     return kept[None], scattered[None]
 
 

time: 35.4 us -> 33.5 us (0.946)
  the two profiles are of different devices: /device:TPU:0 before, /device:TPU:17 now
where the time goes in v4:
time: 33.5 us; the launch traced here: 33.1 us
  starting transfers between devices  14.4 us (43%)
  Pallas kernels  9.27 us (28%)
  waiting for transfers between devices  7.46 us (22%)
  local copies, waits for them, and re-layouts  1.25 us (4%)
  between operations  0.79 us (2%)
    ppermute x6, starting transfers between devices, body(): got = [lax.ppermute(piece, ('cuts', 'group'), pairs) for piece in leaving]  7.27 us
    ppermute x3, starting transfers between devices, across(): return lax.ppermute(value, ('energy', 'group'), pairs)  4.08 us
    ppermute x3, waiting for transfers between devices, across(): return lax.ppermute(value, ('energy', 'group'), pairs)  3.95 us
    ppermute x6, waiting for transfers between devices, body(): got = [lax.ppermute(piece, ('cuts', 'group'), pairs) for piece in leaving]  3.43 us
    ppermute x3, starting transfers between devices, body(): lax.ppermute(edges[lower], ('cuts', 'group'), paired([lower], cuts, group...  3 us
    pallas_call x1, Pallas kernels, composites(): pl.pallas_call(composite_kernel, out_shape=(jax.ShapeDtypeStruct((count -...  2.62 us
    pallas_call x2, Pallas kernels, green_piece(): pl.pallas_call(functools.partial(green_kernel, step, start), out_shape=(j...  1.42 us
    pallas_call x1, Pallas kernels, turned_blocks(): pl.pallas_call(functools.partial(turned_kernel, points, scale), out_shape...  1.28 us
  transfers between devices with their start and end apart: 12, of which 8 were waited for; matrix products, arithmetic and copies ran while one was open for 0% of the time, Pallas kernels for 23%

profile of v4, /device:TPU:17, one launch (start us, length us, event | category | flops | bytes accessed | tf_op | source)
XLA Modules:
  0.0 33.1 jit_solution(8046205726949147471)
XLA Ops:
  0.7 0.7 %collective-permute-start.1 = (f32[72,512]{1,0:T(8,128)S(1)}, f32[72,512]{1,0:T(8,128)S(1)}, u32[]{:S(2)}, u32[]{:S(2)}) collective-permute-start(f32[72,512]{1,0:T(8,128)S(1)} %first_chain.1), channel_id=1, source_target_pairs={{0,8},{1,9},{2,10},{3,11},{8,0},{9,1},{10,2},{11,3},{16,17},{17,16... | collective-permute-start | bytes 442376 | tf_op jit(solution)/shard_map/ppermute | solution.py:416
  1.5 1.0 %copy-done = f32[1,3,512,512]{3,2,1,0:T(8,128)S(1)} copy-done((f32[1,3,512,512]{3,2,1,0:T(8,128)S(1)}, f32[1,3,512,512]{3,2,1,0:T(8,128)}, u32[]{:S(2)}) %copy-start) | copy-done | bytes 3145752
  2.7 2.6 %composites.1 = (f32[1,512,512]{2,1,0:T(8,128)S(1)}, f32[1,512,128]{2,1,0:T(8,128)S(1)}, bf16[512,512]{1,0:T(8,128)(2,1)S(1)}, bf16[512,512]{1,0:T(8,128)(2,1)S(...) custom-call(f32[3,512,512]{2,1,0:T(8,128)S(1)} %bitcast.7, f32[1536,128]{1,0:T(8,128)S(1)} %bitcast.10), custom_call_target="tpu_custom_call" | custom-call | flops 1610612736 | bytes 6291456 | tf_op jit(solution)/shard_map/composites/pallas_call | solution.py:133
  5.3 0.7 %collective-permute-start = (f32[56,512]{1,0:T(8,128)S(1)}, f32[56,512]{1,0:T(8,128)S(1)}, u32[]{:S(2)}, u32[]{:S(2)}) collective-permute-start(f32[56,512]{1,0:T(8,128)S(1)} %get-tuple-element.35.offset_ref), channel_id=1, source_target_pairs={{0,8},{1,9},{2,10},{3,11},{8,0},{9,1},{10,2},{11,3},{16,17},{17,16... | collective-permute-start | bytes 344072 | tf_op jit(solution)/shard_map/ppermute | solution.py:416
  6.4 0.6 %collective-permute-start.2 = (f32[72,512]{1,0:T(8,128)S(1)}, f32[72,512]{1,0:T(8,128)S(1)}, u32[]{:S(2)}, u32[]{:S(2)}) collective-permute-start(f32[72,512]{1,0:T(8,128)S(1)} %get-tuple-element.37._), channel_id=1, source_target_pairs={{0,1},{1,0},{2,3},{3,2},{8,16},{9,17},{10,18},{11,19},{16,8},{17,9... | collective-permute-start | bytes 442376 | tf_op jit(solution)/shard_map/ppermute | solution.py:416
  7.4 2.6 %collective-permute-start.4 = (f32[56,512]{1,0:T(8,128)S(1)}, f32[56,512]{1,0:T(8,128)S(1)}, u32[]{:S(2)}, u32[]{:S(2)}) collective-permute-start(f32[56,512]{1,0:T(8,128)S(1)} %get-tuple-element.38._), channel_id=1, source_target_pairs={{0,1},{1,0},{2,3},{3,2},{8,16},{9,17},{10,18},{11,19},{16,8},{17,9... | collective-permute-start | bytes 344072 | tf_op jit(solution)/shard_map/ppermute | solution.py:416
  10.0 1.3 %turned_blocks.1 = (bf16[512,1024]{1,0:T(8,128)(2,1)S(1)}, bf16[512,1024]{1,0:T(8,128)(2,1)S(1)}, f32[128,1024]{1,0:T(8,128)S(1)}, f32[2,512]{1,0:T(2,128)S(1)}) custom-call(f32[3,512,512]{2,1,0:T(8,128)S(1)} %bitcast.8, f32[1536,128]{1,0:T(8,128)S(1)} %bitcast.11, f32[1,512,512]{2,1,0:T(8,128)S(1)} %get-tuple-element.31.mats_ref, ...), custom_call_target="tpu_custom_call" | custom-call | tf_op jit(solution)/shard_map/turned_blocks/pallas_call | solution.py:177
  11.2 0.7 %collective-permute-done.2.got_ref = f32[72,512]{1,0:T(8,128)S(1)} collective-permute-done((f32[72,512]{1,0:T(8,128)S(1)}, f32[72,512]{1,0:T(8,128)S(1)}, u32[]{:S(2)}, u32[]{:S(2)}) %collective-permute-start.2) | collective-permute-done | bytes 147488 | tf_op jit(solution)/shard_map/ppermute | solution.py:416
  12.2 1.3 %collective-permute-start.3 = (f32[72,512]{1,0:T(8,128)S(1)}, f32[72,512]{1,0:T(8,128)S(1)}, u32[]{:S(2)}, u32[]{:S(2)}) collective-permute-start(f32[72,512]{1,0:T(8,128)S(1)} %get-tuple-element.44._), channel_id=1, source_target_pairs={{16,24},{17,25},{18,26},{19,27},{20,28},{21,29},{22,30},{23,31}} | collective-permute-start | bytes 442376 | tf_op jit(solution)/shard_map/ppermute | solution.py:416
  13.5 0.6 %collective-permute-done.4.got_ref = f32[56,512]{1,0:T(8,128)S(1)} collective-permute-done((f32[56,512]{1,0:T(8,128)S(1)}, f32[56,512]{1,0:T(8,128)S(1)}, u32[]{:S(2)}, u32[]{:S(2)}) %collective-permute-start.4) | collective-permute-done | bytes 114720 | tf_op jit(solution)/shard_map/ppermute | solution.py:416
  14.4 1.3 %collective-permute-start.5 = (f32[56,512]{1,0:T(8,128)S(1)}, f32[56,512]{1,0:T(8,128)S(1)}, u32[]{:S(2)}, u32[]{:S(2)}) collective-permute-start(f32[56,512]{1,0:T(8,128)S(1)} %get-tuple-element.48), channel_id=1, source_target_pairs={{16,24},{17,25},{18,26},{19,27},{20,28},{21,29},{22,30},{23,31}} | collective-permute-start | bytes 344072 | tf_op jit(solution)/shard_map/ppermute | solution.py:416
  15.8 0.7 %green_piece.2 = (f32[72,1536]{1,0:T(8,128)S(1)}, f32[4,512]{1,0:T(4,128)S(1)}) custom-call(bf16[512,1024]{1,0:T(8,128)(2,1)S(1)} %get-tuple-element.39.high_ref, bf16[512,1024]{1,0:T(8,128)(2,1)S(1)} %get-tuple-element.40.low_ref, f32[128,1024]{1,0:T(8,128)S(1)} %get-tuple-element.41.turned_ref, ...), custom_call_target="tpu_custom_call" | custom-call | tf_op jit(solution)/shard_map/green_piece/pallas_call | solution.py:238
  16.5 2.1 %collective-permute-done.5.got_ref = f32[56,512]{1,0:T(8,128)S(1)} collective-permute-done((f32[56,512]{1,0:T(8,128)S(1)}, f32[56,512]{1,0:T(8,128)S(1)}, u32[]{:S(2)}, u32[]{:S(2)}) %collective-permute-start.5) | collective-permute-done | bytes 114720 | tf_op jit(solution)/shard_map/ppermute | solution.py:416
  18.6 0.7 %green_piece.3 = (f32[56,1536]{1,0:T(8,128)S(1)}, f32[4,512]{1,0:T(4,128)S(1)}) custom-call(bf16[512,1024]{1,0:T(8,128)(2,1)S(1)} %get-tuple-element.39.high_ref, bf16[512,1024]{1,0:T(8,128)(2,1)S(1)} %get-tuple-element.40.low_ref, f32[128,1024]{1,0:T(8,128)S(1)} %get-tuple-element.41.turned_ref, ...), custom_call_target="tpu_custom_call" | custom-call | tf_op jit(solution)/shard_map/green_piece/pallas_call | solution.py:238
  19.3 1.5 %collective-permute-start.6 = (f32[4,512]{1,0:T(4,128)S(1)}, f32[4,512]{1,0:T(4,128)S(1)}, u32[]{:S(2)}, u32[]{:S(2)}) collective-permute-start(f32[4,512]{1,0:T(4,128)S(1)} %get-tuple-element.54), channel_id=1, source_target_pairs={{0,1},{1,0},{2,3},{3,2},{4,5},{5,4},{6,7},{7,6},{8,9},{9,8},{10,11... | collective-permute-start | bytes 24584 | tf_op jit(solution)/shard_map/ppermute | solution.py:399
  20.8 0.8 %collective-permute-done.6 = f32[4,512]{1,0:T(4,128)S(1)} collective-permute-done((f32[4,512]{1,0:T(4,128)S(1)}, f32[4,512]{1,0:T(4,128)S(1)}, u32[]{:S(2)}, u32[]{:S(2)}) %collective-permute-start.6) | collective-permute-done | bytes 8224 | tf_op jit(solution)/shard_map/ppermute | solution.py:399
  21.6 1.3 %collective-permute-start.7 = (f32[4,512]{1,0:T(4,128)S(1)}, f32[4,512]{1,0:T(4,128)S(1)}, u32[]{:S(2)}, u32[]{:S(2)}) collective-permute-start(f32[4,512]{1,0:T(4,128)S(1)} %add.9), channel_id=1, source_target_pairs={{0,3},{1,2},{2,1},{3,0},{4,7},{5,6},{6,5},{7,4},{8,11},{9,10},{10,... | collective-permute-start | bytes 24584 | tf_op jit(solution)/shard_map/ppermute | solution.py:399
  22.9 1.8 %collective-permute-done.7 = f32[4,512]{1,0:T(4,128)S(1)} collective-permute-done((f32[4,512]{1,0:T(4,128)S(1)}, f32[4,512]{1,0:T(4,128)S(1)}, u32[]{:S(2)}, u32[]{:S(2)}) %collective-permute-start.7) | collective-permute-done | bytes 8224 | tf_op jit(solution)/shard_map/ppermute | solution.py:399
  24.7 1.3 %collective-permute-start.8 = (f32[4,512]{1,0:T(4,128)S(1)}, f32[4,512]{1,0:T(4,128)S(1)}, u32[]{:S(2)}, u32[]{:S(2)}) collective-permute-start(f32[4,512]{1,0:T(4,128)S(1)} %add.10), channel_id=1, source_target_pairs={{0,5},{1,4},{2,7},{3,6},{4,1},{5,0},{6,3},{7,2},{8,13},{9,12},{10,... | collective-permute-start | bytes 24584 | tf_op jit(solution)/shard_map/ppermute | solution.py:399
  26.4 1.3 %collective-permute-done.8 = f32[4,512]{1,0:T(4,128)S(1)} collective-permute-done((f32[4,512]{1,0:T(4,128)S(1)}, f32[4,512]{1,0:T(4,128)S(1)}, u32[]{:S(2)}, u32[]{:S(2)}) %collective-permute-start.8) | collective-permute-done | bytes 8224 | tf_op jit(solution)/shard_map/ppermute | solution.py:399
  27.8 0.4 %collective-permute-start.9 = (f32[12,512]{1,0:T(8,128)S(1)}, f32[12,512]{1,0:T(8,128)S(1)}, u32[]{:S(2)}, u32[]{:S(2)}) collective-permute-start(f32[12,512]{1,0:T(8,128)S(1)} %get-tuple-element.57), channel_id=1, source_target_pairs={{0,9},{1,8},{2,11},{3,10},{8,1},{9,0},{10,3},{11,2},{16,17},{17,16... | collective-permute-start | bytes 73736 | tf_op jit(solution)/shard_map/ppermute | solution.py:445
  28.2 2.6 %collective-permute-start.11 = (f32[4,512]{1,0:T(4,128)S(1)}, f32[4,512]{1,0:T(4,128)S(1)}, u32[]{:S(2)}, u32[]{:S(2)}) collective-permute-start(f32[4,512]{1,0:T(4,128)S(1)} %get-tuple-element.59), channel_id=1, source_target_pairs={{0,1},{1,0},{2,3},{3,2},{8,9},{9,8},{10,11},{11,10},{16,25},{17,24... | collective-permute-start | bytes 24584 | tf_op jit(solution)/shard_map/ppermute | solution.py:445
  30.8 1.2 %scatter_blocks.1 = (f32[1536,128]{1,0:T(8,128)}, f32[1536,128]{1,0:T(8,128)}) custom-call(bf16[512,512]{1,0:T(8,128)(2,1)S(1)} %copy-done.1, f32[128,1536]{1,0:T(8,128)S(1)} %get-tuple-element.52.inner_ref._, f32[1536,128]{1,0:T(8,128)S(1)} %get-tuple-element.53.green_ref, f32[4,512]{1,0:T(4,128)S(1)} %multiply_add_fusion.mixed_ref), custom_call_target="tpu_custom_call" | custom-call | tf_op jit(solution)/shard_map/scatter_blocks/pallas_call | solution.py:309
  32.1 1.0 %last_block.1 = f32[1536,128]{1,0:T(8,128)} custom-call(bf16[512,512]{1,0:T(8,128)(2,1)S(1)} %copy-done.1, f32[128,1536]{1,0:T(8,128)S(1)} %get-tuple-element.52.inner_ref._, f32[4,512]{1,0:T(4,128)S(1)} %multiply_add_fusion.mixed_ref, f32[1536,128]{1,0:T(8,128)} %get-tuple-element.56._, ...), custom_call_target="tpu_custom_call", output_to_operand_aliasing={{}: (3, {})} | custom-call | tf_op jit(solution)/shard_map/last_block/pallas_call | solution.py:343
  (27 shorter events, 2.1 us)
Async XLA Ops:
  0.6 1.9 %copy-start = (f32[1,3,512,512]{3,2,1,0:T(8,128)S(1)}, f32[1,3,512,512]{3,2,1,0:T(8,128)}, u32[]{:S(2)}) copy-start(f32[1,3,512,512]{3,2,1,0:T(8,128)} %param.5) | copy-start | bytes 9437188
  0.6 2.1 %copy-start.2 = (f32[1,1536,128]{2,1,0:T(8,128)S(1)}, f32[1,1536,128]{2,1,0:T(8,128)}, u32[]{:S(2)}) copy-start(f32[1,1536,128]{2,1,0:T(8,128)} %param.6) | copy-start | bytes 2359300
  0.7 9.2 %copy-start.3 = (f32[8]{0:T(128)S(1)}, f32[8]{0:T(128)}, u32[]{:S(2)}) copy-start(f32[8]{0:T(128)} %strength_ref.1) | copy-start | bytes 100
  0.7 9.2 %copy-start.4 = (s32[8]{0:T(128)S(1)}, s32[8]{0:T(128)}, u32[]{:S(2)}) copy-start(s32[8]{0:T(128)} %shift_ref.1) | copy-start | bytes 100
  0.7 5.3 %collective-permute-start.1 = (f32[72,512]{1,0:T(8,128)S(1)}, f32[72,512]{1,0:T(8,128)S(1)}, u32[]{:S(2)}, u32[]{:S(2)}) collective-permute-start(f32[72,512]{1,0:T(8,128)S(1)} %first_chain.1), channel_id=1, source_target_pairs={{0,8},{1,9},{2,10},{3,11},{8,0},{9,1},{10,2},{11,3},{16,17},{17,16... | collective-permute-start | bytes 442376 | tf_op jit(solution)/shard_map/ppermute | solution.py:416
  5.3 1.7 %collective-permute-start = (f32[56,512]{1,0:T(8,128)S(1)}, f32[56,512]{1,0:T(8,128)S(1)}, u32[]{:S(2)}, u32[]{:S(2)}) collective-permute-start(f32[56,512]{1,0:T(8,128)S(1)} %get-tuple-element.35.offset_ref), channel_id=1, source_target_pairs={{0,8},{1,9},{2,10},{3,11},{8,0},{9,1},{10,2},{11,3},{16,17},{17,16... | collective-permute-start | bytes 344072 | tf_op jit(solution)/shard_map/ppermute | solution.py:416
  6.4 5.5 %collective-permute-start.2 = (f32[72,512]{1,0:T(8,128)S(1)}, f32[72,512]{1,0:T(8,128)S(1)}, u32[]{:S(2)}, u32[]{:S(2)}) collective-permute-start(f32[72,512]{1,0:T(8,128)S(1)} %get-tuple-element.37._), channel_id=1, source_target_pairs={{0,1},{1,0},{2,3},{3,2},{8,16},{9,17},{10,18},{11,19},{16,8},{17,9... | collective-permute-start | bytes 442376 | tf_op jit(solution)/shard_map/ppermute | solution.py:416
  7.4 6.8 %collective-permute-start.4 = (f32[56,512]{1,0:T(8,128)S(1)}, f32[56,512]{1,0:T(8,128)S(1)}, u32[]{:S(2)}, u32[]{:S(2)}) collective-permute-start(f32[56,512]{1,0:T(8,128)S(1)} %get-tuple-element.38._), channel_id=1, source_target_pairs={{0,1},{1,0},{2,3},{3,2},{8,16},{9,17},{10,18},{11,19},{16,8},{17,9... | collective-permute-start | bytes 344072 | tf_op jit(solution)/shard_map/ppermute | solution.py:416
  12.2 3.5 %collective-permute-start.3 = (f32[72,512]{1,0:T(8,128)S(1)}, f32[72,512]{1,0:T(8,128)S(1)}, u32[]{:S(2)}, u32[]{:S(2)}) collective-permute-start(f32[72,512]{1,0:T(8,128)S(1)} %get-tuple-element.44._), channel_id=1, source_target_pairs={{16,24},{17,25},{18,26},{19,27},{20,28},{21,29},{22,30},{23,31}} | collective-permute-start | bytes 442376 | tf_op jit(solution)/shard_map/ppermute | solution.py:416
  14.4 4.2 %collective-permute-start.5 = (f32[56,512]{1,0:T(8,128)S(1)}, f32[56,512]{1,0:T(8,128)S(1)}, u32[]{:S(2)}, u32[]{:S(2)}) collective-permute-start(f32[56,512]{1,0:T(8,128)S(1)} %get-tuple-element.48), channel_id=1, source_target_pairs={{16,24},{17,25},{18,26},{19,27},{20,28},{21,29},{22,30},{23,31}} | collective-permute-start | bytes 344072 | tf_op jit(solution)/shard_map/ppermute | solution.py:416
  15.7 10.3 %copy-start.1 = (bf16[512,512]{1,0:T(8,128)(2,1)S(1)}, bf16[512,512]{1,0:T(8,128)(2,1)}, u32[]{:S(2)}) copy-start(bf16[512,512]{1,0:T(8,128)(2,1)} %coupling_ref.5) | copy-start | bytes 1572868
  19.3 2.3 %collective-permute-start.6 = (f32[4,512]{1,0:T(4,128)S(1)}, f32[4,512]{1,0:T(4,128)S(1)}, u32[]{:S(2)}, u32[]{:S(2)}) collective-permute-start(f32[4,512]{1,0:T(4,128)S(1)} %get-tuple-element.54), channel_id=1, source_target_pairs={{0,1},{1,0},{2,3},{3,2},{4,5},{5,4},{6,7},{7,6},{8,9},{9,8},{10,11... | collective-permute-start | bytes 24584 | tf_op jit(solution)/shard_map/ppermute | solution.py:399
  21.6 3.1 %collective-permute-start.7 = (f32[4,512]{1,0:T(4,128)S(1)}, f32[4,512]{1,0:T(4,128)S(1)}, u32[]{:S(2)}, u32[]{:S(2)}) collective-permute-start(f32[4,512]{1,0:T(4,128)S(1)} %add.9), channel_id=1, source_target_pairs={{0,3},{1,2},{2,1},{3,0},{4,7},{5,6},{6,5},{7,4},{8,11},{9,10},{10,... | collective-permute-start | bytes 24584 | tf_op jit(solution)/shard_map/ppermute | solution.py:399
  24.7 3.1 %collective-permute-start.8 = (f32[4,512]{1,0:T(4,128)S(1)}, f32[4,512]{1,0:T(4,128)S(1)}, u32[]{:S(2)}, u32[]{:S(2)}) collective-permute-start(f32[4,512]{1,0:T(4,128)S(1)} %add.10), channel_id=1, source_target_pairs={{0,5},{1,4},{2,7},{3,6},{4,1},{5,0},{6,3},{7,2},{8,13},{9,12},{10,... | collective-permute-start | bytes 24584 | tf_op jit(solution)/shard_map/ppermute | solution.py:399
  27.8 4.3 %collective-permute-start.9 = (f32[12,512]{1,0:T(8,128)S(1)}, f32[12,512]{1,0:T(8,128)S(1)}, u32[]{:S(2)}, u32[]{:S(2)}) collective-permute-start(f32[12,512]{1,0:T(8,128)S(1)} %get-tuple-element.57), channel_id=1, source_target_pairs={{0,9},{1,8},{2,11},{3,10},{8,1},{9,0},{10,3},{11,2},{16,17},{17,16... | collective-permute-start | bytes 73736 | tf_op jit(solution)/shard_map/ppermute | solution.py:445
  28.2 3.9 %collective-permute-start.10 = (f32[8,512]{1,0:T(8,128)S(1)}, f32[8,512]{1,0:T(8,128)S(1)}, u32[]{:S(2)}, u32[]{:S(2)}) collective-permute-start(f32[8,512]{1,0:T(8,128)S(1)} %get-tuple-element.58), channel_id=1, source_target_pairs={{0,1},{1,0},{2,3},{3,2},{8,17},{9,16},{10,19},{11,18},{16,9},{17,8... | collective-permute-start | bytes 49160 | tf_op jit(solution)/shard_map/ppermute | solution.py:445
  28.2 3.9 %collective-permute-start.11 = (f32[4,512]{1,0:T(4,128)S(1)}, f32[4,512]{1,0:T(4,128)S(1)}, u32[]{:S(2)}, u32[]{:S(2)}) collective-permute-start(f32[4,512]{1,0:T(4,128)S(1)} %get-tuple-element.59), channel_id=1, source_target_pairs={{0,1},{1,0},{2,3},{3,2},{8,9},{9,8},{10,11},{11,10},{16,25},{17,24... | collective-permute-start | bytes 24584 | tf_op jit(solution)/shard_map/ppermute | solution.py:445

commit v5 on v4

--- a/solution.py
+++ b/solution.py
@@ -10,7 +10,6 @@
 F32 = jnp.float32
 BF16 = jnp.bfloat16
 VMEM = pl.BlockSpec(memory_space=pltpu.VMEM)
-SMEM = pl.BlockSpec(memory_space=pltpu.SMEM)
 HBM = pl.BlockSpec(memory_space=pltpu.HBM)
 PARAMS = pltpu.CompilerParams(vmem_limit_bytes=32 * 1024 * 1024)
 WHOLE = pltpu.CompilerParams(vmem_limit_bytes=107 * 512 * 1024)
@@ -155,12 +154,14 @@
 ):
     orbs = first_ref.shape[1]
     here = lax.axis_index("energy")
+    goal = here + shift_ref[...]
+    goal = jnp.where(goal >= points, goal - points, goal)
     for offset in range(points):
-        total = jnp.float32(0.0)
-        for mode in range(strength_ref.shape[0]):
-            taken = lax.rem(here + shift_ref[mode], points) == lax.rem(here + points - offset, points)
-            total = total + jnp.where(taken, strength_ref[mode], 0.0)
-        weight_ref[offset : offset + 1, :] = jnp.full((1, orbs), total * scale, F32)
+        from_here = lax.rem(here + points - offset, points)
+        total = jnp.sum(
+            jnp.where(goal == from_here, strength_ref[...], 0.0), axis=1, keepdims=True
+        )
+        weight_ref[offset : offset + 1, :] = jnp.broadcast_to(total * scale, (1, orbs))
     for k in range(mats_ref.shape[0] + 1):
         columns = slice(k * orbs, (k + 1) * orbs)
         matrix = first_ref[0] if k == 0 else mats_ref[k - 1]
@@ -182,7 +183,7 @@
             jax.ShapeDtypeStruct((width, length), F32),
             jax.ShapeDtypeStruct((points, orbs), F32),
         ),
-        in_specs=[VMEM, VMEM, VMEM, VMEM, SMEM, SMEM, VMEM],
+        in_specs=[VMEM] * 7,
         out_specs=(VMEM,) * 4,
         compiler_params=PARAMS,
         name="turned_blocks",
@@ -283,73 +284,96 @@
     return rows[k + 1] + 0.5 * (rows[k] + rows[k + 2])
 
 
-def scatter_kernel(coupling_ref, inner_ref, green_ref, mixed_ref, out_ref, kept_ref, staged, sems, kept_sem):
+def scattered_block(coupling, inner_ref, rows, k):
+    orbs = coupling.shape[0]
+    columns = slice(k * orbs, (k + 1) * orbs)
+    return dot_t(coupling, (inner_ref[:, columns] * smoothed(rows, k)).astype(BF16))
+
+
+def early_kernel(coupling_ref, inner_ref, green_ref, mixed_ref, out_ref, kept_ref, staged, sems, kept_sem):
     kept_copy = pltpu.make_async_copy(green_ref, kept_ref, kept_sem)
     kept_copy.start()
     orbs = coupling_ref.shape[0]
     count = inner_ref.shape[1] // orbs
+    coupling = coupling_ref[...]
     rows = [mixed_ref[k : k + 1, :] for k in range(count + 1)]
-    coupling = coupling_ref[...]
-    copies = []
+    rows.append(jnp.zeros_like(rows[0]))
+    last = lax.axis_index("cuts") == lax.axis_size("cuts") - 1
+
+    def block_copy(k):
+        columns = slice(k * orbs, (k + 1) * orbs)
+        return pltpu.make_async_copy(staged.at[columns], out_ref.at[columns], sems.at[k])
+
+    def block_start(k):
+        staged[k * orbs : (k + 1) * orbs, :] = scattered_block(coupling, inner_ref, rows, k)
+        block_copy(k).start()
+
     for k in range(count - 1):
-        columns = slice(k * orbs, (k + 1) * orbs)
-        scaled = (inner_ref[:, columns] * smoothed(rows, k)).astype(BF16)
-        staged[columns, :] = dot_t(coupling, scaled)
-        copies.append(pltpu.make_async_copy(staged.at[columns], out_ref.at[columns], sems.at[k]))
-        copies[-1].start()
-    for copy in copies:
-        copy.wait()
+        block_start(k)
+
+    @pl.when(last)
+    def _():
+        block_start(count - 1)
+
+    for k in range(count - 1):
+        block_copy(k).wait()
+
+    @pl.when(last)
+    def _():
+        block_copy(count - 1).wait()
+
     kept_copy.wait()
 
 
-def scatter_blocks(coupling, inner, green, mixed):
+def early_blocks(coupling, inner, green, mixed):
     width, length = inner.shape
     orbs = coupling.shape[0]
     shape = jax.ShapeDtypeStruct((length, width), F32)
     return pl.pallas_call(
-        scatter_kernel,
+        early_kernel,
         out_shape=(shape, shape),
         in_specs=[VMEM] * 4,
         out_specs=(HBM, HBM),
         scratch_shapes=[
-            pltpu.VMEM((length - orbs, width), F32),
-            pltpu.SemaphoreType.DMA((length // orbs - 1,)),
+            pltpu.VMEM((length, width), F32),
+            pltpu.SemaphoreType.DMA((length // orbs,)),
             pltpu.SemaphoreType.DMA,
         ],
         compiler_params=PARAMS,
-        name="scatter_blocks",
+        name="early_blocks",
     )(coupling, inner, green, mixed)
 
 
-def last_kernel(coupling_ref, inner_ref, mixed_ref, _, *rest):
-    *after_refs, out_ref, staged, sem = rest
+def late_kernel(coupling_ref, inner_ref, mixed_ref, _, *rest):
+    *after_refs, out_ref, block, sem = rest
     orbs = coupling_ref.shape[0]
     count = inner_ref.shape[1] // orbs
     here = lax.axis_index("cuts")
-    after = jnp.zeros((1, orbs), F32)
-    for lower, after_ref in enumerate(after_refs):
-        after = jnp.where(here == lower, after_ref[:1, :], after)
-    rows = [mixed_ref[k : k + 1, :] for k in range(count + 1)] + [after]
-    columns = slice((count - 1) * orbs, count * orbs)
-    scaled = (inner_ref[:, columns] * smoothed(rows, count - 1)).astype(BF16)
-    staged[...] = dot_t(coupling_ref[...], scaled)
-    copy = pltpu.make_async_copy(staged, out_ref.at[columns], sem)
-    copy.start()
-    copy.wait()
-
-
-def last_block(coupling, inner, mixed, partial, after):
+
+    @pl.when(here < lax.axis_size("cuts") - 1)
+    def _():
+        after = jnp.zeros((1, orbs), F32)
+        for lower, after_ref in enumerate(after_refs):
+            after = jnp.where(here == lower, after_ref[:1, :], after)
+        rows = [mixed_ref[k : k + 1, :] for k in range(count + 1)] + [after]
+        block[...] = scattered_block(coupling_ref[...], inner_ref, rows, count - 1)
+        copy = pltpu.make_async_copy(block, out_ref.at[slice((count - 1) * orbs, count * orbs)], sem)
+        copy.start()
+        copy.wait()
+
+
+def late_blocks(coupling, inner, mixed, out, after):
     orbs = coupling.shape[0]
     return pl.pallas_call(
-        last_kernel,
-        out_shape=jax.ShapeDtypeStruct(partial.shape, F32),
+        late_kernel,
+        out_shape=jax.ShapeDtypeStruct(out.shape, F32),
         in_specs=[VMEM] * 3 + [HBM] + [VMEM] * len(after),
         out_specs=HBM,
-        scratch_shapes=[pltpu.VMEM((orbs, partial.shape[1]), F32), pltpu.SemaphoreType.DMA],
+        scratch_shapes=[pltpu.VMEM((orbs, out.shape[1]), F32), pltpu.SemaphoreType.DMA],
         input_output_aliases={3: 0},
         compiler_params=PARAMS,
-        name="last_block",
-    )(coupling, inner, mixed, partial, *after)
+        name="late_blocks",
+    )(coupling, inner, mixed, out, *after)
 
 
 def edge_kernel(mixed_ref, _, *out_refs):
@@ -423,7 +447,7 @@
                 leaving.append(after)
         if blocks is None:
             *blocks, weights = turned_blocks(
-                mats, srcs, middle, local, strength, mode_shift, leaving[-1], points, 1.0 / (width * group)
+                mats, srcs, middle, local, strength[None], mode_shift[None], leaving[-1], points, 1.0 / (width * group)
             )
     green, sums = [], None
     for piece in range(pieces):
@@ -447,8 +471,8 @@
         )
         for lower in range(cuts - 1)
     ]
-    partial, kept = scatter_blocks(coupling, inner, kept, mixed)
-    scattered = last_block(coupling, inner, mixed, partial, after)
+    out, kept = early_blocks(coupling, inner, kept, mixed)
+    scattered = late_blocks(coupling, inner, mixed, out, after)
     return kept[None], scattered[None]
 
 

time: 33.5 us -> 33.3 us (level)
  waiting for transfers between devices: 7.46 us -> 8.23 us
  Pallas kernels: 9.27 us -> 8.75 us
    ppermute x6, waiting for transfers between devices: 3.43 us -> 4.01 us  [body(): got = [lax.ppermute(piece, ('cuts', 'group'), pairs) for piece in leaving]]
    pallas_call x1, Pallas kernels: 1.28 us -> 0.78 us  [turned_blocks(): pl.pallas_call(functools.partial(turned_kernel, points, scale), out_shape...]
  transfers between devices with their start and end apart: 12 -> 12, of which waited for: 8 -> 8; matrix products, arithmetic and copies ran while one was open for 0% -> 0% of each run, Pallas kernels for 23% -> 21%
where the time goes in v5:
time: 33.3 us; the launch traced here: 33.2 us
  starting transfers between devices  14.1 us (42%)
  Pallas kernels  8.75 us (26%)
  waiting for transfers between devices  8.23 us (25%)
  local copies, waits for them, and re-layouts  1.28 us (4%)
  between operations  0.79 us (2%)
    ppermute x6, starting transfers between devices, body(): got = [lax.ppermute(piece, ('cuts', 'group'), pairs) for piece in leaving]  7.22 us
    ppermute x3, waiting for transfers between devices, across(): return lax.ppermute(value, ('energy', 'group'), pairs)  4.15 us
    ppermute x6, waiting for transfers between devices, body(): got = [lax.ppermute(piece, ('cuts', 'group'), pairs) for piece in leaving]  4.01 us
    ppermute x3, starting transfers between devices, across(): return lax.ppermute(value, ('energy', 'group'), pairs)  3.89 us
    ppermute x3, starting transfers between devices, body(): lax.ppermute(edges[lower], ('cuts', 'group'), paired([lower], cuts, group...  3.01 us
    pallas_call x1, Pallas kernels, composites(): pl.pallas_call(composite_kernel, out_shape=(jax.ShapeDtypeStruct((count -...  2.62 us
    pallas_call x2, Pallas kernels, green_piece(): pl.pallas_call(functools.partial(green_kernel, step, start), out_shape=(j...  1.4 us
    unnamed x10, local copies, waits for them, and re-layouts  1.27 us
  transfers between devices with their start and end apart: 12, of which 8 were waited for; matrix products, arithmetic and copies ran while one was open for 0% of the time, Pallas kernels for 21%

profile of v5, /device:TPU:17, one launch (start us, length us, event | category | flops | bytes accessed | tf_op | source)
XLA Modules:
  0.0 33.2 jit_solution(5183427642240304431)
XLA Ops:
  0.7 0.7 %collective-permute-start.1 = (f32[72,512]{1,0:T(8,128)S(1)}, f32[72,512]{1,0:T(8,128)S(1)}, u32[]{:S(2)}, u32[]{:S(2)}) collective-permute-start(f32[72,512]{1,0:T(8,128)S(1)} %first_chain.1), channel_id=1, source_target_pairs={{0,8},{1,9},{2,10},{3,11},{8,0},{9,1},{10,2},{11,3},{16,17},{17,16... | collective-permute-start | bytes 442376 | tf_op jit(solution)/shard_map/ppermute | solution.py:440
  1.5 1.1 %copy-done = f32[1,3,512,512]{3,2,1,0:T(8,128)S(1)} copy-done((f32[1,3,512,512]{3,2,1,0:T(8,128)S(1)}, f32[1,3,512,512]{3,2,1,0:T(8,128)}, u32[]{:S(2)}) %copy-start) | copy-done | bytes 3145752
  2.7 2.6 %composites.1 = (f32[1,512,512]{2,1,0:T(8,128)S(1)}, f32[1,512,128]{2,1,0:T(8,128)S(1)}, bf16[512,512]{1,0:T(8,128)(2,1)S(1)}, bf16[512,512]{1,0:T(8,128)(2,1)S(...) custom-call(f32[3,512,512]{2,1,0:T(8,128)S(1)} %bitcast.9, f32[1536,128]{1,0:T(8,128)S(1)} %bitcast.12), custom_call_target="tpu_custom_call" | custom-call | flops 1610612736 | bytes 6291456 | tf_op jit(solution)/shard_map/composites/pallas_call | solution.py:132
  5.4 0.7 %collective-permute-start = (f32[56,512]{1,0:T(8,128)S(1)}, f32[56,512]{1,0:T(8,128)S(1)}, u32[]{:S(2)}, u32[]{:S(2)}) collective-permute-start(f32[56,512]{1,0:T(8,128)S(1)} %get-tuple-element.35.offset_ref), channel_id=1, source_target_pairs={{0,8},{1,9},{2,10},{3,11},{8,0},{9,1},{10,2},{11,3},{16,17},{17,16... | collective-permute-start | bytes 344072 | tf_op jit(solution)/shard_map/ppermute | solution.py:440
  6.4 0.5 %collective-permute-start.2 = (f32[72,512]{1,0:T(8,128)S(1)}, f32[72,512]{1,0:T(8,128)S(1)}, u32[]{:S(2)}, u32[]{:S(2)}) collective-permute-start(f32[72,512]{1,0:T(8,128)S(1)} %get-tuple-element.37._), channel_id=1, source_target_pairs={{0,1},{1,0},{2,3},{3,2},{8,16},{9,17},{10,18},{11,19},{16,8},{17,9... | collective-permute-start | bytes 442376 | tf_op jit(solution)/shard_map/ppermute | solution.py:440
  7.4 2.6 %collective-permute-start.4 = (f32[56,512]{1,0:T(8,128)S(1)}, f32[56,512]{1,0:T(8,128)S(1)}, u32[]{:S(2)}, u32[]{:S(2)}) collective-permute-start(f32[56,512]{1,0:T(8,128)S(1)} %get-tuple-element.38._), channel_id=1, source_target_pairs={{0,1},{1,0},{2,3},{3,2},{8,16},{9,17},{10,18},{11,19},{16,8},{17,9... | collective-permute-start | bytes 344072 | tf_op jit(solution)/shard_map/ppermute | solution.py:440
  10.0 0.8 %turned_blocks.1 = (bf16[512,1024]{1,0:T(8,128)(2,1)S(1)}, bf16[512,1024]{1,0:T(8,128)(2,1)S(1)}, f32[128,1024]{1,0:T(8,128)S(1)}, f32[2,512]{1,0:T(2,128)S(1)}) custom-call(f32[3,512,512]{2,1,0:T(8,128)S(1)} %bitcast.10, f32[1536,128]{1,0:T(8,128)S(1)} %bitcast.13, f32[1,512,512]{2,1,0:T(8,128)S(1)} %get-tuple-element.31.mats_ref, ...), custom_call_target="tpu_custom_call" | custom-call | tf_op jit(solution)/shard_map/turned_blocks/pallas_call | solution.py:178
  10.8 1.2 %collective-permute-done.2.got_ref = f32[72,512]{1,0:T(8,128)S(1)} collective-permute-done((f32[72,512]{1,0:T(8,128)S(1)}, f32[72,512]{1,0:T(8,128)S(1)}, u32[]{:S(2)}, u32[]{:S(2)}) %collective-permute-start.2) | collective-permute-done | bytes 147488 | tf_op jit(solution)/shard_map/ppermute | solution.py:440
  12.3 1.3 %collective-permute-start.3 = (f32[72,512]{1,0:T(8,128)S(1)}, f32[72,512]{1,0:T(8,128)S(1)}, u32[]{:S(2)}, u32[]{:S(2)}) collective-permute-start(f32[72,512]{1,0:T(8,128)S(1)} %get-tuple-element.44._), channel_id=1, source_target_pairs={{16,24},{17,25},{18,26},{19,27},{20,28},{21,29},{22,30},{23,31}} | collective-permute-start | bytes 442376 | tf_op jit(solution)/shard_map/ppermute | solution.py:440
  13.6 0.6 %collective-permute-done.4.got_ref = f32[56,512]{1,0:T(8,128)S(1)} collective-permute-done((f32[56,512]{1,0:T(8,128)S(1)}, f32[56,512]{1,0:T(8,128)S(1)}, u32[]{:S(2)}, u32[]{:S(2)}) %collective-permute-start.4) | collective-permute-done | bytes 114720 | tf_op jit(solution)/shard_map/ppermute | solution.py:440
  14.4 1.3 %collective-permute-start.5 = (f32[56,512]{1,0:T(8,128)S(1)}, f32[56,512]{1,0:T(8,128)S(1)}, u32[]{:S(2)}, u32[]{:S(2)}) collective-permute-start(f32[56,512]{1,0:T(8,128)S(1)} %get-tuple-element.48), channel_id=1, source_target_pairs={{16,24},{17,25},{18,26},{19,27},{20,28},{21,29},{22,30},{23,31}} | collective-permute-start | bytes 344072 | tf_op jit(solution)/shard_map/ppermute | solution.py:440
  15.8 0.7 %green_piece.2 = (f32[72,1536]{1,0:T(8,128)S(1)}, f32[4,512]{1,0:T(4,128)S(1)}) custom-call(bf16[512,1024]{1,0:T(8,128)(2,1)S(1)} %get-tuple-element.39.high_ref, bf16[512,1024]{1,0:T(8,128)(2,1)S(1)} %get-tuple-element.40.low_ref, f32[128,1024]{1,0:T(8,128)S(1)} %get-tuple-element.41.turned_ref, ...), custom_call_target="tpu_custom_call" | custom-call | tf_op jit(solution)/shard_map/green_piece/pallas_call | solution.py:239
  16.5 2.2 %collective-permute-done.5.got_ref = f32[56,512]{1,0:T(8,128)S(1)} collective-permute-done((f32[56,512]{1,0:T(8,128)S(1)}, f32[56,512]{1,0:T(8,128)S(1)}, u32[]{:S(2)}, u32[]{:S(2)}) %collective-permute-start.5) | collective-permute-done | bytes 114720 | tf_op jit(solution)/shard_map/ppermute | solution.py:440
  18.7 0.7 %green_piece.3 = (f32[56,1536]{1,0:T(8,128)S(1)}, f32[4,512]{1,0:T(4,128)S(1)}) custom-call(bf16[512,1024]{1,0:T(8,128)(2,1)S(1)} %get-tuple-element.39.high_ref, bf16[512,1024]{1,0:T(8,128)(2,1)S(1)} %get-tuple-element.40.low_ref, f32[128,1024]{1,0:T(8,128)S(1)} %get-tuple-element.41.turned_ref, ...), custom_call_target="tpu_custom_call" | custom-call | tf_op jit(solution)/shard_map/green_piece/pallas_call | solution.py:239
  19.3 1.5 %collective-permute-start.6 = (f32[4,512]{1,0:T(4,128)S(1)}, f32[4,512]{1,0:T(4,128)S(1)}, u32[]{:S(2)}, u32[]{:S(2)}) collective-permute-start(f32[4,512]{1,0:T(4,128)S(1)} %get-tuple-element.54), channel_id=1, source_target_pairs={{0,1},{1,0},{2,3},{3,2},{4,5},{5,4},{6,7},{7,6},{8,9},{9,8},{10,11... | collective-permute-start | bytes 24584 | tf_op jit(solution)/shard_map/ppermute | solution.py:423
  20.8 0.8 %collective-permute-done.6 = f32[4,512]{1,0:T(4,128)S(1)} collective-permute-done((f32[4,512]{1,0:T(4,128)S(1)}, f32[4,512]{1,0:T(4,128)S(1)}, u32[]{:S(2)}, u32[]{:S(2)}) %collective-permute-start.6) | collective-permute-done | bytes 8224 | tf_op jit(solution)/shard_map/ppermute | solution.py:423
  21.6 1.2 %collective-permute-start.7 = (f32[4,512]{1,0:T(4,128)S(1)}, f32[4,512]{1,0:T(4,128)S(1)}, u32[]{:S(2)}, u32[]{:S(2)}) collective-permute-start(f32[4,512]{1,0:T(4,128)S(1)} %add.9), channel_id=1, source_target_pairs={{0,3},{1,2},{2,1},{3,0},{4,7},{5,6},{6,5},{7,4},{8,11},{9,10},{10,... | collective-permute-start | bytes 24584 | tf_op jit(solution)/shard_map/ppermute | solution.py:423
  22.9 1.9 %collective-permute-done.7 = f32[4,512]{1,0:T(4,128)S(1)} collective-permute-done((f32[4,512]{1,0:T(4,128)S(1)}, f32[4,512]{1,0:T(4,128)S(1)}, u32[]{:S(2)}, u32[]{:S(2)}) %collective-permute-start.7) | collective-permute-done | bytes 8224 | tf_op jit(solution)/shard_map/ppermute | solution.py:423
  24.7 1.2 %collective-permute-start.8 = (f32[4,512]{1,0:T(4,128)S(1)}, f32[4,512]{1,0:T(4,128)S(1)}, u32[]{:S(2)}, u32[]{:S(2)}) collective-permute-start(f32[4,512]{1,0:T(4,128)S(1)} %add.10), channel_id=1, source_target_pairs={{0,5},{1,4},{2,7},{3,6},{4,1},{5,0},{6,3},{7,2},{8,13},{9,12},{10,... | collective-permute-start | bytes 24584 | tf_op jit(solution)/shard_map/ppermute | solution.py:423
  26.4 1.5 %collective-permute-done.8 = f32[4,512]{1,0:T(4,128)S(1)} collective-permute-done((f32[4,512]{1,0:T(4,128)S(1)}, f32[4,512]{1,0:T(4,128)S(1)}, u32[]{:S(2)}, u32[]{:S(2)}) %collective-permute-start.8) | collective-permute-done | bytes 8224 | tf_op jit(solution)/shard_map/ppermute | solution.py:423
  27.8 0.4 %collective-permute-start.9 = (f32[12,512]{1,0:T(8,128)S(1)}, f32[12,512]{1,0:T(8,128)S(1)}, u32[]{:S(2)}, u32[]{:S(2)}) collective-permute-start(f32[12,512]{1,0:T(8,128)S(1)} %get-tuple-element.57), channel_id=1, source_target_pairs={{0,9},{1,8},{2,11},{3,10},{8,1},{9,0},{10,3},{11,2},{16,17},{17,16... | collective-permute-start | bytes 73736 | tf_op jit(solution)/shard_map/ppermute | solution.py:469
  28.2 2.6 %collective-permute-start.11 = (f32[4,512]{1,0:T(4,128)S(1)}, f32[4,512]{1,0:T(4,128)S(1)}, u32[]{:S(2)}, u32[]{:S(2)}) collective-permute-start(f32[4,512]{1,0:T(4,128)S(1)} %get-tuple-element.59), channel_id=1, source_target_pairs={{0,1},{1,0},{2,3},{3,2},{8,9},{9,8},{10,11},{11,10},{16,25},{17,24... | collective-permute-start | bytes 24584 | tf_op jit(solution)/shard_map/ppermute | solution.py:469
  30.8 1.3 %early_blocks.1 = (f32[1536,128]{1,0:T(8,128)}, f32[1536,128]{1,0:T(8,128)}) custom-call(bf16[512,512]{1,0:T(8,128)(2,1)S(1)} %copy-done.1, f32[128,1536]{1,0:T(8,128)S(1)} %get-tuple-element.52.inner_ref._, f32[1536,128]{1,0:T(8,128)S(1)} %get-tuple-element.53.green_ref, f32[4,512]{1,0:T(4,128)S(1)} %multiply_add_fusion.mixed_ref), custom_call_target="tpu_custom_call" | custom-call | tf_op jit(solution)/shard_map/early_blocks/pallas_call | solution.py:332
  32.2 1.0 %late_blocks.1 = f32[1536,128]{1,0:T(8,128)} custom-call(bf16[512,512]{1,0:T(8,128)(2,1)S(1)} %copy-done.1, f32[128,1536]{1,0:T(8,128)S(1)} %get-tuple-element.52.inner_ref._, f32[4,512]{1,0:T(4,128)S(1)} %multiply_add_fusion.mixed_ref, f32[1536,128]{1,0:T(8,128)} %get-tuple-element.56._, ...), custom_call_target="tpu_custom_call", output_to_operand_aliasing={{}: (3, {})} | custom-call | tf_op jit(solution)/shard_map/late_blocks/pallas_call | solution.py:367
  (27 shorter events, 2.1 us)
Async XLA Ops:
  0.6 1.9 %copy-start = (f32[1,3,512,512]{3,2,1,0:T(8,128)S(1)}, f32[1,3,512,512]{3,2,1,0:T(8,128)}, u32[]{:S(2)}) copy-start(f32[1,3,512,512]{3,2,1,0:T(8,128)} %param.5) | copy-start | bytes 9437188
  0.6 2.1 %copy-start.2 = (f32[1,1536,128]{2,1,0:T(8,128)S(1)}, f32[1,1536,128]{2,1,0:T(8,128)}, u32[]{:S(2)}) copy-start(f32[1,1536,128]{2,1,0:T(8,128)} %param.6) | copy-start | bytes 2359300
  0.7 5.4 %collective-permute-start.1 = (f32[72,512]{1,0:T(8,128)S(1)}, f32[72,512]{1,0:T(8,128)S(1)}, u32[]{:S(2)}, u32[]{:S(2)}) collective-permute-start(f32[72,512]{1,0:T(8,128)S(1)} %first_chain.1), channel_id=1, source_target_pairs={{0,8},{1,9},{2,10},{3,11},{8,0},{9,1},{10,2},{11,3},{16,17},{17,16... | collective-permute-start | bytes 442376 | tf_op jit(solution)/shard_map/ppermute | solution.py:440
  5.3 4.6 %copy-start.3 = (f32[8]{0:T(128)S(1)}, f32[8]{0:T(128)}, u32[]{:S(2)}) copy-start(f32[8]{0:T(128)} %param.8) | copy-start | bytes 100
  5.4 4.6 %copy-start.4 = (s32[8]{0:T(128)S(1)}, s32[8]{0:T(128)}, u32[]{:S(2)}) copy-start(s32[8]{0:T(128)} %param.9) | copy-start | bytes 100
  5.4 1.7 %collective-permute-start = (f32[56,512]{1,0:T(8,128)S(1)}, f32[56,512]{1,0:T(8,128)S(1)}, u32[]{:S(2)}, u32[]{:S(2)}) collective-permute-start(f32[56,512]{1,0:T(8,128)S(1)} %get-tuple-element.35.offset_ref), channel_id=1, source_target_pairs={{0,8},{1,9},{2,10},{3,11},{8,0},{9,1},{10,2},{11,3},{16,17},{17,16... | collective-permute-start | bytes 344072 | tf_op jit(solution)/shard_map/ppermute | solution.py:440
  6.4 5.5 %collective-permute-start.2 = (f32[72,512]{1,0:T(8,128)S(1)}, f32[72,512]{1,0:T(8,128)S(1)}, u32[]{:S(2)}, u32[]{:S(2)}) collective-permute-start(f32[72,512]{1,0:T(8,128)S(1)} %get-tuple-element.37._), channel_id=1, source_target_pairs={{0,1},{1,0},{2,3},{3,2},{8,16},{9,17},{10,18},{11,19},{16,8},{17,9... | collective-permute-start | bytes 442376 | tf_op jit(solution)/shard_map/ppermute | solution.py:440
  7.4 6.8 %collective-permute-start.4 = (f32[56,512]{1,0:T(8,128)S(1)}, f32[56,512]{1,0:T(8,128)S(1)}, u32[]{:S(2)}, u32[]{:S(2)}) collective-permute-start(f32[56,512]{1,0:T(8,128)S(1)} %get-tuple-element.38._), channel_id=1, source_target_pairs={{0,1},{1,0},{2,3},{3,2},{8,16},{9,17},{10,18},{11,19},{16,8},{17,9... | collective-permute-start | bytes 344072 | tf_op jit(solution)/shard_map/ppermute | solution.py:440
  12.3 3.5 %collective-permute-start.3 = (f32[72,512]{1,0:T(8,128)S(1)}, f32[72,512]{1,0:T(8,128)S(1)}, u32[]{:S(2)}, u32[]{:S(2)}) collective-permute-start(f32[72,512]{1,0:T(8,128)S(1)} %get-tuple-element.44._), channel_id=1, source_target_pairs={{16,24},{17,25},{18,26},{19,27},{20,28},{21,29},{22,30},{23,31}} | collective-permute-start | bytes 442376 | tf_op jit(solution)/shard_map/ppermute | solution.py:440
  14.4 4.2 %collective-permute-start.5 = (f32[56,512]{1,0:T(8,128)S(1)}, f32[56,512]{1,0:T(8,128)S(1)}, u32[]{:S(2)}, u32[]{:S(2)}) collective-permute-start(f32[56,512]{1,0:T(8,128)S(1)} %get-tuple-element.48), channel_id=1, source_target_pairs={{16,24},{17,25},{18,26},{19,27},{20,28},{21,29},{22,30},{23,31}} | collective-permute-start | bytes 344072 | tf_op jit(solution)/shard_map/ppermute | solution.py:440
  15.8 10.2 %copy-start.1 = (bf16[512,512]{1,0:T(8,128)(2,1)S(1)}, bf16[512,512]{1,0:T(8,128)(2,1)}, u32[]{:S(2)}) copy-start(bf16[512,512]{1,0:T(8,128)(2,1)} %coupling_ref.5) | copy-start | bytes 1572868
  19.3 2.3 %collective-permute-start.6 = (f32[4,512]{1,0:T(4,128)S(1)}, f32[4,512]{1,0:T(4,128)S(1)}, u32[]{:S(2)}, u32[]{:S(2)}) collective-permute-start(f32[4,512]{1,0:T(4,128)S(1)} %get-tuple-element.54), channel_id=1, source_target_pairs={{0,1},{1,0},{2,3},{3,2},{4,5},{5,4},{6,7},{7,6},{8,9},{9,8},{10,11... | collective-permute-start | bytes 24584 | tf_op jit(solution)/shard_map/ppermute | solution.py:423
  21.6 3.1 %collective-permute-start.7 = (f32[4,512]{1,0:T(4,128)S(1)}, f32[4,512]{1,0:T(4,128)S(1)}, u32[]{:S(2)}, u32[]{:S(2)}) collective-permute-start(f32[4,512]{1,0:T(4,128)S(1)} %add.9), channel_id=1, source_target_pairs={{0,3},{1,2},{2,1},{3,0},{4,7},{5,6},{6,5},{7,4},{8,11},{9,10},{10,... | collective-permute-start | bytes 24584 | tf_op jit(solution)/shard_map/ppermute | solution.py:423
  24.7 3.1 %collective-permute-start.8 = (f32[4,512]{1,0:T(4,128)S(1)}, f32[4,512]{1,0:T(4,128)S(1)}, u32[]{:S(2)}, u32[]{:S(2)}) collective-permute-start(f32[4,512]{1,0:T(4,128)S(1)} %add.10), channel_id=1, source_target_pairs={{0,5},{1,4},{2,7},{3,6},{4,1},{5,0},{6,3},{7,2},{8,13},{9,12},{10,... | collective-permute-start | bytes 24584 | tf_op jit(solution)/shard_map/ppermute | solution.py:423
  27.8 4.3 %collective-permute-start.9 = (f32[12,512]{1,0:T(8,128)S(1)}, f32[12,512]{1,0:T(8,128)S(1)}, u32[]{:S(2)}, u32[]{:S(2)}) collective-permute-start(f32[12,512]{1,0:T(8,128)S(1)} %get-tuple-element.57), channel_id=1, source_target_pairs={{0,9},{1,8},{2,11},{3,10},{8,1},{9,0},{10,3},{11,2},{16,17},{17,16... | collective-permute-start | bytes 73736 | tf_op jit(solution)/shard_map/ppermute | solution.py:469
  28.2 3.9 %collective-permute-start.10 = (f32[8,512]{1,0:T(8,128)S(1)}, f32[8,512]{1,0:T(8,128)S(1)}, u32[]{:S(2)}, u32[]{:S(2)}) collective-permute-start(f32[8,512]{1,0:T(8,128)S(1)} %get-tuple-element.58), channel_id=1, source_target_pairs={{0,1},{1,0},{2,3},{3,2},{8,17},{9,16},{10,19},{11,18},{16,9},{17,8... | collective-permute-start | bytes 49160 | tf_op jit(solution)/shard_map/ppermute | solution.py:469
  28.2 3.9 %collective-permute-start.11 = (f32[4,512]{1,0:T(4,128)S(1)}, f32[4,512]{1,0:T(4,128)S(1)}, u32[]{:S(2)}, u32[]{:S(2)}) collective-permute-start(f32[4,512]{1,0:T(4,128)S(1)} %get-tuple-element.59), channel_id=1, source_target_pairs={{0,1},{1,0},{2,3},{3,2},{8,9},{9,8},{10,11},{11,10},{16,25},{17,24... | collective-permute-start | bytes 24584 | tf_op jit(solution)/shard_map/ppermute | solution.py:469

commit v6 on v5

--- a/solution.py
+++ b/solution.py
@@ -457,12 +457,12 @@
         green.append(part)
 
     other = 1 if group % 2 == 0 else 0
-    if other:
-        sums = sums + across(sums, 0, 1)
     sums = sums + sum(across(sums, 0, k + other) for k in range(1 + other, group, 1 + other))
     mixed = sums * weights[:1]
     for offset in range(1, points):
         mixed = mixed + across(sums, offset, other) * weights[offset : offset + 1]
+    if other:
+        mixed = mixed + across(mixed, 0, 1)
     inner, kept = inner_blocks(coupling, green)
     edges = edge_rows(mixed, inner, cuts)
     after = [

time: 33.3 us -> 33.3 us (level)
  starting transfers between devices: 14.1 us -> 15.2 us
  waiting for transfers between devices: 8.23 us -> 7.17 us
    ppermute x3, waiting for transfers between devices: 4.15 us -> 3.09 us  [across(): return lax.ppermute(value, ('energy', 'group'), pairs)]
    ppermute x3, starting transfers between devices: 3.89 us -> 4.96 us  [across(): return lax.ppermute(value, ('energy', 'group'), pairs)]
where the time goes in v6:
time: 33.3 us; the launch traced here: 33.2 us
  starting transfers between devices  15.2 us (46%)
  Pallas kernels  8.75 us (26%)
  waiting for transfers between devices  7.17 us (22%)
  local copies, waits for them, and re-layouts  1.28 us (4%)
  between operations  0.79 us (2%)
    ppermute x6, starting transfers between devices, body(): got = [lax.ppermute(piece, ('cuts', 'group'), pairs) for piece in leaving]  7.22 us
    ppermute x3, starting transfers between devices, across(): return lax.ppermute(value, ('energy', 'group'), pairs)  4.96 us
    ppermute x6, waiting for transfers between devices, body(): got = [lax.ppermute(piece, ('cuts', 'group'), pairs) for piece in leaving]  4.01 us
    ppermute x3, waiting for transfers between devices, across(): return lax.ppermute(value, ('energy', 'group'), pairs)  3.09 us
    ppermute x3, starting transfers between devices, body(): lax.ppermute(edges[lower], ('cuts', 'group'), paired([lower], cuts, group...  3.01 us
    pallas_call x1, Pallas kernels, composites(): pl.pallas_call(composite_kernel, out_shape=(jax.ShapeDtypeStruct((count -...  2.62 us
    pallas_call x2, Pallas kernels, green_piece(): pl.pallas_call(functools.partial(green_kernel, step, start), out_shape=(j...  1.4 us
    unnamed x10, local copies, waits for them, and re-layouts  1.27 us
  transfers between devices with their start and end apart: 12, of which 8 were waited for; matrix products, arithmetic and copies ran while one was open for 0% of the time, Pallas kernels for 21%

profile of v6, /device:TPU:17, one launch (start us, length us, event | category | flops | bytes accessed | tf_op | source)
XLA Modules:
  0.0 33.2 jit_solution(17766454413549699325)
XLA Ops:
  0.7 0.7 %collective-permute-start.1 = (f32[72,512]{1,0:T(8,128)S(1)}, f32[72,512]{1,0:T(8,128)S(1)}, u32[]{:S(2)}, u32[]{:S(2)}) collective-permute-start(f32[72,512]{1,0:T(8,128)S(1)} %first_chain.1), channel_id=1, source_target_pairs={{0,8},{1,9},{2,10},{3,11},{8,0},{9,1},{10,2},{11,3},{16,17},{17,16... | collective-permute-start | bytes 442376 | tf_op jit(solution)/shard_map/ppermute | solution.py:440
  1.5 1.1 %copy-done = f32[1,3,512,512]{3,2,1,0:T(8,128)S(1)} copy-done((f32[1,3,512,512]{3,2,1,0:T(8,128)S(1)}, f32[1,3,512,512]{3,2,1,0:T(8,128)}, u32[]{:S(2)}) %copy-start) | copy-done | bytes 3145752
  2.7 2.6 %composites.1 = (f32[1,512,512]{2,1,0:T(8,128)S(1)}, f32[1,512,128]{2,1,0:T(8,128)S(1)}, bf16[512,512]{1,0:T(8,128)(2,1)S(1)}, bf16[512,512]{1,0:T(8,128)(2,1)S(...) custom-call(f32[3,512,512]{2,1,0:T(8,128)S(1)} %bitcast.9, f32[1536,128]{1,0:T(8,128)S(1)} %bitcast.12), custom_call_target="tpu_custom_call" | custom-call | flops 1610612736 | bytes 6291456 | tf_op jit(solution)/shard_map/composites/pallas_call | solution.py:132
  5.4 0.7 %collective-permute-start = (f32[56,512]{1,0:T(8,128)S(1)}, f32[56,512]{1,0:T(8,128)S(1)}, u32[]{:S(2)}, u32[]{:S(2)}) collective-permute-start(f32[56,512]{1,0:T(8,128)S(1)} %get-tuple-element.35.offset_ref), channel_id=1, source_target_pairs={{0,8},{1,9},{2,10},{3,11},{8,0},{9,1},{10,2},{11,3},{16,17},{17,16... | collective-permute-start | bytes 344072 | tf_op jit(solution)/shard_map/ppermute | solution.py:440
  6.4 0.5 %collective-permute-start.2 = (f32[72,512]{1,0:T(8,128)S(1)}, f32[72,512]{1,0:T(8,128)S(1)}, u32[]{:S(2)}, u32[]{:S(2)}) collective-permute-start(f32[72,512]{1,0:T(8,128)S(1)} %get-tuple-element.37._), channel_id=1, source_target_pairs={{0,1},{1,0},{2,3},{3,2},{8,16},{9,17},{10,18},{11,19},{16,8},{17,9... | collective-permute-start | bytes 442376 | tf_op jit(solution)/shard_map/ppermute | solution.py:440
  7.4 2.6 %collective-permute-start.4 = (f32[56,512]{1,0:T(8,128)S(1)}, f32[56,512]{1,0:T(8,128)S(1)}, u32[]{:S(2)}, u32[]{:S(2)}) collective-permute-start(f32[56,512]{1,0:T(8,128)S(1)} %get-tuple-element.38._), channel_id=1, source_target_pairs={{0,1},{1,0},{2,3},{3,2},{8,16},{9,17},{10,18},{11,19},{16,8},{17,9... | collective-permute-start | bytes 344072 | tf_op jit(solution)/shard_map/ppermute | solution.py:440
  10.0 0.8 %turned_blocks.1 = (bf16[512,1024]{1,0:T(8,128)(2,1)S(1)}, bf16[512,1024]{1,0:T(8,128)(2,1)S(1)}, f32[128,1024]{1,0:T(8,128)S(1)}, f32[2,512]{1,0:T(2,128)S(1)}) custom-call(f32[3,512,512]{2,1,0:T(8,128)S(1)} %bitcast.10, f32[1536,128]{1,0:T(8,128)S(1)} %bitcast.13, f32[1,512,512]{2,1,0:T(8,128)S(1)} %get-tuple-element.31.mats_ref, ...), custom_call_target="tpu_custom_call" | custom-call | tf_op jit(solution)/shard_map/turned_blocks/pallas_call | solution.py:178
  10.8 1.2 %collective-permute-done.2.got_ref = f32[72,512]{1,0:T(8,128)S(1)} collective-permute-done((f32[72,512]{1,0:T(8,128)S(1)}, f32[72,512]{1,0:T(8,128)S(1)}, u32[]{:S(2)}, u32[]{:S(2)}) %collective-permute-start.2) | collective-permute-done | bytes 147488 | tf_op jit(solution)/shard_map/ppermute | solution.py:440
  12.3 1.3 %collective-permute-start.3 = (f32[72,512]{1,0:T(8,128)S(1)}, f32[72,512]{1,0:T(8,128)S(1)}, u32[]{:S(2)}, u32[]{:S(2)}) collective-permute-start(f32[72,512]{1,0:T(8,128)S(1)} %get-tuple-element.44._), channel_id=1, source_target_pairs={{16,24},{17,25},{18,26},{19,27},{20,28},{21,29},{22,30},{23,31}} | collective-permute-start | bytes 442376 | tf_op jit(solution)/shard_map/ppermute | solution.py:440
  13.6 0.6 %collective-permute-done.4.got_ref = f32[56,512]{1,0:T(8,128)S(1)} collective-permute-done((f32[56,512]{1,0:T(8,128)S(1)}, f32[56,512]{1,0:T(8,128)S(1)}, u32[]{:S(2)}, u32[]{:S(2)}) %collective-permute-start.4) | collective-permute-done | bytes 114720 | tf_op jit(solution)/shard_map/ppermute | solution.py:440
  14.4 1.3 %collective-permute-start.5 = (f32[56,512]{1,0:T(8,128)S(1)}, f32[56,512]{1,0:T(8,128)S(1)}, u32[]{:S(2)}, u32[]{:S(2)}) collective-permute-start(f32[56,512]{1,0:T(8,128)S(1)} %get-tuple-element.48), channel_id=1, source_target_pairs={{16,24},{17,25},{18,26},{19,27},{20,28},{21,29},{22,30},{23,31}} | collective-permute-start | bytes 344072 | tf_op jit(solution)/shard_map/ppermute | solution.py:440
  15.8 0.7 %green_piece.2 = (f32[72,1536]{1,0:T(8,128)S(1)}, f32[4,512]{1,0:T(4,128)S(1)}) custom-call(bf16[512,1024]{1,0:T(8,128)(2,1)S(1)} %get-tuple-element.39.high_ref, bf16[512,1024]{1,0:T(8,128)(2,1)S(1)} %get-tuple-element.40.low_ref, f32[128,1024]{1,0:T(8,128)S(1)} %get-tuple-element.41.turned_ref, ...), custom_call_target="tpu_custom_call" | custom-call | tf_op jit(solution)/shard_map/green_piece/pallas_call | solution.py:239
  16.5 2.2 %collective-permute-done.5.got_ref = f32[56,512]{1,0:T(8,128)S(1)} collective-permute-done((f32[56,512]{1,0:T(8,128)S(1)}, f32[56,512]{1,0:T(8,128)S(1)}, u32[]{:S(2)}, u32[]{:S(2)}) %collective-permute-start.5) | collective-permute-done | bytes 114720 | tf_op jit(solution)/shard_map/ppermute | solution.py:440
  18.7 0.7 %green_piece.3 = (f32[56,1536]{1,0:T(8,128)S(1)}, f32[4,512]{1,0:T(4,128)S(1)}) custom-call(bf16[512,1024]{1,0:T(8,128)(2,1)S(1)} %get-tuple-element.39.high_ref, bf16[512,1024]{1,0:T(8,128)(2,1)S(1)} %get-tuple-element.40.low_ref, f32[128,1024]{1,0:T(8,128)S(1)} %get-tuple-element.41.turned_ref, ...), custom_call_target="tpu_custom_call" | custom-call | tf_op jit(solution)/shard_map/green_piece/pallas_call | solution.py:239
  19.3 2.3 %collective-permute-start.6 = (f32[4,512]{1,0:T(4,128)S(1)}, f32[4,512]{1,0:T(4,128)S(1)}, u32[]{:S(2)}, u32[]{:S(2)}) collective-permute-start(f32[4,512]{1,0:T(4,128)S(1)} %get-tuple-element.54), channel_id=1, source_target_pairs={{0,3},{1,2},{2,1},{3,0},{4,7},{5,6},{6,5},{7,4},{8,11},{9,10},{10,... | collective-permute-start | bytes 24584 | tf_op jit(solution)/shard_map/ppermute | solution.py:423
  21.7 1.3 %collective-permute-done.6 = f32[4,512]{1,0:T(4,128)S(1)} collective-permute-done((f32[4,512]{1,0:T(4,128)S(1)}, f32[4,512]{1,0:T(4,128)S(1)}, u32[]{:S(2)}, u32[]{:S(2)}) %collective-permute-start.6) | collective-permute-done | bytes 8224 | tf_op jit(solution)/shard_map/ppermute | solution.py:423
  23.0 1.8 %collective-permute-start.7 = (f32[4,512]{1,0:T(4,128)S(1)}, f32[4,512]{1,0:T(4,128)S(1)}, u32[]{:S(2)}, u32[]{:S(2)}) collective-permute-start(f32[4,512]{1,0:T(4,128)S(1)} %add.9), channel_id=1, source_target_pairs={{0,5},{1,4},{2,7},{3,6},{4,1},{5,0},{6,3},{7,2},{8,13},{9,12},{10,... | collective-permute-start | bytes 24584 | tf_op jit(solution)/shard_map/ppermute | solution.py:423
  24.8 1.3 %collective-permute-done.7 = f32[4,512]{1,0:T(4,128)S(1)} collective-permute-done((f32[4,512]{1,0:T(4,128)S(1)}, f32[4,512]{1,0:T(4,128)S(1)}, u32[]{:S(2)}, u32[]{:S(2)}) %collective-permute-start.7) | collective-permute-done | bytes 8224 | tf_op jit(solution)/shard_map/ppermute | solution.py:423
  26.1 0.8 %collective-permute-start.8 = (f32[4,512]{1,0:T(4,128)S(1)}, f32[4,512]{1,0:T(4,128)S(1)}, u32[]{:S(2)}, u32[]{:S(2)}) collective-permute-start(f32[4,512]{1,0:T(4,128)S(1)} %multiply_add_fusion), channel_id=1, source_target_pairs={{0,1},{1,0},{2,3},{3,2},{4,5},{5,4},{6,7},{7,6},{8,9},{9,8},{10,11... | collective-permute-start | bytes 24584 | tf_op jit(solution)/shard_map/ppermute | solution.py:423
  27.4 0.4 %collective-permute-done.8 = f32[4,512]{1,0:T(4,128)S(1)} collective-permute-done((f32[4,512]{1,0:T(4,128)S(1)}, f32[4,512]{1,0:T(4,128)S(1)}, u32[]{:S(2)}, u32[]{:S(2)}) %collective-permute-start.8) | collective-permute-done | bytes 8224 | tf_op jit(solution)/shard_map/ppermute | solution.py:423
  27.8 0.4 %collective-permute-start.9 = (f32[12,512]{1,0:T(8,128)S(1)}, f32[12,512]{1,0:T(8,128)S(1)}, u32[]{:S(2)}, u32[]{:S(2)}) collective-permute-start(f32[12,512]{1,0:T(8,128)S(1)} %get-tuple-element.57), channel_id=1, source_target_pairs={{0,9},{1,8},{2,11},{3,10},{8,1},{9,0},{10,3},{11,2},{16,17},{17,16... | collective-permute-start | bytes 73736 | tf_op jit(solution)/shard_map/ppermute | solution.py:469
  28.2 2.6 %collective-permute-start.11 = (f32[4,512]{1,0:T(4,128)S(1)}, f32[4,512]{1,0:T(4,128)S(1)}, u32[]{:S(2)}, u32[]{:S(2)}) collective-permute-start(f32[4,512]{1,0:T(4,128)S(1)} %get-tuple-element.59), channel_id=1, source_target_pairs={{0,1},{1,0},{2,3},{3,2},{8,9},{9,8},{10,11},{11,10},{16,25},{17,24... | collective-permute-start | bytes 24584 | tf_op jit(solution)/shard_map/ppermute | solution.py:469
  30.8 1.3 %early_blocks.1 = (f32[1536,128]{1,0:T(8,128)}, f32[1536,128]{1,0:T(8,128)}) custom-call(bf16[512,512]{1,0:T(8,128)(2,1)S(1)} %copy-done.1, f32[128,1536]{1,0:T(8,128)S(1)} %get-tuple-element.52.inner_ref._, f32[1536,128]{1,0:T(8,128)S(1)} %get-tuple-element.53.green_ref, f32[4,512]{1,0:T(4,128)S(1)} %add.11.mixed_ref), custom_call_target="tpu_custom_call" | custom-call | tf_op jit(solution)/shard_map/early_blocks/pallas_call | solution.py:332
  32.2 1.0 %late_blocks.1 = f32[1536,128]{1,0:T(8,128)} custom-call(bf16[512,512]{1,0:T(8,128)(2,1)S(1)} %copy-done.1, f32[128,1536]{1,0:T(8,128)S(1)} %get-tuple-element.52.inner_ref._, f32[4,512]{1,0:T(4,128)S(1)} %add.11.mixed_ref, f32[1536,128]{1,0:T(8,128)} %get-tuple-element.56._, ...), custom_call_target="tpu_custom_call", output_to_operand_aliasing={{}: (3, {})} | custom-call | tf_op jit(solution)/shard_map/late_blocks/pallas_call | solution.py:367
  (27 shorter events, 2.1 us)
Async XLA Ops:
  0.6 1.9 %copy-start = (f32[1,3,512,512]{3,2,1,0:T(8,128)S(1)}, f32[1,3,512,512]{3,2,1,0:T(8,128)}, u32[]{:S(2)}) copy-start(f32[1,3,512,512]{3,2,1,0:T(8,128)} %param.5) | copy-start | bytes 9437188
  0.6 2.1 %copy-start.2 = (f32[1,1536,128]{2,1,0:T(8,128)S(1)}, f32[1,1536,128]{2,1,0:T(8,128)}, u32[]{:S(2)}) copy-start(f32[1,1536,128]{2,1,0:T(8,128)} %param.6) | copy-start | bytes 2359300
  0.7 5.4 %collective-permute-start.1 = (f32[72,512]{1,0:T(8,128)S(1)}, f32[72,512]{1,0:T(8,128)S(1)}, u32[]{:S(2)}, u32[]{:S(2)}) collective-permute-start(f32[72,512]{1,0:T(8,128)S(1)} %first_chain.1), channel_id=1, source_target_pairs={{0,8},{1,9},{2,10},{3,11},{8,0},{9,1},{10,2},{11,3},{16,17},{17,16... | collective-permute-start | bytes 442376 | tf_op jit(solution)/shard_map/ppermute | solution.py:440
  5.3 4.6 %copy-start.3 = (f32[8]{0:T(128)S(1)}, f32[8]{0:T(128)}, u32[]{:S(2)}) copy-start(f32[8]{0:T(128)} %param.8) | copy-start | bytes 100
  5.4 4.6 %copy-start.4 = (s32[8]{0:T(128)S(1)}, s32[8]{0:T(128)}, u32[]{:S(2)}) copy-start(s32[8]{0:T(128)} %param.9) | copy-start | bytes 100
  5.4 1.7 %collective-permute-start = (f32[56,512]{1,0:T(8,128)S(1)}, f32[56,512]{1,0:T(8,128)S(1)}, u32[]{:S(2)}, u32[]{:S(2)}) collective-permute-start(f32[56,512]{1,0:T(8,128)S(1)} %get-tuple-element.35.offset_ref), channel_id=1, source_target_pairs={{0,8},{1,9},{2,10},{3,11},{8,0},{9,1},{10,2},{11,3},{16,17},{17,16... | collective-permute-start | bytes 344072 | tf_op jit(solution)/shard_map/ppermute | solution.py:440
  6.4 5.5 %collective-permute-start.2 = (f32[72,512]{1,0:T(8,128)S(1)}, f32[72,512]{1,0:T(8,128)S(1)}, u32[]{:S(2)}, u32[]{:S(2)}) collective-permute-start(f32[72,512]{1,0:T(8,128)S(1)} %get-tuple-element.37._), channel_id=1, source_target_pairs={{0,1},{1,0},{2,3},{3,2},{8,16},{9,17},{10,18},{11,19},{16,8},{17,9... | collective-permute-start | bytes 442376 | tf_op jit(solution)/shard_map/ppermute | solution.py:440
  7.4 6.8 %collective-permute-start.4 = (f32[56,512]{1,0:T(8,128)S(1)}, f32[56,512]{1,0:T(8,128)S(1)}, u32[]{:S(2)}, u32[]{:S(2)}) collective-permute-start(f32[56,512]{1,0:T(8,128)S(1)} %get-tuple-element.38._), channel_id=1, source_target_pairs={{0,1},{1,0},{2,3},{3,2},{8,16},{9,17},{10,18},{11,19},{16,8},{17,9... | collective-permute-start | bytes 344072 | tf_op jit(solution)/shard_map/ppermute | solution.py:440
  12.3 3.5 %collective-permute-start.3 = (f32[72,512]{1,0:T(8,128)S(1)}, f32[72,512]{1,0:T(8,128)S(1)}, u32[]{:S(2)}, u32[]{:S(2)}) collective-permute-start(f32[72,512]{1,0:T(8,128)S(1)} %get-tuple-element.44._), channel_id=1, source_target_pairs={{16,24},{17,25},{18,26},{19,27},{20,28},{21,29},{22,30},{23,31}} | collective-permute-start | bytes 442376 | tf_op jit(solution)/shard_map/ppermute | solution.py:440
  14.4 4.2 %collective-permute-start.5 = (f32[56,512]{1,0:T(8,128)S(1)}, f32[56,512]{1,0:T(8,128)S(1)}, u32[]{:S(2)}, u32[]{:S(2)}) collective-permute-start(f32[56,512]{1,0:T(8,128)S(1)} %get-tuple-element.48), channel_id=1, source_target_pairs={{16,24},{17,25},{18,26},{19,27},{20,28},{21,29},{22,30},{23,31}} | collective-permute-start | bytes 344072 | tf_op jit(solution)/shard_map/ppermute | solution.py:440
  15.8 11.2 %copy-start.1 = (bf16[512,512]{1,0:T(8,128)(2,1)S(1)}, bf16[512,512]{1,0:T(8,128)(2,1)}, u32[]{:S(2)}) copy-start(bf16[512,512]{1,0:T(8,128)(2,1)} %coupling_ref.5) | copy-start | bytes 1572868
  19.3 3.7 %collective-permute-start.6 = (f32[4,512]{1,0:T(4,128)S(1)}, f32[4,512]{1,0:T(4,128)S(1)}, u32[]{:S(2)}, u32[]{:S(2)}) collective-permute-start(f32[4,512]{1,0:T(4,128)S(1)} %get-tuple-element.54), channel_id=1, source_target_pairs={{0,3},{1,2},{2,1},{3,0},{4,7},{5,6},{6,5},{7,4},{8,11},{9,10},{10,... | collective-permute-start | bytes 24584 | tf_op jit(solution)/shard_map/ppermute | solution.py:423
  23.0 3.1 %collective-permute-start.7 = (f32[4,512]{1,0:T(4,128)S(1)}, f32[4,512]{1,0:T(4,128)S(1)}, u32[]{:S(2)}, u32[]{:S(2)}) collective-permute-start(f32[4,512]{1,0:T(4,128)S(1)} %add.9), channel_id=1, source_target_pairs={{0,5},{1,4},{2,7},{3,6},{4,1},{5,0},{6,3},{7,2},{8,13},{9,12},{10,... | collective-permute-start | bytes 24584 | tf_op jit(solution)/shard_map/ppermute | solution.py:423
  26.1 1.7 %collective-permute-start.8 = (f32[4,512]{1,0:T(4,128)S(1)}, f32[4,512]{1,0:T(4,128)S(1)}, u32[]{:S(2)}, u32[]{:S(2)}) collective-permute-start(f32[4,512]{1,0:T(4,128)S(1)} %multiply_add_fusion), channel_id=1, source_target_pairs={{0,1},{1,0},{2,3},{3,2},{4,5},{5,4},{6,7},{7,6},{8,9},{9,8},{10,11... | collective-permute-start | bytes 24584 | tf_op jit(solution)/shard_map/ppermute | solution.py:423
  27.8 4.3 %collective-permute-start.9 = (f32[12,512]{1,0:T(8,128)S(1)}, f32[12,512]{1,0:T(8,128)S(1)}, u32[]{:S(2)}, u32[]{:S(2)}) collective-permute-start(f32[12,512]{1,0:T(8,128)S(1)} %get-tuple-element.57), channel_id=1, source_target_pairs={{0,9},{1,8},{2,11},{3,10},{8,1},{9,0},{10,3},{11,2},{16,17},{17,16... | collective-permute-start | bytes 73736 | tf_op jit(solution)/shard_map/ppermute | solution.py:469
  28.2 3.9 %collective-permute-start.10 = (f32[8,512]{1,0:T(8,128)S(1)}, f32[8,512]{1,0:T(8,128)S(1)}, u32[]{:S(2)}, u32[]{:S(2)}) collective-permute-start(f32[8,512]{1,0:T(8,128)S(1)} %get-tuple-element.58), channel_id=1, source_target_pairs={{0,1},{1,0},{2,3},{3,2},{8,17},{9,16},{10,19},{11,18},{16,9},{17,8... | collective-permute-start | bytes 49160 | tf_op jit(solution)/shard_map/ppermute | solution.py:469
  28.2 3.9 %collective-permute-start.11 = (f32[4,512]{1,0:T(4,128)S(1)}, f32[4,512]{1,0:T(4,128)S(1)}, u32[]{:S(2)}, u32[]{:S(2)}) collective-permute-start(f32[4,512]{1,0:T(4,128)S(1)} %get-tuple-element.59), channel_id=1, source_target_pairs={{0,1},{1,0},{2,3},{3,2},{8,9},{9,8},{10,11},{11,10},{16,25},{17,24... | collective-permute-start | bytes 24584 | tf_op jit(solution)/shard_map/ppermute | solution.py:469

commit v7 on v6

--- a/solution.py
+++ b/solution.py
@@ -13,7 +13,7 @@
 HBM = pl.BlockSpec(memory_space=pltpu.HBM)
 PARAMS = pltpu.CompilerParams(vmem_limit_bytes=32 * 1024 * 1024)
 WHOLE = pltpu.CompilerParams(vmem_limit_bytes=107 * 512 * 1024)
-SHARES = (9, 7)
+SHARES = (1, 1)
 
 
 def split(value):

time: 33.3 us -> 33.3 us (level)
  transfers between devices with their start and end apart: 12 -> 12, of which waited for: 8 -> 9; matrix products, arithmetic and copies ran while one was open for 0% -> 0% of each run, Pallas kernels for 21% -> 21%
where the time goes in v7:
time: 33.3 us; the launch traced here: 32.9 us
  starting transfers between devices  15.3 us (46%)
  Pallas kernels  8.65 us (26%)
  waiting for transfers between devices  6.98 us (21%)
  local copies, waits for them, and re-layouts  1.25 us (4%)
  between operations  0.77 us (2%)
    ppermute x6, starting transfers between devices, body(): got = [lax.ppermute(piece, ('cuts', 'group'), pairs) for piece in leaving]  7.24 us
    ppermute x3, starting transfers between devices, across(): return lax.ppermute(value, ('energy', 'group'), pairs)  5.01 us
    ppermute x6, waiting for transfers between devices, body(): got = [lax.ppermute(piece, ('cuts', 'group'), pairs) for piece in leaving]  3.78 us
    ppermute x3, waiting for transfers between devices, across(): return lax.ppermute(value, ('energy', 'group'), pairs)  3.14 us
    ppermute x3, starting transfers between devices, body(): lax.ppermute(edges[lower], ('cuts', 'group'), paired([lower], cuts, group...  3.01 us
    pallas_call x1, Pallas kernels, composites(): pl.pallas_call(composite_kernel, out_shape=(jax.ShapeDtypeStruct((count -...  2.62 us
    pallas_call x2, Pallas kernels, green_piece(): pl.pallas_call(functools.partial(green_kernel, step, start), out_shape=(j...  1.32 us
    pallas_call x1, Pallas kernels, early_blocks(): pl.pallas_call(early_kernel, out_shape=(shape, shape), in_specs=[VMEM] *...  1.27 us
  transfers between devices with their start and end apart: 12, of which 9 were waited for; matrix products, arithmetic and copies ran while one was open for 0% of the time, Pallas kernels for 21%

profile of v7, /device:TPU:17, one launch (start us, length us, event | category | flops | bytes accessed | tf_op | source)
XLA Modules:
  0.0 32.9 jit_solution(16383164024270854717)
XLA Ops:
  0.7 0.7 %collective-permute-start.1 = (f32[64,512]{1,0:T(8,128)S(1)}, f32[64,512]{1,0:T(8,128)S(1)}, u32[]{:S(2)}, u32[]{:S(2)}) collective-permute-start(f32[64,512]{1,0:T(8,128)S(1)} %first_chain.1), channel_id=1, source_target_pairs={{0,8},{1,9},{2,10},{3,11},{8,0},{9,1},{10,2},{11,3},{16,17},{17,16... | collective-permute-start | bytes 393224 | tf_op jit(solution)/shard_map/ppermute | solution.py:440
  1.5 1.0 %copy-done = f32[1,3,512,512]{3,2,1,0:T(8,128)S(1)} copy-done((f32[1,3,512,512]{3,2,1,0:T(8,128)S(1)}, f32[1,3,512,512]{3,2,1,0:T(8,128)}, u32[]{:S(2)}) %copy-start) | copy-done | bytes 3145752
  2.7 2.6 %composites.1 = (f32[1,512,512]{2,1,0:T(8,128)S(1)}, f32[1,512,128]{2,1,0:T(8,128)S(1)}, bf16[512,512]{1,0:T(8,128)(2,1)S(1)}, bf16[512,512]{1,0:T(8,128)(2,1)S(...) custom-call(f32[3,512,512]{2,1,0:T(8,128)S(1)} %bitcast.9, f32[1536,128]{1,0:T(8,128)S(1)} %bitcast.12), custom_call_target="tpu_custom_call" | custom-call | flops 1610612736 | bytes 6291456 | tf_op jit(solution)/shard_map/composites/pallas_call | solution.py:132
  5.3 0.7 %collective-permute-start = (f32[64,512]{1,0:T(8,128)S(1)}, f32[64,512]{1,0:T(8,128)S(1)}, u32[]{:S(2)}, u32[]{:S(2)}) collective-permute-start(f32[64,512]{1,0:T(8,128)S(1)} %get-tuple-element.35.offset_ref), channel_id=1, source_target_pairs={{0,8},{1,9},{2,10},{3,11},{8,0},{9,1},{10,2},{11,3},{16,17},{17,16... | collective-permute-start | bytes 393224 | tf_op jit(solution)/shard_map/ppermute | solution.py:440
  6.6 0.4 %collective-permute-done.got_ref = f32[64,512]{1,0:T(8,128)S(1)} collective-permute-done((f32[64,512]{1,0:T(8,128)S(1)}, f32[64,512]{1,0:T(8,128)S(1)}, u32[]{:S(2)}, u32[]{:S(2)}) %collective-permute-start) | collective-permute-done | bytes 131104 | tf_op jit(solution)/shard_map/ppermute | solution.py:440
  7.4 2.9 %collective-permute-start.4 = (f32[64,512]{1,0:T(8,128)S(1)}, f32[64,512]{1,0:T(8,128)S(1)}, u32[]{:S(2)}, u32[]{:S(2)}) collective-permute-start(f32[64,512]{1,0:T(8,128)S(1)} %get-tuple-element.38._), channel_id=1, source_target_pairs={{0,1},{1,0},{2,3},{3,2},{8,16},{9,17},{10,18},{11,19},{16,8},{17,9... | collective-permute-start | bytes 393224 | tf_op jit(solution)/shard_map/ppermute | solution.py:440
  10.3 0.8 %turned_blocks.1 = (bf16[512,1024]{1,0:T(8,128)(2,1)S(1)}, bf16[512,1024]{1,0:T(8,128)(2,1)S(1)}, f32[128,1024]{1,0:T(8,128)S(1)}, f32[2,512]{1,0:T(2,128)S(1)}) custom-call(f32[3,512,512]{2,1,0:T(8,128)S(1)} %bitcast.10, f32[1536,128]{1,0:T(8,128)S(1)} %bitcast.13, f32[1,512,512]{2,1,0:T(8,128)S(1)} %get-tuple-element.31.mats_ref, ...), custom_call_target="tpu_custom_call" | custom-call | tf_op jit(solution)/shard_map/turned_blocks/pallas_call | solution.py:178
  11.1 0.5 %collective-permute-done.2.got_ref = f32[64,512]{1,0:T(8,128)S(1)} collective-permute-done((f32[64,512]{1,0:T(8,128)S(1)}, f32[64,512]{1,0:T(8,128)S(1)}, u32[]{:S(2)}, u32[]{:S(2)}) %collective-permute-start.2) | collective-permute-done | bytes 131104 | tf_op jit(solution)/shard_map/ppermute | solution.py:440
  11.9 1.3 %collective-permute-start.3 = (f32[64,512]{1,0:T(8,128)S(1)}, f32[64,512]{1,0:T(8,128)S(1)}, u32[]{:S(2)}, u32[]{:S(2)}) collective-permute-start(f32[64,512]{1,0:T(8,128)S(1)} %get-tuple-element.44._), channel_id=1, source_target_pairs={{16,24},{17,25},{18,26},{19,27},{20,28},{21,29},{22,30},{23,31}} | collective-permute-start | bytes 393224 | tf_op jit(solution)/shard_map/ppermute | solution.py:440
  13.7 1.3 %collective-permute-start.5 = (f32[64,512]{1,0:T(8,128)S(1)}, f32[64,512]{1,0:T(8,128)S(1)}, u32[]{:S(2)}, u32[]{:S(2)}) collective-permute-start(f32[64,512]{1,0:T(8,128)S(1)} %get-tuple-element.48), channel_id=1, source_target_pairs={{16,24},{17,25},{18,26},{19,27},{20,28},{21,29},{22,30},{23,31}} | collective-permute-start | bytes 393224 | tf_op jit(solution)/shard_map/ppermute | solution.py:440
  15.1 0.7 %green_piece.2 = (f32[64,1536]{1,0:T(8,128)S(1)}, f32[4,512]{1,0:T(4,128)S(1)}) custom-call(bf16[512,1024]{1,0:T(8,128)(2,1)S(1)} %get-tuple-element.39.high_ref, bf16[512,1024]{1,0:T(8,128)(2,1)S(1)} %get-tuple-element.40.low_ref, f32[128,1024]{1,0:T(8,128)S(1)} %get-tuple-element.41.turned_ref, ...), custom_call_target="tpu_custom_call" | custom-call | tf_op jit(solution)/shard_map/green_piece/pallas_call | solution.py:239
  15.8 2.5 %collective-permute-done.5.got_ref = f32[64,512]{1,0:T(8,128)S(1)} collective-permute-done((f32[64,512]{1,0:T(8,128)S(1)}, f32[64,512]{1,0:T(8,128)S(1)}, u32[]{:S(2)}, u32[]{:S(2)}) %collective-permute-start.5) | collective-permute-done | bytes 131104 | tf_op jit(solution)/shard_map/ppermute | solution.py:440
  18.3 0.7 %green_piece.3 = (f32[64,1536]{1,0:T(8,128)S(1)}, f32[4,512]{1,0:T(4,128)S(1)}) custom-call(bf16[512,1024]{1,0:T(8,128)(2,1)S(1)} %get-tuple-element.39.high_ref, bf16[512,1024]{1,0:T(8,128)(2,1)S(1)} %get-tuple-element.40.low_ref, f32[128,1024]{1,0:T(8,128)S(1)} %get-tuple-element.41.turned_ref, ...), custom_call_target="tpu_custom_call" | custom-call | tf_op jit(solution)/shard_map/green_piece/pallas_call | solution.py:239
  19.0 2.9 %collective-permute-start.6 = (f32[4,512]{1,0:T(4,128)S(1)}, f32[4,512]{1,0:T(4,128)S(1)}, u32[]{:S(2)}, u32[]{:S(2)}) collective-permute-start(f32[4,512]{1,0:T(4,128)S(1)} %get-tuple-element.54), channel_id=1, source_target_pairs={{0,3},{1,2},{2,1},{3,0},{4,7},{5,6},{6,5},{7,4},{8,11},{9,10},{10,... | collective-permute-start | bytes 24584 | tf_op jit(solution)/shard_map/ppermute | solution.py:423
  21.9 1.4 %collective-permute-done.6 = f32[4,512]{1,0:T(4,128)S(1)} collective-permute-done((f32[4,512]{1,0:T(4,128)S(1)}, f32[4,512]{1,0:T(4,128)S(1)}, u32[]{:S(2)}, u32[]{:S(2)}) %collective-permute-start.6) | collective-permute-done | bytes 8224 | tf_op jit(solution)/shard_map/ppermute | solution.py:423
  23.2 1.8 %collective-permute-start.7 = (f32[4,512]{1,0:T(4,128)S(1)}, f32[4,512]{1,0:T(4,128)S(1)}, u32[]{:S(2)}, u32[]{:S(2)}) collective-permute-start(f32[4,512]{1,0:T(4,128)S(1)} %add.9), channel_id=1, source_target_pairs={{0,5},{1,4},{2,7},{3,6},{4,1},{5,0},{6,3},{7,2},{8,13},{9,12},{10,... | collective-permute-start | bytes 24584 | tf_op jit(solution)/shard_map/ppermute | solution.py:423
  25.0 1.3 %collective-permute-done.7 = f32[4,512]{1,0:T(4,128)S(1)} collective-permute-done((f32[4,512]{1,0:T(4,128)S(1)}, f32[4,512]{1,0:T(4,128)S(1)}, u32[]{:S(2)}, u32[]{:S(2)}) %collective-permute-start.7) | collective-permute-done | bytes 8224 | tf_op jit(solution)/shard_map/ppermute | solution.py:423
  26.4 0.3 %collective-permute-start.8 = (f32[4,512]{1,0:T(4,128)S(1)}, f32[4,512]{1,0:T(4,128)S(1)}, u32[]{:S(2)}, u32[]{:S(2)}) collective-permute-start(f32[4,512]{1,0:T(4,128)S(1)} %multiply_add_fusion), channel_id=1, source_target_pairs={{0,1},{1,0},{2,3},{3,2},{4,5},{5,4},{6,7},{7,6},{8,9},{9,8},{10,11... | collective-permute-start | bytes 24584 | tf_op jit(solution)/shard_map/ppermute | solution.py:423
  26.7 0.4 %inner_blocks.1 = (f32[128,1536]{1,0:T(8,128)S(1)}, f32[1536,128]{1,0:T(8,128)S(1)}) custom-call(bf16[512,512]{1,0:T(8,128)(2,1)S(1)} %copy-done.1, f32[64,1536]{1,0:T(8,128)S(1)} %get-tuple-element.46.rest_0_, f32[64,1536]{1,0:T(8,128)S(1)} %get-tuple-element.51.rest_1_), custom_call_target="tpu_custom_call" | custom-call | flops 201326592 | bytes 2359296 | tf_op jit(solution)/shard_map/inner_blocks/pallas_call | solution.py:267
  27.1 0.4 %collective-permute-done.8 = f32[4,512]{1,0:T(4,128)S(1)} collective-permute-done((f32[4,512]{1,0:T(4,128)S(1)}, f32[4,512]{1,0:T(4,128)S(1)}, u32[]{:S(2)}, u32[]{:S(2)}) %collective-permute-start.8) | collective-permute-done | bytes 8224 | tf_op jit(solution)/shard_map/ppermute | solution.py:423
  27.6 0.4 %collective-permute-start.9 = (f32[12,512]{1,0:T(8,128)S(1)}, f32[12,512]{1,0:T(8,128)S(1)}, u32[]{:S(2)}, u32[]{:S(2)}) collective-permute-start(f32[12,512]{1,0:T(8,128)S(1)} %get-tuple-element.57), channel_id=1, source_target_pairs={{0,9},{1,8},{2,11},{3,10},{8,1},{9,0},{10,3},{11,2},{16,17},{17,16... | collective-permute-start | bytes 73736 | tf_op jit(solution)/shard_map/ppermute | solution.py:469
  28.0 2.6 %collective-permute-start.11 = (f32[4,512]{1,0:T(4,128)S(1)}, f32[4,512]{1,0:T(4,128)S(1)}, u32[]{:S(2)}, u32[]{:S(2)}) collective-permute-start(f32[4,512]{1,0:T(4,128)S(1)} %get-tuple-element.59), channel_id=1, source_target_pairs={{0,1},{1,0},{2,3},{3,2},{8,9},{9,8},{10,11},{11,10},{16,25},{17,24... | collective-permute-start | bytes 24584 | tf_op jit(solution)/shard_map/ppermute | solution.py:469
  30.6 1.3 %early_blocks.1 = (f32[1536,128]{1,0:T(8,128)}, f32[1536,128]{1,0:T(8,128)}) custom-call(bf16[512,512]{1,0:T(8,128)(2,1)S(1)} %copy-done.1, f32[128,1536]{1,0:T(8,128)S(1)} %get-tuple-element.52.inner_ref._, f32[1536,128]{1,0:T(8,128)S(1)} %get-tuple-element.53.green_ref, f32[4,512]{1,0:T(4,128)S(1)} %add.11.mixed_ref), custom_call_target="tpu_custom_call" | custom-call | tf_op jit(solution)/shard_map/early_blocks/pallas_call | solution.py:332
  31.9 1.0 %late_blocks.1 = f32[1536,128]{1,0:T(8,128)} custom-call(bf16[512,512]{1,0:T(8,128)(2,1)S(1)} %copy-done.1, f32[128,1536]{1,0:T(8,128)S(1)} %get-tuple-element.52.inner_ref._, f32[4,512]{1,0:T(4,128)S(1)} %add.11.mixed_ref, f32[1536,128]{1,0:T(8,128)} %get-tuple-element.56._, ...), custom_call_target="tpu_custom_call", output_to_operand_aliasing={{}: (3, {})} | custom-call | tf_op jit(solution)/shard_map/late_blocks/pallas_call | solution.py:367
  (27 shorter events, 2.1 us)
Async XLA Ops:
  0.6 1.9 %copy-start = (f32[1,3,512,512]{3,2,1,0:T(8,128)S(1)}, f32[1,3,512,512]{3,2,1,0:T(8,128)}, u32[]{:S(2)}) copy-start(f32[1,3,512,512]{3,2,1,0:T(8,128)} %param.5) | copy-start | bytes 9437188
  0.6 2.1 %copy-start.2 = (f32[1,1536,128]{2,1,0:T(8,128)S(1)}, f32[1,1536,128]{2,1,0:T(8,128)}, u32[]{:S(2)}) copy-start(f32[1,1536,128]{2,1,0:T(8,128)} %param.6) | copy-start | bytes 2359300
  0.7 9.6 %copy-start.3 = (f32[8]{0:T(128)S(1)}, f32[8]{0:T(128)}, u32[]{:S(2)}) copy-start(f32[8]{0:T(128)} %param.8) | copy-start | bytes 100
  0.7 9.6 %copy-start.4 = (s32[8]{0:T(128)S(1)}, s32[8]{0:T(128)}, u32[]{:S(2)}) copy-start(s32[8]{0:T(128)} %param.9) | copy-start | bytes 100
  0.7 5.3 %collective-permute-start.1 = (f32[64,512]{1,0:T(8,128)S(1)}, f32[64,512]{1,0:T(8,128)S(1)}, u32[]{:S(2)}, u32[]{:S(2)}) collective-permute-start(f32[64,512]{1,0:T(8,128)S(1)} %first_chain.1), channel_id=1, source_target_pairs={{0,8},{1,9},{2,10},{3,11},{8,0},{9,1},{10,2},{11,3},{16,17},{17,16... | collective-permute-start | bytes 393224 | tf_op jit(solution)/shard_map/ppermute | solution.py:440
  5.3 1.7 %collective-permute-start = (f32[64,512]{1,0:T(8,128)S(1)}, f32[64,512]{1,0:T(8,128)S(1)}, u32[]{:S(2)}, u32[]{:S(2)}) collective-permute-start(f32[64,512]{1,0:T(8,128)S(1)} %get-tuple-element.35.offset_ref), channel_id=1, source_target_pairs={{0,8},{1,9},{2,10},{3,11},{8,0},{9,1},{10,2},{11,3},{16,17},{17,16... | collective-permute-start | bytes 393224 | tf_op jit(solution)/shard_map/ppermute | solution.py:440
  6.4 5.2 %collective-permute-start.2 = (f32[64,512]{1,0:T(8,128)S(1)}, f32[64,512]{1,0:T(8,128)S(1)}, u32[]{:S(2)}, u32[]{:S(2)}) collective-permute-start(f32[64,512]{1,0:T(8,128)S(1)} %get-tuple-element.37._), channel_id=1, source_target_pairs={{0,1},{1,0},{2,3},{3,2},{8,16},{9,17},{10,18},{11,19},{16,8},{17,9... | collective-permute-start | bytes 393224 | tf_op jit(solution)/shard_map/ppermute | solution.py:440
  7.4 6.0 %collective-permute-start.4 = (f32[64,512]{1,0:T(8,128)S(1)}, f32[64,512]{1,0:T(8,128)S(1)}, u32[]{:S(2)}, u32[]{:S(2)}) collective-permute-start(f32[64,512]{1,0:T(8,128)S(1)} %get-tuple-element.38._), channel_id=1, source_target_pairs={{0,1},{1,0},{2,3},{3,2},{8,16},{9,17},{10,18},{11,19},{16,8},{17,9... | collective-permute-start | bytes 393224 | tf_op jit(solution)/shard_map/ppermute | solution.py:440
  11.9 3.2 %collective-permute-start.3 = (f32[64,512]{1,0:T(8,128)S(1)}, f32[64,512]{1,0:T(8,128)S(1)}, u32[]{:S(2)}, u32[]{:S(2)}) collective-permute-start(f32[64,512]{1,0:T(8,128)S(1)} %get-tuple-element.44._), channel_id=1, source_target_pairs={{16,24},{17,25},{18,26},{19,27},{20,28},{21,29},{22,30},{23,31}} | collective-permute-start | bytes 393224 | tf_op jit(solution)/shard_map/ppermute | solution.py:440
  13.7 4.6 %collective-permute-start.5 = (f32[64,512]{1,0:T(8,128)S(1)}, f32[64,512]{1,0:T(8,128)S(1)}, u32[]{:S(2)}, u32[]{:S(2)}) collective-permute-start(f32[64,512]{1,0:T(8,128)S(1)} %get-tuple-element.48), channel_id=1, source_target_pairs={{16,24},{17,25},{18,26},{19,27},{20,28},{21,29},{22,30},{23,31}} | collective-permute-start | bytes 393224 | tf_op jit(solution)/shard_map/ppermute | solution.py:440
  15.1 11.6 %copy-start.1 = (bf16[512,512]{1,0:T(8,128)(2,1)S(1)}, bf16[512,512]{1,0:T(8,128)(2,1)}, u32[]{:S(2)}) copy-start(bf16[512,512]{1,0:T(8,128)(2,1)} %coupling_ref.5) | copy-start | bytes 1572868
  19.0 4.2 %collective-permute-start.6 = (f32[4,512]{1,0:T(4,128)S(1)}, f32[4,512]{1,0:T(4,128)S(1)}, u32[]{:S(2)}, u32[]{:S(2)}) collective-permute-start(f32[4,512]{1,0:T(4,128)S(1)} %get-tuple-element.54), channel_id=1, source_target_pairs={{0,3},{1,2},{2,1},{3,0},{4,7},{5,6},{6,5},{7,4},{8,11},{9,10},{10,... | collective-permute-start | bytes 24584 | tf_op jit(solution)/shard_map/ppermute | solution.py:423
  23.2 3.1 %collective-permute-start.7 = (f32[4,512]{1,0:T(4,128)S(1)}, f32[4,512]{1,0:T(4,128)S(1)}, u32[]{:S(2)}, u32[]{:S(2)}) collective-permute-start(f32[4,512]{1,0:T(4,128)S(1)} %add.9), channel_id=1, source_target_pairs={{0,5},{1,4},{2,7},{3,6},{4,1},{5,0},{6,3},{7,2},{8,13},{9,12},{10,... | collective-permute-start | bytes 24584 | tf_op jit(solution)/shard_map/ppermute | solution.py:423
  26.4 1.2 %collective-permute-start.8 = (f32[4,512]{1,0:T(4,128)S(1)}, f32[4,512]{1,0:T(4,128)S(1)}, u32[]{:S(2)}, u32[]{:S(2)}) collective-permute-start(f32[4,512]{1,0:T(4,128)S(1)} %multiply_add_fusion), channel_id=1, source_target_pairs={{0,1},{1,0},{2,3},{3,2},{4,5},{5,4},{6,7},{7,6},{8,9},{9,8},{10,11... | collective-permute-start | bytes 24584 | tf_op jit(solution)/shard_map/ppermute | solution.py:423
  27.6 4.3 %collective-permute-start.9 = (f32[12,512]{1,0:T(8,128)S(1)}, f32[12,512]{1,0:T(8,128)S(1)}, u32[]{:S(2)}, u32[]{:S(2)}) collective-permute-start(f32[12,512]{1,0:T(8,128)S(1)} %get-tuple-element.57), channel_id=1, source_target_pairs={{0,9},{1,8},{2,11},{3,10},{8,1},{9,0},{10,3},{11,2},{16,17},{17,16... | collective-permute-start | bytes 73736 | tf_op jit(solution)/shard_map/ppermute | solution.py:469
  28.0 3.9 %collective-permute-start.10 = (f32[8,512]{1,0:T(8,128)S(1)}, f32[8,512]{1,0:T(8,128)S(1)}, u32[]{:S(2)}, u32[]{:S(2)}) collective-permute-start(f32[8,512]{1,0:T(8,128)S(1)} %get-tuple-element.58), channel_id=1, source_target_pairs={{0,1},{1,0},{2,3},{3,2},{8,17},{9,16},{10,19},{11,18},{16,9},{17,8... | collective-permute-start | bytes 49160 | tf_op jit(solution)/shard_map/ppermute | solution.py:469
  28.0 3.9 %collective-permute-start.11 = (f32[4,512]{1,0:T(4,128)S(1)}, f32[4,512]{1,0:T(4,128)S(1)}, u32[]{:S(2)}, u32[]{:S(2)}) collective-permute-start(f32[4,512]{1,0:T(4,128)S(1)} %get-tuple-element.59), channel_id=1, source_target_pairs={{0,1},{1,0},{2,3},{3,2},{8,9},{9,8},{10,11},{11,10},{16,25},{17,24... | collective-permute-start | bytes 24584 | tf_op jit(solution)/shard_map/ppermute | solution.py:469
